TPU v7x, 32 devices: a whole 2x2x4 slice. The times are simulated.
32 devices in a mesh: replica: 8 (over y, x, core), shard: 4 (over z).
Axes of the slice: x: 2, y: 2, z: 4, core: 2. Of those that a mesh axis runs over, the one named last changes fastest.
Arguments:
- tokens_in: bfloat16 [16384, 1088], P(('replica', 'shard')), may hold values from -6 to 6
- lengths: int32 [32, 4], P(('replica', 'shard')), may hold values from 1 to 384, 512 in all within a row
- ln1_gain: bfloat16 [2, 1088], P(None, 'shard'), may hold values from 0.5 to 1.5
- ln1_bias: bfloat16 [2, 1088], P(None, 'shard'), may hold values from -1 to 1
- qkv_weight: bfloat16 [2, 1088, 3264], P(None, 'shard'), may hold values from -0.1875 to 0.1875
- query_bias: bfloat16 [2, 1088], P(None, 'shard'), may hold values from -1 to 1
- value_bias: bfloat16 [2, 1088], P(None, 'shard'), may hold values from -1 to 1
- out_weight: bfloat16 [2, 1088, 1088], P(None, 'shard'), may hold values from -0.75 to 0.75
- out_bias: bfloat16 [2, 1088], P(None, 'shard'), may hold values from -1 to 1
- ln2_gain: bfloat16 [2, 1088], P(None, 'shard'), may hold values from 0.5 to 1.5
- ln2_bias: bfloat16 [2, 1088], P(None, 'shard'), may hold values from -1 to 1
- up_weight: bfloat16 [2, 1088, 4352], P(None, 'shard'), may hold values from -0.1875 to 0.1875
- up_bias: bfloat16 [2, 4352], P(None, 'shard'), may hold values from -1 to 1
- down_weight: bfloat16 [2, 4352, 1088], P(None, 'shard'), may hold values from -0.09375 to 0.09375
- down_bias: bfloat16 [2, 1088], P(None, 'shard'), may hold values from -1 to 1
- cotangent: bfloat16 [16384, 1088], P(('replica', 'shard')), may hold values from -6 to 6
Outputs:
- block_out: bfloat16 [16384, 1088], P(('replica', 'shard'))
- grad_in: float32 [16384, 1088], P(('replica', 'shard'))
- grad_ln1_gain: float32 [2, 1088], P(None, 'shard')
- grad_ln1_bias: float32 [2, 1088], P(None, 'shard')
- grad_qkv_weight: float32 [2, 1088, 3264], P(None, 'shard')
- grad_query_bias: float32 [2, 1088], P(None, 'shard')
- grad_value_bias: float32 [2, 1088], P(None, 'shard')
- grad_out_weight: float32 [2, 1088, 1088], P(None, 'shard')
- grad_out_bias: float32 [2, 1088], P(None, 'shard')
- grad_ln2_gain: float32 [2, 1088], P(None, 'shard')
- grad_ln2_bias: float32 [2, 1088], P(None, 'shard')
- grad_up_weight: float32 [2, 1088, 4352], P(None, 'shard')
- grad_up_bias: float32 [2, 4352], P(None, 'shard')
- grad_down_weight: float32 [2, 4352, 1088], P(None, 'shard')
- grad_down_bias: float32 [2, 1088], P(None, 'shard')
Inputs may be any that keep to these rules, and one draw needn't show every extreme that they name: Each device's row of 4 lengths sums to 512, and one of them equals 384.
All inputs are finite; a program needn't handle non-finite values.
Results may differ from a plain program's by a relative error of at most 0.02.
Values may be sent and summed in bfloat16 or wider, within the bound.
No kernel may reach another device: no remote copies, remote signals or barrier semaphores. Data moves between devices by JAX's collectives and lax.ppermute only.
A program may use at most 320 MiB of HBM per device.

v0:
```python
import jax
import jax.numpy as jnp
from jax import lax
from jax.sharding import PartitionSpec as P

HEADS = 17
HEAD = 64


norm_eps = 1e-05
score_scale = 0.125
masked_fill = -1e30


def layer_norm(values, norm_gain, norm_shift):
    center = values - jnp.mean(values, axis=-1, keepdims=True)
    spread = jnp.mean(center * center, axis=-1, keepdims=True)
    return center * lax.rsqrt(spread + norm_eps) * norm_gain + norm_shift


def gelu_tanh(values):
    return jax.nn.gelu(values, approximate=True)


def causal_mask(lengths, count):
    seq_ends = jnp.cumsum(lengths[0])
    positions = jnp.arange(count, dtype=jnp.int32)
    segment = jnp.sum((positions[:, None] >= seq_ends[None, :]).astype(jnp.int32), axis=1)
    return (segment[:, None] == segment[None, :]) & (positions[:, None] >= positions[None, :])


def split_heads(rows):
    return rows.reshape(rows.shape[0], HEADS, HEAD)


def three_parts(projected):
    width = projected.shape[1] // 3
    return (
        split_heads(projected[:, :width]),
        split_heads(projected[:, width : 2 * width]),
        split_heads(projected[:, 2 * width :]),
    )


def scores_of(queries, key_rows, allowed):
    scores = (
        jnp.einsum("qhd,khd->hqk", queries, key_rows, preferred_element_type=jnp.float32)
        * score_scale
    )
    return jnp.where(allowed[None], scores, masked_fill)


def attend(projected, allowed):
    queries, key_rows, value_rows = three_parts(projected)
    scores = scores_of(queries, key_rows, allowed)
    row_max = jnp.max(scores, axis=-1, keepdims=True)
    exponent = jnp.where(allowed[None], jnp.exp(scores - row_max), 0.0)
    totals = jnp.sum(exponent, axis=-1, keepdims=True)
    attn_probs = (exponent / totals).astype(jnp.bfloat16)
    mixed = jnp.einsum("hqk,khd->qhd", attn_probs, value_rows, preferred_element_type=jnp.float32)
    mixed = mixed.reshape(projected.shape[0], projected.shape[1] // 3)
    return (mixed.astype(jnp.bfloat16), row_max + jnp.log(totals))


def attend_back(projected, log_total, grad_mixed, allowed):
    count = projected.shape[0]
    width = projected.shape[1] // 3
    queries, key_rows, value_rows = three_parts(projected)
    grad_heads = split_heads(grad_mixed)
    scores = scores_of(queries, key_rows, allowed)
    attn_probs = jnp.where(allowed[None], jnp.exp(scores - log_total), 0.0)
    grad_values = jnp.einsum(
        "hqk,qhd->khd",
        attn_probs.astype(jnp.bfloat16),
        grad_heads,
        preferred_element_type=jnp.float32,
    )
    grad_probs = jnp.einsum(
        "qhd,khd->hqk", grad_heads, value_rows, preferred_element_type=jnp.float32
    )
    row_dot = jnp.sum(attn_probs * grad_probs, axis=-1, keepdims=True)
    grad_scores = (attn_probs * (grad_probs - row_dot)).astype(jnp.bfloat16)
    grad_queries = (
        jnp.einsum("hqk,khd->qhd", grad_scores, key_rows, preferred_element_type=jnp.float32)
        * score_scale
    )
    grad_keys = (
        jnp.einsum("hqk,qhd->khd", grad_scores, queries, preferred_element_type=jnp.float32)
        * score_scale
    )
    joined = jnp.concatenate(
        [
            grad_queries.reshape(count, width),
            grad_keys.reshape(count, width),
            grad_values.reshape(count, width),
        ],
        axis=1,
    )
    return joined.astype(jnp.bfloat16)


def forward_layer(stream, weights, allowed):
    (
        norm1_gain,
        norm1_shift,
        qkv_weight,
        query_bias,
        value_bias,
        out_weight,
        out_bias,
        norm2_gain,
        norm2_shift,
        up_weight,
        up_bias,
        down_weight,
        down_bias,
    ) = weights
    normed = layer_norm(
        stream, norm1_gain.astype(jnp.float32), norm1_shift.astype(jnp.float32)
    ).astype(jnp.bfloat16)
    qkv_bias = jnp.concatenate([query_bias, jnp.zeros_like(query_bias), value_bias]).astype(
        jnp.float32
    )
    projected = (jnp.dot(normed, qkv_weight, preferred_element_type=jnp.float32) + qkv_bias).astype(
        jnp.bfloat16
    )
    mixed, log_total = attend(projected, allowed)
    after_attn = (
        stream
        + jnp.dot(mixed, out_weight, preferred_element_type=jnp.float32)
        + out_bias.astype(jnp.float32)
    )
    normed_two = layer_norm(
        after_attn, norm2_gain.astype(jnp.float32), norm2_shift.astype(jnp.float32)
    ).astype(jnp.bfloat16)
    hidden_pre = jnp.dot(
        normed_two, up_weight, preferred_element_type=jnp.float32
    ) + up_bias.astype(jnp.float32)
    activated = gelu_tanh(hidden_pre).astype(jnp.bfloat16)
    result = (
        after_attn
        + jnp.dot(activated, down_weight, preferred_element_type=jnp.float32)
        + down_bias.astype(jnp.float32)
    )
    return (
        result,
        (
            stream,
            normed,
            projected,
            mixed,
            log_total,
            after_attn,
            normed_two,
            hidden_pre,
            activated,
        ),
    )


def backward_layer(grad_out, weights, saved, allowed):
    (
        norm1_gain,
        norm1_shift,
        qkv_weight,
        query_bias,
        value_bias,
        out_weight,
        out_bias,
        norm2_gain,
        norm2_shift,
        up_weight,
        up_bias,
        down_weight,
        down_bias,
    ) = weights
    stream, normed, projected, mixed, log_total, after_attn, normed_two, hidden_pre, activated = (
        saved
    )
    width = stream.shape[1]
    grad_branch = grad_out.astype(jnp.bfloat16)
    grad_down_bias = jnp.sum(grad_branch.astype(jnp.float32), axis=0)
    grad_act = jnp.einsum("td,fd->tf", grad_branch, down_weight, preferred_element_type=jnp.float32)
    gelu_value, gelu_pull = jax.vjp(gelu_tanh, hidden_pre)
    grad_pre = gelu_pull(grad_act)[0].astype(jnp.bfloat16)
    grad_up_bias = jnp.sum(grad_pre.astype(jnp.float32), axis=0)
    grad_normed_two = jnp.einsum(
        "tf,df->td", grad_pre, up_weight, preferred_element_type=jnp.float32
    )
    norm_value, norm_pull = jax.vjp(
        layer_norm, after_attn, norm2_gain.astype(jnp.float32), norm2_shift.astype(jnp.float32)
    )
    grad_after, grad_gain_two, grad_shift_two = norm_pull(grad_normed_two)
    grad_after = grad_out + grad_after
    grad_attn = grad_after.astype(jnp.bfloat16)
    grad_out_bias = jnp.sum(grad_attn.astype(jnp.float32), axis=0)
    grad_mixed = jnp.einsum(
        "te,de->td", grad_attn, out_weight, preferred_element_type=jnp.float32
    ).astype(jnp.bfloat16)
    grad_projected = attend_back(projected, log_total, grad_mixed, allowed)
    grad_query_bias = jnp.sum(grad_projected[:, :width].astype(jnp.float32), axis=0)
    grad_value_bias = jnp.sum(grad_projected[:, 2 * width :].astype(jnp.float32), axis=0)
    grad_normed = jnp.einsum(
        "te,de->td", grad_projected, qkv_weight, preferred_element_type=jnp.float32
    )
    first_value, first_pull = jax.vjp(
        layer_norm, stream, norm1_gain.astype(jnp.float32), norm1_shift.astype(jnp.float32)
    )
    grad_stream, grad_gain_one, grad_shift_one = first_pull(grad_normed)
    vectors = (
        grad_gain_one,
        grad_shift_one,
        grad_query_bias,
        grad_value_bias,
        grad_out_bias,
        grad_gain_two,
        grad_shift_two,
        grad_up_bias,
        grad_down_bias,
    )
    operands = (
        normed,
        grad_projected,
        mixed,
        grad_attn,
        normed_two,
        grad_pre,
        activated,
        grad_branch,
    )
    return (grad_after + grad_stream, vectors, operands)


def weight_products(operands):
    normed, grad_projected, mixed, grad_attn, normed_two, grad_pre, activated, grad_branch = (
        operands
    )
    return (
        jnp.einsum("td,te->de", normed, grad_projected, preferred_element_type=jnp.float32),
        jnp.einsum("td,te->de", mixed, grad_attn, preferred_element_type=jnp.float32),
        jnp.einsum("td,tf->df", normed_two, grad_pre, preferred_element_type=jnp.float32),
        jnp.einsum("tf,td->fd", activated, grad_branch, preferred_element_type=jnp.float32),
    )


def arrange(vectors, matrices):
    return (
        vectors[0],
        vectors[1],
        matrices[0],
        vectors[2],
        vectors[3],
        matrices[1],
        vectors[4],
        vectors[5],
        vectors[6],
        matrices[2],
        vectors[7],
        matrices[3],
        vectors[8],
    )


def body(
    tokens_in,
    lengths,
    ln1_gain,
    ln1_bias,
    qkv_weight,
    query_bias,
    value_bias,
    out_weight,
    out_bias,
    ln2_gain,
    ln2_bias,
    up_weight,
    up_bias,
    down_weight,
    down_bias,
    cotangent,
):
    allowed = causal_mask(lengths, tokens_in.shape[0])
    layer_count = ln1_gain.shape[0]
    stream = tokens_in.astype(jnp.float32)
    saved_all = []
    held = []
    for layer_idx in range(layer_count):
        weights = (
            lax.all_gather(ln1_gain[layer_idx], "shard", axis=0, tiled=True),
            lax.all_gather(ln1_bias[layer_idx], "shard", axis=0, tiled=True),
            lax.all_gather(qkv_weight[layer_idx], "shard", axis=0, tiled=True),
            lax.all_gather(query_bias[layer_idx], "shard", axis=0, tiled=True),
            lax.all_gather(value_bias[layer_idx], "shard", axis=0, tiled=True),
            lax.all_gather(out_weight[layer_idx], "shard", axis=0, tiled=True),
            lax.all_gather(out_bias[layer_idx], "shard", axis=0, tiled=True),
            lax.all_gather(ln2_gain[layer_idx], "shard", axis=0, tiled=True),
            lax.all_gather(ln2_bias[layer_idx], "shard", axis=0, tiled=True),
            lax.all_gather(up_weight[layer_idx], "shard", axis=0, tiled=True),
            lax.all_gather(up_bias[layer_idx], "shard", axis=0, tiled=True),
            lax.all_gather(down_weight[layer_idx], "shard", axis=0, tiled=True),
            lax.all_gather(down_bias[layer_idx], "shard", axis=0, tiled=True),
        )
        held.append(None)
        stream, saved = forward_layer(stream, weights, allowed)
        saved_all.append(saved)
    block_out = stream.astype(jnp.bfloat16)
    grad_stream = cotangent.astype(jnp.float32)
    shares = [None] * layer_count
    for layer_idx in reversed(range(layer_count)):
        weights = (
            lax.all_gather(ln1_gain[layer_idx], "shard", axis=0, tiled=True),
            lax.all_gather(ln1_bias[layer_idx], "shard", axis=0, tiled=True),
            lax.all_gather(qkv_weight[layer_idx], "shard", axis=0, tiled=True),
            lax.all_gather(query_bias[layer_idx], "shard", axis=0, tiled=True),
            lax.all_gather(value_bias[layer_idx], "shard", axis=0, tiled=True),
            lax.all_gather(out_weight[layer_idx], "shard", axis=0, tiled=True),
            lax.all_gather(out_bias[layer_idx], "shard", axis=0, tiled=True),
            lax.all_gather(ln2_gain[layer_idx], "shard", axis=0, tiled=True),
            lax.all_gather(ln2_bias[layer_idx], "shard", axis=0, tiled=True),
            lax.all_gather(up_weight[layer_idx], "shard", axis=0, tiled=True),
            lax.all_gather(up_bias[layer_idx], "shard", axis=0, tiled=True),
            lax.all_gather(down_weight[layer_idx], "shard", axis=0, tiled=True),
            lax.all_gather(down_bias[layer_idx], "shard", axis=0, tiled=True),
        )
        grad_stream, vectors, operands = backward_layer(
            grad_stream, weights, saved_all[layer_idx], allowed
        )
        grads = arrange(vectors, weight_products(operands))
        owned = (
            lax.psum_scatter(
                grads[0].astype(jnp.bfloat16), "shard", scatter_dimension=0, tiled=True
            ).astype(jnp.float32),
            lax.psum_scatter(
                grads[1].astype(jnp.bfloat16), "shard", scatter_dimension=0, tiled=True
            ).astype(jnp.float32),
            lax.psum_scatter(
                grads[2].astype(jnp.bfloat16), "shard", scatter_dimension=0, tiled=True
            ).astype(jnp.float32),
            lax.psum_scatter(
                grads[3].astype(jnp.bfloat16), "shard", scatter_dimension=0, tiled=True
            ).astype(jnp.float32),
            lax.psum_scatter(
                grads[4].astype(jnp.bfloat16), "shard", scatter_dimension=0, tiled=True
            ).astype(jnp.float32),
            lax.psum_scatter(
                grads[5].astype(jnp.bfloat16), "shard", scatter_dimension=0, tiled=True
            ).astype(jnp.float32),
            lax.psum_scatter(
                grads[6].astype(jnp.bfloat16), "shard", scatter_dimension=0, tiled=True
            ).astype(jnp.float32),
            lax.psum_scatter(
                grads[7].astype(jnp.bfloat16), "shard", scatter_dimension=0, tiled=True
            ).astype(jnp.float32),
            lax.psum_scatter(
                grads[8].astype(jnp.bfloat16), "shard", scatter_dimension=0, tiled=True
            ).astype(jnp.float32),
            lax.psum_scatter(
                grads[9].astype(jnp.bfloat16), "shard", scatter_dimension=0, tiled=True
            ).astype(jnp.float32),
            lax.psum_scatter(
                grads[10].astype(jnp.bfloat16), "shard", scatter_dimension=0, tiled=True
            ).astype(jnp.float32),
            lax.psum_scatter(
                grads[11].astype(jnp.bfloat16), "shard", scatter_dimension=0, tiled=True
            ).astype(jnp.float32),
            lax.psum_scatter(
                grads[12].astype(jnp.bfloat16), "shard", scatter_dimension=0, tiled=True
            ).astype(jnp.float32),
        )
        owned = (
            lax.psum(owned[0].astype(jnp.bfloat16), "replica").astype(jnp.float32),
            lax.psum(owned[1].astype(jnp.bfloat16), "replica").astype(jnp.float32),
            lax.psum(owned[2].astype(jnp.bfloat16), "replica").astype(jnp.float32),
            lax.psum(owned[3].astype(jnp.bfloat16), "replica").astype(jnp.float32),
            lax.psum(owned[4].astype(jnp.bfloat16), "replica").astype(jnp.float32),
            lax.psum(owned[5].astype(jnp.bfloat16), "replica").astype(jnp.float32),
            lax.psum(owned[6].astype(jnp.bfloat16), "replica").astype(jnp.float32),
            lax.psum(owned[7].astype(jnp.bfloat16), "replica").astype(jnp.float32),
            lax.psum(owned[8].astype(jnp.bfloat16), "replica").astype(jnp.float32),
            lax.psum(owned[9].astype(jnp.bfloat16), "replica").astype(jnp.float32),
            lax.psum(owned[10].astype(jnp.bfloat16), "replica").astype(jnp.float32),
            lax.psum(owned[11].astype(jnp.bfloat16), "replica").astype(jnp.float32),
            lax.psum(owned[12].astype(jnp.bfloat16), "replica").astype(jnp.float32),
        )
        shares[layer_idx] = owned
    stacked = [jnp.stack([share[position] for share in shares]) for position in range(13)]
    return (
        block_out,
        grad_stream,
        stacked[0],
        stacked[1],
        stacked[2],
        stacked[3],
        stacked[4],
        stacked[5],
        stacked[6],
        stacked[7],
        stacked[8],
        stacked[9],
        stacked[10],
        stacked[11],
        stacked[12],
    )


def solution(mesh):
    in_specs = (
        P(("replica", "shard"), None),
        P(("replica", "shard"), None),
        P(None, "shard"),
        P(None, "shard"),
        P(None, "shard", None),
        P(None, "shard"),
        P(None, "shard"),
        P(None, "shard", None),
        P(None, "shard"),
        P(None, "shard"),
        P(None, "shard"),
        P(None, "shard", None),
        P(None, "shard"),
        P(None, "shard", None),
        P(None, "shard"),
        P(("replica", "shard"), None),
    )
    out_specs = (
        P(("replica", "shard"), None),
        P(("replica", "shard"), None),
        P(None, "shard"),
        P(None, "shard"),
        P(None, "shard", None),
        P(None, "shard"),
        P(None, "shard"),
        P(None, "shard", None),
        P(None, "shard"),
        P(None, "shard"),
        P(None, "shard"),
        P(None, "shard", None),
        P(None, "shard"),
        P(None, "shard", None),
        P(None, "shard"),
    )
    return jax.shard_map(body, mesh=mesh, in_specs=in_specs, out_specs=out_specs, check_vma=False)
```

profile of v0, /device:TPU:0, one launch (start us, length us, event | category | flops | bytes accessed | tf_op | source)
XLA Modules:
  0.0 2418.2 jit_solution(11519426178294011643)
XLA Ops:
  34.6 27.9 %all-reduce.39 = (bf16[1088]{0:T(1024)(128)(2,1)S(1)}, bf16[1088]{0:T(1024)(128)(2,1)S(1)}, bf16[1088]{0:T(1024)(128)(2,1)S(1)}, bf16[1088]{0:T(1024)(128)(2,1)S...) all-reduce(bf16[1088]{0:T(1024)(128)(2,1)S(1)} %dynamic-update-slic, ...), channel_id=5, replica_groups=mesh['replica'=8,'shard'=4] {'shard'}, use_global_device_ids=true, to_apply=%add.2 | all-reduce | flops 25024 | bytes 100096 | tf_op jit(solution)/shard_map/all_gather | solution.py:292
  63.1 84.5 %all-gather.35.cloned.1.call-done = bf16[1,1088,3264]{2,1,0:T(8,128)(2,1)} async-done(((bf16[1,272,3264]{2,1,0:T(8,128)(2,1)}), bf16[1,1088,3264]{2,1,0:T(8,128)(2,1)}) %all-gather.35.cloned.1.call-update) | async-done | bytes 7102480 | tf_op jit(solution)/shard_map/all_gather | solution.py:291
  147.6 8.0 add_convert_fusion.1
  156.8 8.0 fusion.2
  164.9 10.4 fusion
  175.4 10.1 fusion.95
  185.5 14.9 all-gather.37.cloned.1.call-done
  204.6 164.1 %all-gather.39.cloned.1.call-done = bf16[1,1088,4352]{2,1,0:T(8,128)(2,1)} async-done(((bf16[1,272,4352]{2,1,0:T(8,128)(2,1)}), bf16[1,1088,4352]{2,1,0:T(8,128)(2,1)}) %all-gather.39.cloned.1.call-update) | async-done | bytes 9469968 | tf_op jit(solution)/shard_map/all_gather | solution.py:298
  368.7 12.5 fusion.44
  381.2 164.1 %all-gather.41.cloned.1.call-done = bf16[1,4352,1088]{2,1,0:T(8,128)(2,1)} async-done(((bf16[1,1088,1088]{2,1,0:T(8,128)(2,1)}), bf16[1,4352,1088]{2,1,0:T(8,128)(2,1)}) %all-gather.41.cloned.1.call-update) | async-done | bytes 9469968 | tf_op jit(solution)/shard_map/all_gather | solution.py:300
  545.4 12.1 fusion.147
  559.1 116.8 %all-gather.43.cloned.1.call-done = bf16[1,1088,3264]{2,1,0:T(8,128)(2,1)} async-done(((bf16[1,272,3264]{2,1,0:T(8,128)(2,1)}), bf16[1,1088,3264]{2,1,0:T(8,128)(2,1)}) %all-gather.43.cloned.1.call-update) | async-done | bytes 7102480 | tf_op jit(solution)/shard_map/all_gather | solution.py:291
  675.9 8.6 add_convert_fusion
  685.9 8.3 fusion.3
  694.2 10.4 fusion.1
  704.6 10.2 fusion.94
  714.8 13.8 all-gather.45.cloned.1.call-done
  733.3 163.5 %all-gather.47.cloned.1.call-done = bf16[1,1088,4352]{2,1,0:T(8,128)(2,1)} async-done(((bf16[1,272,4352]{2,1,0:T(8,128)(2,1)}), bf16[1,1088,4352]{2,1,0:T(8,128)(2,1)}) %all-gather.47.cloned.1.call-update) | async-done | bytes 9469968 | tf_op jit(solution)/shard_map/all_gather | solution.py:298
  896.8 12.4 fusion.47
  909.2 164.4 %all-gather.49.cloned.1.call-done = bf16[1,4352,1088]{2,1,0:T(8,128)(2,1)} async-done(((bf16[1,1088,1088]{2,1,0:T(8,128)(2,1)}), bf16[1,4352,1088]{2,1,0:T(8,128)(2,1)}) %all-gather.49.cloned.1.call-update) | async-done | bytes 9469968 | tf_op jit(solution)/shard_map/all_gather | solution.py:300
  1073.6 15.7 fusion.149
  1089.3 9.3 multiply_reduce_fusion.2
  1108.1 10.4 bitcast_reduce_fusion.2
  1118.5 12.9 multiply_reduce_fusion.1
  1131.4 13.5 multiply_convert_fusion.1
  1153.6 9.2 fusion.132
  1166.6 16.5 fusion.150
  1183.1 10.0 multiply_reduce_fusion.3
  1200.5 7.9 convolution_convert_fusion.4
  1213.3 13.5 multiply_reduce_fusion
  1226.8 16.9 multiply_convert_fusion
  1243.7 7.4 multiply_convert_fusion.4
  1264.5 9.5 convolution_convert_fusion.5
  1275.7 10.1 convolution_convert_fusion.2
  1285.9 12.9 convolution_convert_fusion
  1298.9 13.5 convolution_convert_fusion.1
  1313.1 10.4 convolution_convert_fusion.3
  1323.6 58.3 %reduce-scatter.11.cloned.1.call-done = bf16[272,3264]{1,0:T(8,128)(2,1)} async-done(((bf16[1088,3264]{1,0:T(8,128)(2,1)}), bf16[272,3264]{1,0:T(8,128)(2,1)}) %reduce-scatter.11.cloned.1.call-update) | async-done | bytes 1775632 | tf_op jit(solution)/shard_map/reduce_scatter | solution.py:336
  1381.9 129.0 %reduce-scatter.9.cloned.1.call-done = bf16[272,3264]{1,0:T(8,128)(2,1)} async-done(((bf16[1088,3264]{1,0:T(8,128)(2,1)}), bf16[272,3264]{1,0:T(8,128)(2,1)}) %reduce-scatter.9.cloned.1.call-update) | async-done | bytes 1775632 | tf_op jit(solution)/shard_map/reduce_scatter | solution.py:336
  1510.9 165.6 %reduce-scatter.19.cloned.1.call-done = bf16[272,4352]{1,0:T(8,128)(2,1)} async-done(((bf16[1088,4352]{1,0:T(8,128)(2,1)}), bf16[272,4352]{1,0:T(8,128)(2,1)}) %reduce-scatter.19.cloned.1.call-update) | async-done | bytes 2367504 | tf_op jit(solution)/shard_map/reduce_scatter | solution.py:357
  1676.5 174.3 %reduce-scatter.23.cloned.1.call-done = bf16[1088,1088]{1,0:T(8,128)(2,1)} async-done(((bf16[4352,1088]{1,0:T(8,128)(2,1)}), bf16[1088,1088]{1,0:T(8,128)(2,1)}) %reduce-scatter.23.cloned.1.call-update) | async-done | bytes 2367504 | tf_op jit(solution)/shard_map/reduce_scatter | solution.py:363
  1850.8 173.9 %reduce-scatter.21.cloned.1.call-done = bf16[1088,1088]{1,0:T(8,128)(2,1)} async-done(((bf16[4352,1088]{1,0:T(8,128)(2,1)}), bf16[1088,1088]{1,0:T(8,128)(2,1)}) %reduce-scatter.21.cloned.1.call-update) | async-done | bytes 2367504 | tf_op jit(solution)/shard_map/reduce_scatter | solution.py:363
  2024.7 165.4 %reduce-scatter.17.cloned.1.call-done = bf16[272,4352]{1,0:T(8,128)(2,1)} async-done(((bf16[1088,4352]{1,0:T(8,128)(2,1)}), bf16[272,4352]{1,0:T(8,128)(2,1)}) %reduce-scatter.17.cloned.1.call-update) | async-done | bytes 2367504 | tf_op jit(solution)/shard_map/reduce_scatter | solution.py:357
  2191.8 8.2 fusion.131
  2202.6 20.7 all-reduce.38
  2225.5 25.0 %all-reduce.36 = (bf16[1,272]{1,0:T(2,128)(2,1)S(1)}, bf16[1,272]{1,0:T(2,128)(2,1)S(1)}, bf16[1,272]{1,0:T(2,128)(2,1)S(1)}, bf16[1,272]{1,0:T(2,128)(2,1)S(1)}...) all-reduce(bf16[1,272]{1,0:T(2,128)(2,1)S(1)} %stack.183, ...), channel_id=1, replica_groups=mesh['replica'=8,'shard'=4] {'replica'}, use_global_device_ids=true, to_apply=%region_29.30 | all-reduce | flops 6528 | bytes 26112 | tf_op jit(solution)/shard_map/psum | solution.py:371
  2258.7 14.8 fusion.80
  2273.5 120.7 %all-reduce.42.cloned.1.call-done = (bf16[1,272,3264]{2,1,0:T(8,128)(2,1)}, bf16[1,272,3264]{2,1,0:T(8,128)(2,1)}, bf16[1,272,1088]{2,1,0:T(8,128)(2,1)}, bf16[1...) async-done(((bf16[1,272,3264]{2,1,0:T(8,128)(2,1)}, ...) | async-done | bytes 14204944 | tf_op jit(solution)/shard_map/psum | solution.py:373
  (425 shorter events, 119.5 us)
Async XLA Ops:
  7.2 140.4 %all-gather.35.cloned.1.call-start = ((), (), s32[]{:S(2)}) async-start(), calls=%async_computation.16 | async-start | bytes 9052160 | tf_op jit(solution)/shard_map/all_gather | solution.py:291
  11.3 189.1 %all-gather.37.cloned.1.call-start = ((), (), s32[]{:S(2)}) async-start(), calls=%async_computation.17 | async-start | bytes 3133440 | tf_op jit(solution)/shard_map/all_gather | solution.py:294
  13.8 355.0 %all-gather.39.cloned.1.call-start = ((), (), s32[]{:S(2)}) async-start(), calls=%async_computation.18 | async-start | bytes 11837440 | tf_op jit(solution)/shard_map/all_gather | solution.py:298
  18.7 526.7 %all-gather.41.cloned.1.call-start = ((), (), s32[]{:S(2)}) async-start(), calls=%async_computation.19 | async-start | bytes 12533760 | tf_op jit(solution)/shard_map/all_gather | solution.py:300
  24.2 651.7 %all-gather.43.cloned.1.call-start = ((), (), s32[]{:S(2)}) async-start(), calls=%async_computation.20 | async-start | bytes 9052160 | tf_op jit(solution)/shard_map/all_gather | solution.py:291
  24.8 703.7 %all-gather.45.cloned.1.call-start = ((), (), s32[]{:S(2)}) async-start(), calls=%async_computation.21 | async-start | bytes 3133440 | tf_op jit(solution)/shard_map/all_gather | solution.py:294
  25.4 871.4 %all-gather.47.cloned.1.call-start = ((), (), s32[]{:S(2)}) async-start(), calls=%async_computation.22 | async-start | bytes 11837440 | tf_op jit(solution)/shard_map/all_gather | solution.py:298
  26.1 1047.5 %all-gather.49.cloned.1.call-start = ((), (), s32[]{:S(2)}) async-start(), calls=%async_computation.23 | async-start | bytes 12533760 | tf_op jit(solution)/shard_map/all_gather | solution.py:300
  26.9 1296.7 %reduce-scatter.15.cloned.1.call-start = ((), (), s32[]{:S(2)}) async-start(), calls=%async_computation.11 | async-start | bytes 3133440 | tf_op jit(solution)/shard_map/reduce_scatter | solution.py:345
  29.3 126.3 %copy-start.64 = (f32[512]{0:T(512)}, f32[512]{0:T(512)S(1)}, u32[]{:S(2)}) copy-start(f32[512]{0:T(512)S(1)} %broadcast_multiply_fusion.3) | copy-start | bytes 6148
  29.7 32.8 %copy-start.69 = (f32[512]{0:T(512)}, f32[512]{0:T(512)S(1)}, u32[]{:S(2)}) copy-start(f32[512]{0:T(512)S(1)} %fusion.92) | copy-start | bytes 6148
  29.7 125.9 %copy-start.76 = (f32[512]{0:T(512)}, f32[512]{0:T(512)S(1)}, u32[]{:S(2)}) copy-start(f32[512]{0:T(512)S(1)} %fusion.106) | copy-start | bytes 6148
  62.5 93.1 %copy-start.58 = (f32[1088]{0:T(1024)}, f32[1088]{0:T(1024)S(1)}, u32[]{:S(2)}) copy-start(f32[1088]{0:T(1024)S(1)} %convert_element_type.379) | copy-start | bytes 13060
  62.5 306.2 %copy-start.44 = (f32[1088]{0:T(1024)}, f32[1088]{0:T(1024)S(1)}, u32[]{:S(2)}) copy-start(f32[1088]{0:T(1024)S(1)} %convert_element_type.382) | copy-start | bytes 13060
  62.6 1036.1 %copy-start.46 = (f32[1088]{0:T(1024)}, f32[1088]{0:T(1024)S(1)}, u32[]{:S(2)}) copy-start(f32[1088]{0:T(1024)S(1)} %convert_element_type.389) | copy-start | bytes 13060
  62.6 93.0 %copy-start.84 = (f32[1088]{0:T(1024)}, f32[1088]{0:T(1024)S(1)}, u32[]{:S(2)}) copy-start(f32[1088]{0:T(1024)S(1)} %convert_element_type.380) | copy-start | bytes 13060
  62.6 306.1 %copy-start.50 = (f32[1088]{0:T(1024)}, f32[1088]{0:T(1024)S(1)}, u32[]{:S(2)}) copy-start(f32[1088]{0:T(1024)S(1)} %convert_element_type.383) | copy-start | bytes 13060
  62.6 613.3 %copy-start.86 = (f32[1088]{0:T(1024)}, f32[1088]{0:T(1024)S(1)}, u32[]{:S(2)}) copy-start(f32[1088]{0:T(1024)S(1)} %convert_element_type.387) | copy-start | bytes 13060
  62.6 834.1 %copy-start.52 = (f32[1088]{0:T(1024)}, f32[1088]{0:T(1024)S(1)}, u32[]{:S(2)}) copy-start(f32[1088]{0:T(1024)S(1)} %convert_element_type.390) | copy-start | bytes 13060
  63.1 112.2 %copy-start.14 = (pred[512,512]{0,1:T(8,128)(4,1)}, pred[512,512]{0,1:T(8,128)(4,1)S(1)}, u32[]{:S(2)}) copy-start(pred[512,512]{0,1:T(8,128)(4,1)S(1)} %fusion.103) | copy-start | bytes 786436
  204.2 341.1 %copy-start.2 = (f32[512,1088]{0,1:T(8,128)}, f32[512,1088]{0,1:T(8,128)S(1)}, u32[]{:S(2)}) copy-start(f32[512,1088]{0,1:T(8,128)S(1)} %get-tuple-element.139) | copy-start | bytes 6684676
  204.3 176.9 %copy-start.54 = (f32[512]{0:T(512)}, f32[512]{0:T(512)S(1)}, u32[]{:S(2)}) copy-start(f32[512]{0:T(512)S(1)} %broadcast_multiply_fusion.2) | copy-start | bytes 6148
  204.6 176.6 %copy-start.72 = (f32[512]{0:T(512)}, f32[512]{0:T(512)S(1)}, u32[]{:S(2)}) copy-start(f32[512]{0:T(512)S(1)} %multiply_reduce_fusion.10) | copy-start | bytes 6148
  204.6 176.6 %copy-start.60 = (f32[512]{0:T(512)}, f32[512]{0:T(512)S(1)}, u32[]{:S(2)}) copy-start(f32[512]{0:T(512)S(1)} %fusion.107) | copy-start | bytes 6148
  559.1 125.4 %copy-start.74 = (f32[512]{0:T(512)}, f32[512]{0:T(512)S(1)}, u32[]{:S(2)}) copy-start(f32[512]{0:T(512)S(1)} %multiply_reduce_fusion.9) | copy-start | bytes 6148
  559.1 125.4 %copy-start.67 = (f32[512]{0:T(512)}, f32[512]{0:T(512)S(1)}, u32[]{:S(2)}) copy-start(f32[512]{0:T(512)S(1)} %fusion.108) | copy-start | bytes 6148
  732.9 365.7 %copy-start = (f32[512,1088]{0,1:T(8,128)}, f32[512,1088]{0,1:T(8,128)S(1)}, u32[]{:S(2)}) copy-start(f32[512,1088]{0,1:T(8,128)S(1)} %get-tuple-element.145) | copy-start | bytes 6684676
  732.9 365.7 %copy-start.56 = (f32[512]{0:T(512)}, f32[512]{0:T(512)S(1)}, u32[]{:S(2)}) copy-start(f32[512]{0:T(512)S(1)} %broadcast_multiply_fusion) | copy-start | bytes 6148
  733.3 365.4 %copy-start.62 = (f32[512]{0:T(512)}, f32[512]{0:T(512)S(1)}, u32[]{:S(2)}) copy-start(f32[512]{0:T(512)S(1)} %fusion.109) | copy-start | bytes 6148
  1073.6 15.7 copy-start.18
  1152.0 171.6 %reduce-scatter.13.cloned.1.call-start = ((), (), s32[]{:S(2)}) async-start(), calls=%async_computation.10 | async-start | bytes 3133440 | tf_op jit(solution)/shard_map/reduce_scatter | solution.py:345
  1166.6 27.2 %copy-start.4 = (f32[512,1088]{0,1:T(8,128)}, f32[512,1088]{0,1:T(8,128)S(1)}, u32[]{:S(2)}) copy-start(f32[512,1088]{0,1:T(8,128)S(1)} %get-tuple-element.110) | copy-start | bytes 6684676
  1166.6 16.5 copy-start.3
  1166.6 16.5 copy-start.45
  1166.6 16.5 copy-start.55
  1166.6 16.5 copy-start.61
  1199.2 182.6 %reduce-scatter.11.cloned.1.call-start = ((), (), s32[]{:S(2)}) async-start(), calls=%async_computation.9 | async-start | bytes 9052160 | tf_op jit(solution)/shard_map/reduce_scatter | solution.py:336
  1208.4 302.5 %reduce-scatter.9.cloned.1.call-start = ((), (), s32[]{:S(2)}) async-start(), calls=%async_computation.8 | async-start | bytes 9052160 | tf_op jit(solution)/shard_map/reduce_scatter | solution.py:336
  1213.2 13.5 copy-start.106
  1226.8 17.0 copy-start.20
  1226.8 30.1 %slice-start = ((s8[17825792]{0:T(1024)(128)(4,1)}), s8[4194304]{0:T(1024)(128)(4,1)S(1)}, s32[]{:S(2)}) async-start(s8[17825792]{0:T(1024)(128)(4,1)} %bitcast.163), calls=%async_computation.25 | async-start | bytes 8388608
  1226.8 30.1 %slice-start.1 = ((s8[17825792]{0:T(1024)(128)(4,1)}), s8[4194304]{0:T(1024)(128)(4,1)S(1)}, s32[]{:S(2)}) async-start(s8[17825792]{0:T(1024)(128)(4,1)} %bitcast.163), calls=%async_computation.26 | async-start | bytes 8388608
  1226.8 30.1 %slice-start.2 = ((s8[17825792]{0:T(1024)(128)(4,1)}), s8[4194304]{0:T(1024)(128)(4,1)S(1)}, s32[]{:S(2)}) async-start(s8[17825792]{0:T(1024)(128)(4,1)} %bitcast.163), calls=%async_computation.27 | async-start | bytes 8388608
  1274.0 402.4 %reduce-scatter.19.cloned.1.call-start = ((), (), s32[]{:S(2)}) async-start(), calls=%async_computation.13 | async-start | bytes 11837440 | tf_op jit(solution)/shard_map/reduce_scatter | solution.py:357
  1285.8 565.0 %reduce-scatter.23.cloned.1.call-start = ((), (), s32[]{:S(2)}) async-start(), calls=%async_computation.15 | async-start | bytes 12533760 | tf_op jit(solution)/shard_map/reduce_scatter | solution.py:363
  1298.8 725.9 %reduce-scatter.21.cloned.1.call-start = ((), (), s32[]{:S(2)}) async-start(), calls=%async_computation.14 | async-start | bytes 12533760 | tf_op jit(solution)/shard_map/reduce_scatter | solution.py:363
  1312.4 877.7 %reduce-scatter.17.cloned.1.call-start = ((), (), s32[]{:S(2)}) async-start(), calls=%async_computation.12 | async-start | bytes 11837440 | tf_op jit(solution)/shard_map/reduce_scatter | solution.py:357
  1323.5 1070.8 %all-reduce.42.cloned.1.call-start = ((), (), s32[]{:S(2)}) async-start(), calls=%async_computation.24 | async-start | bytes 29245440 | tf_op jit(solution)/shard_map/psum | solution.py:373
  (81 other events, 349.4 us)
Sparse Core Ops, SparseCore 0:
  11.5 136.1 all-gather.34
  149.2 51.2 all-gather.36
  202.6 166.0 all-gather.38
  370.7 174.6 all-gather.40
  546.8 129.0 all-gather.42
  677.3 51.1 all-gather.44
  730.7 166.0 all-gather.46
  898.9 174.6 all-gather.48
  1152.1 48.6 reduce-scatter.14
  1203.1 50.0 reduce-scatter.12
  1256.1 125.7 reduce-scatter.10
  1384.2 126.6 reduce-scatter.8
  1513.8 162.6 reduce-scatter.18
  1679.3 171.4 reduce-scatter.22
  1853.0 171.6 reduce-scatter.20
  2026.9 163.1 reduce-scatter.16
  2194.7 199.5 all-reduce.41
where the time goes:
time: 2420 us
  waiting for transfers between devices  1880 us (78%)
  matrix products  323 us (13%)
  other arithmetic  85 us (4%)
  blocking collectives  73.6 us (3%)
  local copies, waits for them, and re-layouts  42.1 us (2%)
    reduce_scatter x2, waiting for transfers between devices, body(): lax.psum_scatter(grads[11].astype(jnp.bfloat16), 'shard', scatter_dimensi...  348 us
    reduce_scatter x2, waiting for transfers between devices, body(): lax.psum_scatter(grads[9].astype(jnp.bfloat16), 'shard', scatter_dimensio...  331 us
    all_gather x2, waiting for transfers between devices, body(): lax.all_gather(down_weight[layer_idx], 'shard', axis=0, tiled=True)  329 us
    all_gather x2, waiting for transfers between devices, body(): lax.all_gather(up_weight[layer_idx], 'shard', axis=0, tiled=True)  328 us
    all_gather x2, waiting for transfers between devices, body(): lax.all_gather(qkv_weight[layer_idx], 'shard', axis=0, tiled=True)  201 us
    reduce_scatter x2, waiting for transfers between devices, body(): lax.psum_scatter(grads[2].astype(jnp.bfloat16), 'shard', scatter_dimensio...  187 us
    psum x1, waiting for transfers between devices, body(): lax.psum(owned[2].astype(jnp.bfloat16), 'replica').astype(jnp.float32)  121 us
  transfers between devices with their start and end apart: 17, of which 15 were waited for; matrix products, arithmetic and copies ran while one was open for 14% of the time, Pallas kernels for 0%

commit v1 on v0

v1 whole, which is shorter than its diff:
```python
import functools

import jax
import jax.numpy as jnp
from jax import lax
from jax.experimental import pallas as pl
from jax.experimental.pallas import tpu as pltpu
from jax.sharding import PartitionSpec as P

HEADS = 17
HEAD = 64


norm_eps = 1e-05
score_scale = 0.125
masked_fill = -1e30


def layer_norm(values, norm_gain, norm_shift):
    center = values - jnp.mean(values, axis=-1, keepdims=True)
    spread = jnp.mean(center * center, axis=-1, keepdims=True)
    return center * lax.rsqrt(spread + norm_eps) * norm_gain + norm_shift


def gelu_tanh(values):
    return jax.nn.gelu(values, approximate=True)


def causal_mask(lengths, count):
    seq_ends = jnp.cumsum(lengths[0])
    positions = jnp.arange(count, dtype=jnp.int32)
    segment = jnp.sum((positions[:, None] >= seq_ends[None, :]).astype(jnp.int32), axis=1)
    return (segment[:, None] == segment[None, :]) & (positions[:, None] >= positions[None, :])


def split_heads(rows):
    return rows.reshape(rows.shape[0], HEADS, HEAD)


def three_parts(projected):
    width = projected.shape[1] // 3
    return (
        split_heads(projected[:, :width]),
        split_heads(projected[:, width : 2 * width]),
        split_heads(projected[:, 2 * width :]),
    )


def scores_of(queries, key_rows, allowed):
    scores = (
        jnp.einsum("qhd,khd->hqk", queries, key_rows, preferred_element_type=jnp.float32)
        * score_scale
    )
    return jnp.where(allowed[None], scores, masked_fill)


def attend(projected, allowed):
    queries, key_rows, value_rows = three_parts(projected)
    scores = scores_of(queries, key_rows, allowed)
    row_max = jnp.max(scores, axis=-1, keepdims=True)
    exponent = jnp.where(allowed[None], jnp.exp(scores - row_max), 0.0)
    totals = jnp.sum(exponent, axis=-1, keepdims=True)
    attn_probs = (exponent / totals).astype(jnp.bfloat16)
    mixed = jnp.einsum("hqk,khd->qhd", attn_probs, value_rows, preferred_element_type=jnp.float32)
    mixed = mixed.reshape(projected.shape[0], projected.shape[1] // 3)
    return (mixed.astype(jnp.bfloat16), row_max + jnp.log(totals))


def attend_back(projected, log_total, grad_mixed, allowed):
    count = projected.shape[0]
    width = projected.shape[1] // 3
    queries, key_rows, value_rows = three_parts(projected)
    grad_heads = split_heads(grad_mixed)
    scores = scores_of(queries, key_rows, allowed)
    attn_probs = jnp.where(allowed[None], jnp.exp(scores - log_total), 0.0)
    grad_values = jnp.einsum(
        "hqk,qhd->khd",
        attn_probs.astype(jnp.bfloat16),
        grad_heads,
        preferred_element_type=jnp.float32,
    )
    grad_probs = jnp.einsum(
        "qhd,khd->hqk", grad_heads, value_rows, preferred_element_type=jnp.float32
    )
    row_dot = jnp.sum(attn_probs * grad_probs, axis=-1, keepdims=True)
    grad_scores = (attn_probs * (grad_probs - row_dot)).astype(jnp.bfloat16)
    grad_queries = (
        jnp.einsum("hqk,khd->qhd", grad_scores, key_rows, preferred_element_type=jnp.float32)
        * score_scale
    )
    grad_keys = (
        jnp.einsum("hqk,qhd->khd", grad_scores, queries, preferred_element_type=jnp.float32)
        * score_scale
    )
    joined = jnp.concatenate(
        [
            grad_queries.reshape(count, width),
            grad_keys.reshape(count, width),
            grad_values.reshape(count, width),
        ],
        axis=1,
    )
    return joined.astype(jnp.bfloat16)


def dot_columns(rows, chunks):
    return jnp.concatenate(
        [jnp.dot(rows, chunk, preferred_element_type=jnp.float32) for chunk in chunks], axis=1
    )


def dot_columns_back(rows, chunks):
    width = chunks[0].shape[1]
    return sum(
        jnp.einsum(
            "te,de->td",
            rows[:, i * width : (i + 1) * width],
            chunk,
            preferred_element_type=jnp.float32,
        )
        for i, chunk in enumerate(chunks)
    )


def forward_layer(stream, weights, allowed):
    small, qkv_weight, out_weight, up_weight, down_weight = weights
    (
        norm1_gain,
        norm1_shift,
        query_bias,
        value_bias,
        out_bias,
        norm2_gain,
        norm2_shift,
        up_bias,
        down_bias,
    ) = small
    normed = layer_norm(
        stream, norm1_gain.astype(jnp.float32), norm1_shift.astype(jnp.float32)
    ).astype(jnp.bfloat16)
    qkv_bias = jnp.concatenate([query_bias, jnp.zeros_like(query_bias), value_bias]).astype(
        jnp.float32
    )
    projected = (dot_columns(normed, qkv_weight) + qkv_bias).astype(
        jnp.bfloat16
    )
    mixed, log_total = attend(projected, allowed)
    after_attn = (
        stream
        + dot_columns(mixed, out_weight)
        + out_bias.astype(jnp.float32)
    )
    normed_two = layer_norm(
        after_attn, norm2_gain.astype(jnp.float32), norm2_shift.astype(jnp.float32)
    ).astype(jnp.bfloat16)
    hidden_pre = dot_columns(normed_two, up_weight) + up_bias.astype(jnp.float32)
    activated = gelu_tanh(hidden_pre).astype(jnp.bfloat16)
    result = (
        after_attn
        + jnp.dot(activated, down_weight, preferred_element_type=jnp.float32)
        + down_bias.astype(jnp.float32)
    )
    return (
        result,
        (
            stream,
            normed,
            projected,
            mixed,
            log_total,
            after_attn,
            normed_two,
            hidden_pre,
            activated,
        ),
    )


def backward_layer(grad_out, weights, saved, allowed):
    small, qkv_weight, out_weight, up_weight, down_weight = weights
    (
        norm1_gain,
        norm1_shift,
        query_bias,
        value_bias,
        out_bias,
        norm2_gain,
        norm2_shift,
        up_bias,
        down_bias,
    ) = small
    stream, normed, projected, mixed, log_total, after_attn, normed_two, hidden_pre, activated = (
        saved
    )
    width = stream.shape[1]
    grad_branch = grad_out.astype(jnp.bfloat16)
    grad_down_bias = jnp.sum(grad_branch.astype(jnp.float32), axis=0)
    grad_act = jnp.einsum("td,fd->tf", grad_branch, down_weight, preferred_element_type=jnp.float32)
    gelu_value, gelu_pull = jax.vjp(gelu_tanh, hidden_pre)
    grad_pre = gelu_pull(grad_act)[0].astype(jnp.bfloat16)
    grad_up_bias = jnp.sum(grad_pre.astype(jnp.float32), axis=0)
    grad_normed_two = dot_columns_back(grad_pre, up_weight)
    norm_value, norm_pull = jax.vjp(
        layer_norm, after_attn, norm2_gain.astype(jnp.float32), norm2_shift.astype(jnp.float32)
    )
    grad_after, grad_gain_two, grad_shift_two = norm_pull(grad_normed_two)
    grad_after = grad_out + grad_after
    grad_attn = grad_after.astype(jnp.bfloat16)
    grad_out_bias = jnp.sum(grad_attn.astype(jnp.float32), axis=0)
    grad_mixed = dot_columns_back(grad_attn, out_weight).astype(jnp.bfloat16)
    grad_projected = attend_back(projected, log_total, grad_mixed, allowed)
    grad_query_bias = jnp.sum(grad_projected[:, :width].astype(jnp.float32), axis=0)
    grad_value_bias = jnp.sum(grad_projected[:, 2 * width :].astype(jnp.float32), axis=0)
    grad_normed = dot_columns_back(grad_projected, qkv_weight)
    first_value, first_pull = jax.vjp(
        layer_norm, stream, norm1_gain.astype(jnp.float32), norm1_shift.astype(jnp.float32)
    )
    grad_stream, grad_gain_one, grad_shift_one = first_pull(grad_normed)
    vectors = (
        grad_gain_one,
        grad_shift_one,
        grad_query_bias,
        grad_value_bias,
        grad_out_bias,
        grad_gain_two,
        grad_shift_two,
        grad_up_bias,
        grad_down_bias,
    )
    operands = (
        normed,
        grad_projected,
        mixed,
        grad_attn,
        normed_two,
        grad_pre,
        activated,
        grad_branch,
    )
    return (grad_after + grad_stream, vectors, operands)


class Layout:
    def __init__(self, mesh):
        self.copies = mesh.shape["replica"]
        self.shards = mesh.shape["shard"]
        self.across = self.copies // 4
        self.chips = self.copies // 2
        self.crossed = self.across == 2

    def index(self, a, b, c):
        return (a % self.across) * 4 + (b % 2) * 2 + c

    def pairs(self, way):
        out = []
        for i in range(self.copies):
            a, b, c = i // 4, (i // 2) % 2, i % 2
            turned = self.crossed and c == 1
            if way == "core":
                to = self.index(a, b, 1 - c)
            elif (way == "first") != turned:
                to = self.index(a, b + 1, c)
            else:
                to = self.index(a + 1, b, c)
            out.append((i, to))
        return out

    def move(self, value, way):
        return lax.ppermute(value, "replica", self.pairs(way))

    def place(self):
        r = lax.axis_index("replica")
        return r // 4, (r // 2) % 2, r % 2, lax.axis_index("shard")

    def chip_at(self, core, f, k):
        a, b, _, _ = self.place()
        plain = ((a + k) % self.across) * 2 + (b + f) % 2
        if not self.crossed:
            return plain
        turned = ((a + f) % self.across) * 2 + (b + k) % 2
        return jnp.where(core == 1, turned, plain)

    def slots(self):
        return [(f, k) for k in range(self.across) for f in range(2)]


def place_kernel(by_shard, index_ref, *refs):
    chips_cores = (len(refs) - 2)
    blocks, out_ref, sems = refs[:chips_cores], refs[chips_cores], refs[chips_cores + 1]
    shards = blocks[0].shape[0]
    copies = []
    for p in range(chips_cores):
        chip, core = index_ref[0, p], index_ref[1, p]
        for s in range(shards):
            shard = index_ref[2, s]
            target = out_ref.at[shard, chip, core] if by_shard else out_ref.at[chip, shard, core]
            copies.append(pltpu.make_async_copy(blocks[p].at[s], target, sems.at[p * shards + s]))
            copies[-1].start()
    for copy in copies:
        copy.wait()


def assemble(layout, blocks, by_shard):
    _, _, core, shard = layout.place()
    chips, shards = layout.chips, layout.shards
    own = [layout.chip_at(core, -f, -k) for f, k in layout.slots()]
    other = [layout.chip_at(1 - core, -f, -k) for f, k in layout.slots()]
    count = 2 * chips
    width = max(count, shards)

    def row(values):
        return jnp.stack(list(values) + [jnp.int32(0)] * (width - len(values)))

    index = jnp.stack(
        [
            row(own + other),
            row([core] * chips + [1 - core] * chips),
            row([(shard + s) % shards for s in range(shards)]),
        ]
    ).astype(jnp.int32)
    _, rows, cols = blocks[0].shape
    outer = (shards, chips) if by_shard else (chips, shards)
    return pl.pallas_call(
        functools.partial(place_kernel, by_shard),
        out_shape=jax.ShapeDtypeStruct(outer + (2, rows, cols), blocks[0].dtype),
        in_specs=[pl.BlockSpec(memory_space=pltpu.SMEM)]
        + [pl.BlockSpec(memory_space=pl.ANY)] * count,
        out_specs=pl.BlockSpec(memory_space=pltpu.VMEM),
        scratch_shapes=[pltpu.SemaphoreType.DMA((count * shards,))],
        compiler_params=pltpu.CompilerParams(vmem_limit_bytes=40 << 20),
        cost_estimate=pl.CostEstimate(
            flops=0, bytes_accessed=4 * count * shards * rows * cols, transcendentals=0
        ),
    )(index, *blocks)


def gather_shards(layout, piece):
    n = layout.shards
    _, _, _, shard = layout.place()
    right, left = [piece], [piece]
    for t in range(1, n):
        right.append(lax.ppermute(right[-1], "shard", [(i, i + 1) for i in range(t - 1, n - 1)]))
        left.append(lax.ppermute(left[-1], "shard", [(i, i - 1) for i in range(1, n - t + 1)]))
    parts = [piece] + [jnp.where(shard + k < n, left[k], right[n - k]) for k in range(1, n)]
    return jnp.stack(parts)


def gather_group(layout, piece, by_shard):
    block = gather_shards(layout, piece)
    held = {(0, 0): block}
    held[1, 0] = layout.move(block, "first")
    for k in range(1, layout.across):
        for f in range(2):
            held[f, k] = layout.move(held[f, k - 1], "second")
    own = [held[slot] for slot in layout.slots()]
    other = [layout.move(block, "core") for block in own]
    return assemble(layout, own + other, by_shard)


def add_low(left, right):
    return (left.astype(jnp.float32) + right.astype(jnp.float32)).astype(jnp.bfloat16)


def reduce_shards(layout, parts):
    n = layout.shards
    right = left = None
    for t in range(1, n):
        right = parts[n - t] if right is None else add_low(parts[n - t], right)
        left = parts[t] if left is None else add_low(parts[t], left)
        right = lax.ppermute(right, "shard", [(i, i + 1) for i in range(min(t, n - 1))])
        left = lax.ppermute(left, "shard", [(i, i - 1) for i in range(max(1, n - t), n)])
    total = parts[0].astype(jnp.float32) + right.astype(jnp.float32) + left.astype(jnp.float32)
    return total.astype(jnp.bfloat16)


def reduce_group(layout, product):
    _, _, core, _ = layout.place()
    n = layout.shards
    sums = {}
    for f, k in layout.slots():
        away = product(layout.chip_at(1 - core, f, k), 1 - core).astype(jnp.bfloat16)
        came = layout.move(away, "core")
        here = product(layout.chip_at(core, f, k), core)
        sums[f, k] = (here + came.astype(jnp.float32)).astype(jnp.bfloat16)
    halves = []
    for f in range(2):
        total = sums[f, layout.across - 1]
        for step in range(1, layout.across):
            total = add_low(layout.move(total, "second"), sums[f, layout.across - 1 - step])
        halves.append(total)
    total = add_low(layout.move(halves[1], "first"), halves[0])
    total = total.reshape((n, total.shape[0] // n) + total.shape[1:])
    piece = reduce_shards(layout, [total[s] for s in range(n)])
    return lax.all_gather(piece, "replica", axis=0, tiled=False)


def rolled(value, shift):
    return lax.dynamic_slice_in_dim(
        jnp.concatenate([value, value], axis=0), shift, value.shape[0], axis=0
    )


def by_shard_rows(layout, rows, chips):
    n = layout.shards
    _, _, _, shard = layout.place()
    turned = rows.T.reshape(n, chips, 2, rows.shape[1] // (2 * n * chips), rows.shape[0])
    return rolled(turned, shard).transpose(1, 2, 0, 3, 4)


def column_chunks(layout, rows):
    return rows.reshape(rows.shape[0], layout.chips, -1).transpose(1, 0, 2)


def weight_sums(layout, operands):
    normed, grad_projected, mixed, grad_attn, normed_two, grad_pre, activated, grad_branch = (
        operands
    )
    chips = layout.chips

    def flat(block):
        return block.reshape(-1, block.shape[-1])

    def pick(value, i):
        return lax.dynamic_index_in_dim(value, i, axis=0, keepdims=False)

    act_rows = by_shard_rows(layout, activated, chips)

    def down_product(chip, core):
        return jnp.dot(
            flat(pick(pick(act_rows, chip), core)), grad_branch, preferred_element_type=jnp.float32
        )

    two_rows = by_shard_rows(layout, normed_two, 1)[0]
    pre_chunks = column_chunks(layout, grad_pre)

    def up_product(chip, core):
        return jnp.dot(
            flat(pick(two_rows, core)), pick(pre_chunks, chip), preferred_element_type=jnp.float32
        )

    one_rows = by_shard_rows(layout, normed, 1)[0]
    mixed_rows = by_shard_rows(layout, mixed, 1)[0]
    first_chunks = column_chunks(layout, jnp.concatenate([grad_projected, grad_attn], axis=1))

    def first_product(chip, core):
        rows = jnp.where(chip < 3 * chips // 4, pick(one_rows, core), pick(mixed_rows, core))
        return jnp.dot(flat(rows), pick(first_chunks, chip), preferred_element_type=jnp.float32)

    down = reduce_group(layout, down_product)
    up = reduce_group(layout, up_product)
    first = reduce_group(layout, first_product)

    def columns(gathered):
        blocks = gathered.reshape((chips, 2) + gathered.shape[1:])
        blocks = blocks.transpose(1, 2, 0, 3)
        return blocks.reshape(blocks.shape[0] * blocks.shape[1], -1).astype(jnp.float32)

    first = columns(first)
    width = first.shape[1] // 4
    return (
        first[:, : 3 * width],
        first[:, 3 * width :],
        columns(up),
        flat(down).astype(jnp.float32),
    )


def solution(mesh):
    layout = Layout(mesh)

    def body(
        tokens_in,
        lengths,
        ln1_gain,
        ln1_bias,
        qkv_weight,
        query_bias,
        value_bias,
        out_weight,
        out_bias,
        ln2_gain,
        ln2_bias,
        up_weight,
        up_bias,
        down_weight,
        down_bias,
        cotangent,
    ):
        allowed = causal_mask(lengths, tokens_in.shape[0])
        layer_count = ln1_gain.shape[0]
        chips, shards = layout.chips, layout.shards
        a, b, core, shard = layout.place()
        chip = a * 2 + b

        vectors_in = (
            ln1_gain,
            ln1_bias,
            query_bias,
            value_bias,
            out_bias,
            ln2_gain,
            ln2_bias,
            up_bias,
            down_bias,
        )
        joined = lax.all_gather(jnp.concatenate(vectors_in, axis=1), "shard", axis=0, tiled=False)

        def own_columns(weight):
            rows, cols = weight.shape[0] // 2, weight.shape[1] // chips
            return lax.dynamic_slice(weight, (core * rows, chip * cols), (rows, cols))

        def own_rows(weight):
            rows = weight.shape[0] // (2 * chips)
            return lax.dynamic_slice_in_dim(weight, (chip * 2 + core) * rows, rows, axis=0)

        weights = []
        for l in range(layer_count):
            first_piece = own_columns(jnp.concatenate([qkv_weight[l], out_weight[l]], axis=1))
            first = gather_group(layout, first_piece, False)
            up = gather_group(layout, own_columns(up_weight[l]), False)
            down = gather_group(layout, own_rows(down_weight[l]), True)
            first = first.reshape(chips, -1, first.shape[-1])
            up = up.reshape(chips, -1, up.shape[-1])
            down = down.reshape(-1, down.shape[-1])
            small, at = [], 0
            for vector in vectors_in:
                size = vector.shape[1]
                small.append(joined[:, l, at : at + size].reshape(shards * size))
                at += size
            cut = 3 * chips // 4
            weights.append(
                (
                    small,
                    [first[i] for i in range(cut)],
                    [first[i] for i in range(cut, chips)],
                    [up[i] for i in range(chips)],
                    down,
                )
            )

        stream = tokens_in.astype(jnp.float32)
        saved_all = []
        for l in range(layer_count):
            stream, saved = forward_layer(stream, weights[l], allowed)
            saved_all.append(saved)
        block_out = stream.astype(jnp.bfloat16)
        grad_stream = cotangent.astype(jnp.float32)
        shares = [None] * layer_count
        for l in reversed(range(layer_count)):
            grad_stream, vectors, operands = backward_layer(
                grad_stream, weights[l], saved_all[l], allowed
            )
            sums = lax.psum(jnp.concatenate(vectors), ("replica", "shard"))
            small, at = [], 0
            for vector in vectors:
                size = vector.shape[0] // shards
                small.append(lax.dynamic_slice_in_dim(sums, at + shard * size, size))
                at += vector.shape[0]
            shares[l] = (small, weight_sums(layout, operands))

        def stacked(group, i):
            return jnp.stack([share[group][i] for share in shares])

        return (
            block_out,
            grad_stream,
            stacked(0, 0),
            stacked(0, 1),
            stacked(1, 0),
            stacked(0, 2),
            stacked(0, 3),
            stacked(1, 1),
            stacked(0, 4),
            stacked(0, 5),
            stacked(0, 6),
            stacked(1, 2),
            stacked(0, 7),
            stacked(1, 3),
            stacked(0, 8),
        )

    rows = P(("replica", "shard"), None)
    vector = P(None, "shard")
    matrix = P(None, "shard", None)
    params = (
        vector,
        vector,
        matrix,
        vector,
        vector,
        matrix,
        vector,
        vector,
        vector,
        matrix,
        vector,
        matrix,
        vector,
    )
    return jax.shard_map(
        body,
        mesh=mesh,
        in_specs=(rows, rows) + params + (rows,),
        out_specs=(rows, rows) + params,
        check_vma=False,
    )
```

time: 2420 us -> 1280 us (0.53)
  waiting for transfers between devices: 1880 us -> 350 us
  starting transfers between devices: 0.69 us -> 204 us
  other arithmetic: 85 us -> 181 us
  local copies, waits for them, and re-layouts: 42.1 us -> 121 us
  blocking collectives: 73.6 us -> 14.6 us
  Pallas kernels: 0 us -> 47 us
    all_gather x8 -> x6, waiting for transfers between devices: 886 us -> 0.03 us  [reduce_group(): return lax.all_gather(piece, 'replica', axis=0, tiled=False)]
    reduce_scatter x8 -> x0, waiting for transfers between devices: 867 us -> none  [the longest x2 348 us: body(): lax.psum_scatter(grads[11].astype(jnp.bfloat16), 'shard', scatter_dimensi...]
    ppermute x0 -> x156, waiting for transfers between devices: none -> 350 us  [the longest x84 230 us: move(): return lax.ppermute(value, 'replica', self.pairs(way))]
    ppermute x0 -> x156, starting transfers between devices: none -> 203 us  [the longest x18 82.5 us: reduce_shards(): lax.ppermute(right, 'shard', [(i, i + 1) for i in range(min(t, n - 1))])]
    psum x1, waiting for transfers between devices: 121 us -> 0.01 us  [body(): sums = lax.psum(jnp.concatenate(vectors), ('replica', 'shard'))]
    convert_element_type x10 -> x40, other arithmetic: 0.03 us -> 67.6 us  [the longest x24 33.1 us: add_low(): (left.astype(jnp.float32) + right.astype(jnp.float32)).astype(jnp.bfloat16)]
    pallas_call x0 -> x6, Pallas kernels: none -> 47 us  [assemble(): pl.pallas_call(functools.partial(place_kernel, by_shard), out_shape=jax.S...]
    convert_element_type x0 -> x22, local copies, waits for them, and re-layouts: none -> 37.2 us  [the longest x8 33.1 us: columns(): blocks.reshape(blocks.shape[0] * blocks.shape[1], -1).astype(jnp.float32)]
  transfers between devices with their start and end apart: 17 -> 163, of which waited for: 15 -> 62; matrix products, arithmetic and copies ran while one was open for 14% -> 31% of each run, Pallas kernels for 0% -> 3%
where the time goes in v1:
time: 1280 us; the launch traced here: 1260 us
  waiting for transfers between devices  350 us (27%)
  matrix products  327 us (26%)
  starting transfers between devices  204 us (16%)
  other arithmetic  181 us (14%)
  local copies, waits for them, and re-layouts  121 us (9%)
  Pallas kernels  47 us (4%)
  between operations  20 us (2%)
  blocking collectives  14.6 us (1%)
    ppermute x84, waiting for transfers between devices, move(): return lax.ppermute(value, 'replica', self.pairs(way))  230 us
    ppermute x18, starting transfers between devices, reduce_shards(): lax.ppermute(right, 'shard', [(i, i + 1) for i in range(min(t, n - 1))])  82.5 us
    ppermute x18, waiting for transfers between devices, gather_shards(): lax.ppermute(left[-1], 'shard', [(i, i - 1) for i in range(1, n - t + 1)])  58.9 us
    pallas_call x6, Pallas kernels, assemble(): pl.pallas_call(functools.partial(place_kernel, by_shard), out_shape=jax.S...  47 us
    ppermute x84, starting transfers between devices, move(): return lax.ppermute(value, 'replica', self.pairs(way))  43.1 us
    dot_general x2, matrix products, backward_layer(): jnp.einsum('td,fd->tf', grad_branch, down_weight, preferred_element_type=...  41.5 us
    dot_general x16, matrix products, up_product(): jnp.dot(flat(pick(two_rows, core)), pick(pre_chunks, chip), preferred_ele...  38.5 us
    ppermute x18, starting transfers between devices, gather_shards(): lax.ppermute(right[-1], 'shard', [(i, i + 1) for i in range(t - 1, n - 1)])  36.9 us
  transfers between devices with their start and end apart: 163, of which 62 were waited for; matrix products, arithmetic and copies ran while one was open for 31% of the time, Pallas kernels for 3%

profile of v1, /device:TPU:0, one launch (start us, length us, event | category | flops | bytes accessed | tf_op | source)
XLA Modules:
  0.0 1264.4 jit_solution(6522537726868368221)
XLA Ops:
  15.7 6.3 collective-permute-start.40
  38.5 14.6 %all-gather.7 = bf16[4,2,3264]{2,1,0:T(2,128)(2,1)S(1)} all-gather(bf16[1,2,3264]{2,1,0:T(2,128)(2,1)S(1)} %bitcast.650), channel_id=2, replica_groups=mesh['replica'=8,'shard'=4] {'shard'}, dimensions={0}, use_global_device_ids=true | all-gather | bytes 65280 | tf_op jit(solution)/shard_map/all_gather | solution.py:506
  80.8 7.0 collective-permute-start.53
  181.1 25.5 %collective-permute-done.6.refs_1_ = bf16[4,136,1088]{2,1,0:T(8,128)(2,1)S(1)} collective-permute-done((bf16[4,136,1088]{2,1,0:T(8,128)(2,1)S(1)}, bf16[4,136,1088]{2,1,0:T(8,128)(2,1)S(1)}, u32[]{:S(2)}, u32[]{:S(2)}) %collective-permute-start.6) | collective-permute-done | bytes 1183776 | tf_op jit(solution)/shard_map/ppermute | solution.py:269
  219.3 14.3 %collective-permute-done.19.refs_1_ = bf16[4,136,1088]{2,1,0:T(8,128)(2,1)} collective-permute-done((bf16[4,136,1088]{2,1,0:T(8,128)(2,1)}, bf16[4,136,1088]{2,1,0:T(8,128)(2,1)}, u32[]{:S(2)}, u32[]{:S(2)}) %collective-permute-start.19) | collective-permute-done | bytes 1183776 | tf_op jit(solution)/shard_map/ppermute | solution.py:269
  234.7 7.2 collective-permute-done.20.refs_2_
  244.7 19.7 %collective-permute-done.21.refs_3_ = bf16[4,136,1088]{2,1,0:T(8,128)(2,1)} collective-permute-done((bf16[4,136,1088]{2,1,0:T(8,128)(2,1)}, bf16[4,136,1088]{2,1,0:T(8,128)(2,1)}, u32[]{:S(2)}, u32[]{:S(2)}) %collective-permute-start.21) | collective-permute-done | bytes 1183776 | tf_op jit(solution)/shard_map/ppermute | solution.py:269
  266.2 7.6 shard_map.271
  289.2 8.2 fusion.2
  297.4 10.3 fusion
  307.7 9.3 fusion.52
  325.7 8.6 shard_map.272
  339.0 11.9 collective-permute-done.46.refs_2_
  353.5 11.3 collective-permute-done.47.refs_3_
  379.5 22.4 %collective-permute-done.60.refs_3_ = bf16[4,136,1088]{2,1,0:T(8,128)(2,1)S(1)} collective-permute-done((bf16[4,136,1088]{2,1,0:T(8,128)(2,1)S(1)}, bf16[4,136,1088]{2,1,0:T(8,128)(2,1)S(1)}, u32[]{:S(2)}, u32[]{:S(2)}) %collective-permute-start.60) | collective-permute-done | bytes 1183776 | tf_op jit(solution)/shard_map/ppermute | solution.py:269
  407.9 7.1 shard_map.274
  415.0 6.9 fusion.294
  426.1 7.6 shard_map.275
  434.3 7.4 fusion.293
  441.7 10.7 collective-permute-done.72.refs_2_
  454.6 11.2 collective-permute-done.33.refs_2_
  465.8 13.4 %collective-permute-done.34.refs_3_ = bf16[4,136,1088]{2,1,0:T(8,128)(2,1)S(1)} collective-permute-done((bf16[4,136,1088]{2,1,0:T(8,128)(2,1)S(1)}, bf16[4,136,1088]{2,1,0:T(8,128)(2,1)S(1)}, u32[]{:S(2)}, u32[]{:S(2)}) %collective-permute-start.34) | collective-permute-done | bytes 1183776 | tf_op jit(solution)/shard_map/ppermute | solution.py:269
  479.3 7.9 multiply_convert_fusion.3
  493.4 7.6 shard_map.273
  501.0 8.0 fusion.310
  521.1 7.8 fusion.3
  529.0 10.9 fusion.1
  541.3 9.4 fusion.51
  563.0 7.5 multiply_convert_fusion.2
  570.5 8.4 shard_map.276
  579.0 20.8 %convert_reduce_fusion = (f32[4352]{0:T(1024)}, bf16[512,4352]{0,1:T(8,128)(2,1)}) fusion(f32[4352]{0:T(1024)S(1)} %copy-done.152, f32[512,1088]{0,1:T(8,128)} %copy-done.106, f32[512,1088]{0,1:T(8,128)} %copy-done.107, f32[512,1088]{0,1:T(8,128)} %copy-done.108, f32[512,1088]{0,1:T(8,128)} %copy-done.109, bf16[4352,1088]{1,0:T(8,128)(2,1)} %bitcast.517, ...), kind=kOutput, calls=%fused_computation.73 | convolution fusion | flops 4906545152 | bytes 23988224 | tf_op jit(solution)/shard_map/td,fd->tf/dot_general | solution.py:198
  636.1 8.7 fusion.53
  644.8 13.3 %multiply_reduce_fusion.1 = (f32[17,512]{1,0:T(8,128)S(1)}, f32[17,512,512]{1,2,0:T(8,128)}) fusion(f32[17,512]{1,0:T(8,128)S(1)} %copy-done.144, f32[17,512,512]{1,2,0:T(8,128)} %get-tuple-element.202, pred[512,512]{0,1:T(8,128)(4,1)S(1)} %copy-done.37, bf16[512,17,64]{0,2,1:T(8,128)(2,1)S(1)} %bitcast.657, bf16[512,17,64]{0,2,1:T(8,128)(2,1)S(1)} %bitcast.613), kind=kOutput, calls=%fused_computation.4 | convolution fusion | flops 597155328 | bytes 38211584 | tf_op jit(solution)/shard_map/qhd,khd->hqk/dot_general | solution.py:82
  658.1 13.3 %multiply_convert_fusion.1 = bf16[17,512,512]{1,2,0:T(8,128)(2,1)S(1)} fusion(f32[17,512,512]{1,2,0:T(8,128)} %get-tuple-element.207, f32[17,512]{1,0:T(8,128)S(1)} %get-tuple-element.206, f32[17,512]{1,0:T(8,128)S(1)} %copy-done.144, f32[17,512,512]{1,2,0:T(8,128)} %get-tuple-element.202, pred[512,512]{0,1:T(8,128)(4,1)S(1)} %copy-done.37), kind=kLoop, calls=%fused_computation.3 | loop fusion | flops 31195136 | bytes 44896256 | tf_op jit(solution)/shard_map/convert_element_type | solution.py:86
  686.9 20.7 %convert_reduce_fusion.1 = (f32[4352]{0:T(1024)S(1)}, bf16[512,4352]{0,1:T(8,128)(2,1)}) fusion(f32[4352]{0:T(1024)S(1)} %copy-done.151, f32[512,1088]{0,1:T(8,128)} %fusion.318, f32[512,1088]{0,1:T(8,128)} %fusion.317, f32[512,1088]{0,1:T(8,128)} %fusion.316, f32[512,1088]{0,1:T(8,128)} %fusion.315, bf16[4352,1088]{1,0:T(8,128)(2,1)} %bitcast.520, ...), kind=kOutput, calls=%fused_computation.74 | convolution fusion | flops 4906545152 | bytes 23988224 | tf_op jit(solution)/shard_map/td,fd->tf/dot_general | solution.py:198
  738.8 8.7 fusion.56
  747.5 13.4 %multiply_reduce_fusion = (f32[17,512]{1,0:T(8,128)S(1)}, f32[17,512,512]{1,2,0:T(8,128)}) fusion(f32[17,512]{1,0:T(8,128)S(1)} %copy-done.143, f32[17,512,512]{1,2,0:T(8,128)} %get-tuple-element.196, pred[512,512]{0,1:T(8,128)(4,1)S(1)} %copy-done.37, bf16[512,17,64]{0,2,1:T(8,128)(2,1)S(1)} %bitcast.659, bf16[512,17,64]{0,2,1:T(8,128)(2,1)S(1)} %bitcast.611), kind=kOutput, calls=%fused_computation.1 | convolution fusion | flops 597155328 | bytes 38211584 | tf_op jit(solution)/shard_map/qhd,khd->hqk/dot_general | solution.py:82
  760.9 13.1 %multiply_convert_fusion = bf16[17,512,512]{1,2,0:T(8,128)(2,1)S(1)} fusion(f32[17,512,512]{1,2,0:T(8,128)} %get-tuple-element.211, f32[17,512]{1,0:T(8,128)S(1)} %get-tuple-element.210, f32[17,512]{1,0:T(8,128)S(1)} %copy-done.143, f32[17,512,512]{1,2,0:T(8,128)} %get-tuple-element.196, pred[512,512]{0,1:T(8,128)(4,1)S(1)} %copy-done.37), kind=kLoop, calls=%fused_computation | loop fusion | flops 31195136 | bytes 44896256 | tf_op jit(solution)/shard_map/convert_element_type | solution.py:86
  838.8 13.3 %fusion.43 = bf16[512,1088]{0,1:T(8,128)(2,1)} fusion(f32[512,1088]{0,1:T(8,128)S(1)} %copy-done.8, bf16[512,4352]{0,1:T(8,128)(2,1)} %multiply_convert_fusion.2, bf16[4352,1088]{1,0:T(8,128)(2,1)} %bitcast.518, f32[1088]{0:T(1024)S(1)} %copy-done.180), kind=kOutput, calls=%fused_computation.150 | convolution fusion | flops 4850286592 | bytes 17273088 | tf_op jit(solution)/shard_map/dot_general | solution.py:160
  864.7 7.2 collective-permute-done.118
  878.8 16.6 %collective-permute-done.122 = bf16[544,1088]{1,0:T(8,128)(2,1)S(1)} collective-permute-done((bf16[544,1088]{1,0:T(8,128)(2,1)S(1)}, bf16[544,1088]{1,0:T(8,128)(2,1)S(1)}, u32[]{:S(2)}, u32[]{:S(2)}) %collective-permute-start.122) | collective-permute-done | bytes 1183776 | tf_op jit(solution)/shard_map/ppermute | solution.py:269
  989.6 8.6 collective-permute-done.109
  1028.7 7.0 collective-permute-start.113
  1174.9 7.6 collective-permute-start.139
  1205.3 6.5 reshape.1163
  1223.8 6.9 reshape.1162
  1234.7 6.1 maximum_convert_fusion.1
  1244.3 7.2 maximum_convert_fusion
  (1030 shorter events, 729.1 us)
Async XLA Ops:
  8.0 1129.1 %all-reduce.3.cloned.1.call-start = ((), (), s32[]{:S(2)}) async-start(), calls=%async_computation.6 | async-start | bytes 212992 | tf_op jit(solution)/shard_map/psum | solution.py:553
  14.4 62.1 %collective-permute-start.39 = (bf16[136,1088]{1,0:T(8,128)(2,1)S(1)}, bf16[136,1088]{1,0:T(8,128)(2,1)}, u32[]{:S(2)}, u32[]{:S(2)}) collective-permute-start(bf16[136,1088]{1,0:T(8,128)(2,1)S(1)} %fusion.213), channel_id=1, source_target_pairs={{1,0},{2,1},{3,2},{5,4},{6,5},{7,6},{9,8},{10,9},{11,10},{13,12},{... | collective-permute-start | bytes 887816 | tf_op jit(solution)/shard_map/ppermute | solution.py:343
  15.7 62.1 %collective-permute-start.40 = (bf16[136,1088]{1,0:T(8,128)(2,1)S(1)}, bf16[136,1088]{1,0:T(8,128)(2,1)}, u32[]{:S(2)}, u32[]{:S(2)}) collective-permute-start(bf16[136,1088]{1,0:T(8,128)(2,1)S(1)} %fusion.213), channel_id=1, source_target_pairs={{0,1},{1,2},{2,3},{4,5},{5,6},{6,7},{8,9},{9,10},{10,11},{12,13},{... | collective-permute-start | bytes 887816 | tf_op jit(solution)/shard_map/ppermute | solution.py:342
  23.2 56.3 %collective-permute-start = (bf16[136,1088]{1,0:T(8,128)(2,1)}, bf16[136,1088]{1,0:T(8,128)(2,1)}, u32[]{:S(2)}, u32[]{:S(2)}) collective-permute-start(bf16[136,1088]{1,0:T(8,128)(2,1)} %fusion.214), channel_id=1, source_target_pairs={{1,0},{2,1},{3,2},{5,4},{6,5},{7,6},{9,8},{10,9},{11,10},{13,12},{... | collective-permute-start | bytes 887816 | tf_op jit(solution)/shard_map/ppermute | solution.py:343
  24.6 56.2 %collective-permute-start.1 = (bf16[136,1088]{1,0:T(8,128)(2,1)}, bf16[136,1088]{1,0:T(8,128)(2,1)}, u32[]{:S(2)}, u32[]{:S(2)}) collective-permute-start(bf16[136,1088]{1,0:T(8,128)(2,1)} %fusion.214), channel_id=1, source_target_pairs={{0,1},{1,2},{2,3},{4,5},{5,6},{6,7},{8,9},{9,10},{10,11},{12,13},{... | collective-permute-start | bytes 887816 | tf_op jit(solution)/shard_map/ppermute | solution.py:342
  34.9 56.0 %collective-permute-start.14 = (bf16[136,1088]{1,0:T(8,128)(2,1)}, bf16[136,1088]{1,0:T(8,128)(2,1)}, u32[]{:S(2)}, u32[]{:S(2)}) collective-permute-start(bf16[136,1088]{1,0:T(8,128)(2,1)} %fusion.485), channel_id=1, source_target_pairs={{0,1},{1,2},{2,3},{4,5},{5,6},{6,7},{8,9},{9,10},{10,11},{12,13},{... | collective-permute-start | bytes 887816 | tf_op jit(solution)/shard_map/ppermute | solution.py:342
  169.4 39.3 %collective-permute-start.68 = (bf16[136,1088]{1,0:T(8,128)(2,1)S(1)}, bf16[136,1088]{1,0:T(8,128)(2,1)S(1)}, u32[]{:S(2)}, u32[]{:S(2)}) collective-permute-start(bf16[136,1088]{1,0:T(8,128)(2,1)S(1)} %collective-permute-done.67), channel_id=1, source_target_pairs={{2,3},{6,7},{10,11},{14,15},{18,19},{22,23},{26,27},{30,31}} | collective-permute-start | bytes 887816 | tf_op jit(solution)/shard_map/ppermute | solution.py:342
  171.4 47.3 %collective-permute-start.9 = (bf16[4,136,1088]{2,1,0:T(8,128)(2,1)S(1)}, bf16[4,136,1088]{2,1,0:T(8,128)(2,1)S(1)}, u32[]{:S(2)}, u32[]{:S(2)}) collective-permute-start(bf16[4,136,1088]{2,1,0:T(8,128)(2,1)S(1)} %pad_maximum_fusion.4.refs_0_), channel_id=1, source_target_pairs={{0,4},{4,0},{8,12},{12,8},{16,20},{20,16},{24,28},{28,24},{1,5},{5... | collective-permute-start | bytes 3551240 | tf_op jit(solution)/shard_map/ppermute | solution.py:269
  177.7 41.1 %collective-permute-start.7 = (bf16[4,136,1088]{2,1,0:T(8,128)(2,1)S(1)}, bf16[4,136,1088]{2,1,0:T(8,128)(2,1)S(1)}, u32[]{:S(2)}, u32[]{:S(2)}) collective-permute-start(bf16[4,136,1088]{2,1,0:T(8,128)(2,1)S(1)} %pad_maximum_fusion.4.refs_0_), channel_id=1, source_target_pairs={{0,16},{4,12},{8,24},{12,4},{16,0},{20,28},{24,8},{28,20},{1,17},{... | collective-permute-start | bytes 3551240 | tf_op jit(solution)/shard_map/ppermute | solution.py:269
  180.3 53.2 %collective-permute-start.19 = (bf16[4,136,1088]{2,1,0:T(8,128)(2,1)}, bf16[4,136,1088]{2,1,0:T(8,128)(2,1)}, u32[]{:S(2)}, u32[]{:S(2)}) collective-permute-start(bf16[4,136,1088]{2,1,0:T(8,128)(2,1)} %pad_maximum_fusion.5.refs_0_), channel_id=1, source_target_pairs={{0,8},{4,20},{8,0},{12,28},{16,24},{20,4},{24,16},{28,12},{1,9},{5... | collective-permute-start | bytes 3551240 | tf_op jit(solution)/shard_map/ppermute | solution.py:269
  242.0 78.7 %collective-permute-start.22 = (bf16[4,136,1088]{2,1,0:T(8,128)(2,1)}, bf16[4,136,1088]{2,1,0:T(8,128)(2,1)}, u32[]{:S(2)}, u32[]{:S(2)}) collective-permute-start(bf16[4,136,1088]{2,1,0:T(8,128)(2,1)} %pad_maximum_fusion.5.refs_0_), channel_id=1, source_target_pairs={{0,4},{4,0},{8,12},{12,8},{16,20},{20,16},{24,28},{28,24},{1,5},{5... | collective-permute-start | bytes 3551240 | tf_op jit(solution)/shard_map/ppermute | solution.py:269
  243.4 76.7 %collective-permute-start.45 = (bf16[4,136,1088]{2,1,0:T(8,128)(2,1)}, bf16[4,136,1088]{2,1,0:T(8,128)(2,1)}, u32[]{:S(2)}, u32[]{:S(2)}) collective-permute-start(bf16[4,136,1088]{2,1,0:T(8,128)(2,1)} %pad_maximum_fusion.7.refs_0_), channel_id=1, source_target_pairs={{0,8},{4,20},{8,0},{12,28},{16,24},{20,4},{24,16},{28,12},{1,9},{5... | collective-permute-start | bytes 3551240 | tf_op jit(solution)/shard_map/ppermute | solution.py:269
  244.7 78.4 %collective-permute-start.23 = (bf16[4,136,1088]{2,1,0:T(8,128)(2,1)}, bf16[4,136,1088]{2,1,0:T(8,128)(2,1)}, u32[]{:S(2)}, u32[]{:S(2)}) collective-permute-start(bf16[4,136,1088]{2,1,0:T(8,128)(2,1)} %collective-permute-done.19.refs_1_), channel_id=1, source_target_pairs={{0,4},{4,0},{8,12},{12,8},{16,20},{20,16},{24,28},{28,24},{1,5},{5... | collective-permute-start | bytes 3551240 | tf_op jit(solution)/shard_map/ppermute | solution.py:269
  264.4 57.0 %collective-permute-start.24 = (bf16[4,136,1088]{2,1,0:T(8,128)(2,1)}, bf16[4,136,1088]{2,1,0:T(8,128)(2,1)}, u32[]{:S(2)}, u32[]{:S(2)}) collective-permute-start(bf16[4,136,1088]{2,1,0:T(8,128)(2,1)} %collective-permute-done.20.refs_2_), channel_id=1, source_target_pairs={{0,4},{4,0},{8,12},{12,8},{16,20},{20,16},{24,28},{28,24},{1,5},{5... | collective-permute-start | bytes 3551240 | tf_op jit(solution)/shard_map/ppermute | solution.py:269
  266.2 58.3 %collective-permute-start.25 = (bf16[4,136,1088]{2,1,0:T(8,128)(2,1)}, bf16[4,136,1088]{2,1,0:T(8,128)(2,1)}, u32[]{:S(2)}, u32[]{:S(2)}) collective-permute-start(bf16[4,136,1088]{2,1,0:T(8,128)(2,1)} %collective-permute-done.21.refs_3_), channel_id=1, source_target_pairs={{0,4},{4,0},{8,12},{12,8},{16,20},{20,16},{24,28},{28,24},{1,5},{5... | collective-permute-start | bytes 3551240 | tf_op jit(solution)/shard_map/ppermute | solution.py:269
  323.1 41.6 %collective-permute-start.47 = (bf16[4,136,1088]{2,1,0:T(8,128)(2,1)}, bf16[4,136,1088]{2,1,0:T(8,128)(2,1)S(1)}, u32[]{:S(2)}, u32[]{:S(2)}) collective-permute-start(bf16[4,136,1088]{2,1,0:T(8,128)(2,1)} %collective-permute-done.45.refs_1_), channel_id=1, source_target_pairs={{0,16},{4,12},{8,24},{12,4},{16,0},{20,28},{24,8},{28,20},{1,17},{... | collective-permute-start | bytes 3551240 | tf_op jit(solution)/shard_map/ppermute | solution.py:269
  324.5 53.7 %collective-permute-start.59 = (bf16[4,136,1088]{2,1,0:T(8,128)(2,1)S(1)}, bf16[4,136,1088]{2,1,0:T(8,128)(2,1)S(1)}, u32[]{:S(2)}, u32[]{:S(2)}) collective-permute-start(bf16[4,136,1088]{2,1,0:T(8,128)(2,1)S(1)} %copy-done), channel_id=1, source_target_pairs={{0,16},{4,12},{8,24},{12,4},{16,0},{20,28},{24,8},{28,20},{1,17},{... | collective-permute-start | bytes 3551240 | tf_op jit(solution)/shard_map/ppermute | solution.py:269
  338.9 40.5 %collective-permute-start.49 = (bf16[4,136,1088]{2,1,0:T(8,128)(2,1)}, bf16[4,136,1088]{2,1,0:T(8,128)(2,1)S(1)}, u32[]{:S(2)}, u32[]{:S(2)}) collective-permute-start(bf16[4,136,1088]{2,1,0:T(8,128)(2,1)} %collective-permute-done.45.refs_1_), channel_id=1, source_target_pairs={{0,4},{4,0},{8,12},{12,8},{16,20},{20,16},{24,28},{28,24},{1,5},{5... | collective-permute-start | bytes 3551240 | tf_op jit(solution)/shard_map/ppermute | solution.py:269
  352.3 49.5 %collective-permute-start.60 = (bf16[4,136,1088]{2,1,0:T(8,128)(2,1)S(1)}, bf16[4,136,1088]{2,1,0:T(8,128)(2,1)S(1)}, u32[]{:S(2)}, u32[]{:S(2)}) collective-permute-start(bf16[4,136,1088]{2,1,0:T(8,128)(2,1)S(1)} %collective-permute-done.58.refs_1_), channel_id=1, source_target_pairs={{0,16},{4,12},{8,24},{12,4},{16,0},{20,28},{24,8},{28,20},{1,17},{... | collective-permute-start | bytes 3551240 | tf_op jit(solution)/shard_map/ppermute | solution.py:269
  378.2 43.7 %collective-permute-start.61 = (bf16[4,136,1088]{2,1,0:T(8,128)(2,1)S(1)}, bf16[4,136,1088]{2,1,0:T(8,128)(2,1)S(1)}, u32[]{:S(2)}, u32[]{:S(2)}) collective-permute-start(bf16[4,136,1088]{2,1,0:T(8,128)(2,1)S(1)} %copy-done), channel_id=1, source_target_pairs={{0,4},{4,0},{8,12},{12,8},{16,20},{20,16},{24,28},{28,24},{1,5},{5... | collective-permute-start | bytes 3551240 | tf_op jit(solution)/shard_map/ppermute | solution.py:269
  378.2 44.5 %collective-permute-start.32 = (bf16[4,136,1088]{2,1,0:T(8,128)(2,1)S(1)}, bf16[4,136,1088]{2,1,0:T(8,128)(2,1)S(1)}, u32[]{:S(2)}, u32[]{:S(2)}) collective-permute-start(bf16[4,136,1088]{2,1,0:T(8,128)(2,1)S(1)} %pad_maximum_fusion.6.refs_0_), channel_id=1, source_target_pairs={{0,8},{4,20},{8,0},{12,28},{16,24},{20,4},{24,16},{28,12},{1,9},{5... | collective-permute-start | bytes 3551240 | tf_op jit(solution)/shard_map/ppermute | solution.py:269
  379.5 44.5 %collective-permute-start.62 = (bf16[4,136,1088]{2,1,0:T(8,128)(2,1)S(1)}, bf16[4,136,1088]{2,1,0:T(8,128)(2,1)S(1)}, u32[]{:S(2)}, u32[]{:S(2)}) collective-permute-start(bf16[4,136,1088]{2,1,0:T(8,128)(2,1)S(1)} %collective-permute-done.58.refs_1_), channel_id=1, source_target_pairs={{0,4},{4,0},{8,12},{12,8},{16,20},{20,16},{24,28},{28,24},{1,5},{5... | collective-permute-start | bytes 3551240 | tf_op jit(solution)/shard_map/ppermute | solution.py:269
  424.0 63.2 %collective-permute-start.35 = (bf16[4,136,1088]{2,1,0:T(8,128)(2,1)S(1)}, bf16[4,136,1088]{2,1,0:T(8,128)(2,1)S(1)}, u32[]{:S(2)}, u32[]{:S(2)}) collective-permute-start(bf16[4,136,1088]{2,1,0:T(8,128)(2,1)S(1)} %pad_maximum_fusion.6.refs_0_), channel_id=1, source_target_pairs={{0,4},{4,0},{8,12},{12,8},{16,20},{20,16},{24,28},{28,24},{1,5},{5... | collective-permute-start | bytes 3551240 | tf_op jit(solution)/shard_map/ppermute | solution.py:269
  424.0 41.8 %collective-permute-start.33 = (bf16[4,136,1088]{2,1,0:T(8,128)(2,1)S(1)}, bf16[4,136,1088]{2,1,0:T(8,128)(2,1)S(1)}, u32[]{:S(2)}, u32[]{:S(2)}) collective-permute-start(bf16[4,136,1088]{2,1,0:T(8,128)(2,1)S(1)} %pad_maximum_fusion.6.refs_0_), channel_id=1, source_target_pairs={{0,16},{4,12},{8,24},{12,4},{16,0},{20,28},{24,8},{28,20},{1,17},{... | collective-permute-start | bytes 3551240 | tf_op jit(solution)/shard_map/ppermute | solution.py:269
  425.3 53.9 %collective-permute-start.34 = (bf16[4,136,1088]{2,1,0:T(8,128)(2,1)S(1)}, bf16[4,136,1088]{2,1,0:T(8,128)(2,1)S(1)}, u32[]{:S(2)}, u32[]{:S(2)}) collective-permute-start(bf16[4,136,1088]{2,1,0:T(8,128)(2,1)S(1)} %collective-permute-done.32.refs_1_), channel_id=1, source_target_pairs={{0,16},{4,12},{8,24},{12,4},{16,0},{20,28},{24,8},{28,20},{1,17},{... | collective-permute-start | bytes 3551240 | tf_op jit(solution)/shard_map/ppermute | solution.py:269
  452.5 40.8 %collective-permute-start.36 = (bf16[4,136,1088]{2,1,0:T(8,128)(2,1)S(1)}, bf16[4,136,1088]{2,1,0:T(8,128)(2,1)S(1)}, u32[]{:S(2)}, u32[]{:S(2)}) collective-permute-start(bf16[4,136,1088]{2,1,0:T(8,128)(2,1)S(1)} %collective-permute-done.32.refs_1_), channel_id=1, source_target_pairs={{0,4},{4,0},{8,12},{12,8},{16,20},{20,16},{24,28},{28,24},{1,5},{5... | collective-permute-start | bytes 3551240 | tf_op jit(solution)/shard_map/ppermute | solution.py:269
  453.3 39.5 %collective-permute-start.73 = (bf16[4,136,1088]{2,1,0:T(8,128)(2,1)}, bf16[4,136,1088]{2,1,0:T(8,128)(2,1)}, u32[]{:S(2)}, u32[]{:S(2)}) collective-permute-start(bf16[4,136,1088]{2,1,0:T(8,128)(2,1)} %collective-permute-done.71.refs_1_), channel_id=1, source_target_pairs={{0,16},{4,12},{8,24},{12,4},{16,0},{20,28},{24,8},{28,20},{1,17},{... | collective-permute-start | bytes 3551240 | tf_op jit(solution)/shard_map/ppermute | solution.py:269
  487.2 83.3 %collective-permute-start.74 = (bf16[4,136,1088]{2,1,0:T(8,128)(2,1)S(1)}, bf16[4,136,1088]{2,1,0:T(8,128)(2,1)}, u32[]{:S(2)}, u32[]{:S(2)}) collective-permute-start(bf16[4,136,1088]{2,1,0:T(8,128)(2,1)S(1)} %pad_maximum_fusion.9.refs_0_), channel_id=1, source_target_pairs={{0,4},{4,0},{8,12},{12,8},{16,20},{20,16},{24,28},{28,24},{1,5},{5... | collective-permute-start | bytes 3551240 | tf_op jit(solution)/shard_map/ppermute | solution.py:269
  492.8 77.7 %collective-permute-start.75 = (bf16[4,136,1088]{2,1,0:T(8,128)(2,1)}, bf16[4,136,1088]{2,1,0:T(8,128)(2,1)}, u32[]{:S(2)}, u32[]{:S(2)}) collective-permute-start(bf16[4,136,1088]{2,1,0:T(8,128)(2,1)} %collective-permute-done.71.refs_1_), channel_id=1, source_target_pairs={{0,4},{4,0},{8,12},{12,8},{16,20},{20,16},{24,28},{28,24},{1,5},{5... | collective-permute-start | bytes 3551240 | tf_op jit(solution)/shard_map/ppermute | solution.py:269
  492.8 77.7 %collective-permute-start.76 = (bf16[4,136,1088]{2,1,0:T(8,128)(2,1)}, bf16[4,136,1088]{2,1,0:T(8,128)(2,1)}, u32[]{:S(2)}, u32[]{:S(2)}) collective-permute-start(bf16[4,136,1088]{2,1,0:T(8,128)(2,1)} %collective-permute-done.72.refs_2_), channel_id=1, source_target_pairs={{0,4},{4,0},{8,12},{12,8},{16,20},{20,16},{24,28},{28,24},{1,5},{5... | collective-permute-start | bytes 3551240 | tf_op jit(solution)/shard_map/ppermute | solution.py:269
  493.3 77.2 %collective-permute-start.77 = (bf16[4,136,1088]{2,1,0:T(8,128)(2,1)}, bf16[4,136,1088]{2,1,0:T(8,128)(2,1)}, u32[]{:S(2)}, u32[]{:S(2)}) collective-permute-start(bf16[4,136,1088]{2,1,0:T(8,128)(2,1)} %collective-permute-done.73.refs_3_), channel_id=1, source_target_pairs={{0,4},{4,0},{8,12},{12,8},{16,20},{20,16},{24,28},{28,24},{1,5},{5... | collective-permute-start | bytes 3551240 | tf_op jit(solution)/shard_map/ppermute | solution.py:269
  782.8 80.4 %collective-permute-start.119 = (bf16[544,1088]{1,0:T(8,128)(2,1)}, bf16[544,1088]{1,0:T(8,128)(2,1)}, u32[]{:S(2)}, u32[]{:S(2)}) collective-permute-start(bf16[544,1088]{1,0:T(8,128)(2,1)} %convolution_convert_fusion.10), channel_id=1, source_target_pairs={{0,4},{4,0},{8,12},{12,8},{16,20},{20,16},{24,28},{28,24},{1,5},{5... | collective-permute-start | bytes 3551240 | tf_op jit(solution)/shard_map/ppermute | solution.py:269
  783.3 77.1 %collective-permute-start.121 = (bf16[544,1088]{1,0:T(8,128)(2,1)}, bf16[544,1088]{1,0:T(8,128)(2,1)}, u32[]{:S(2)}, u32[]{:S(2)}) collective-permute-start(bf16[544,1088]{1,0:T(8,128)(2,1)} %convolution_convert_fusion.9), channel_id=1, source_target_pairs={{0,4},{4,0},{8,12},{12,8},{16,20},{20,16},{24,28},{28,24},{1,5},{5... | collective-permute-start | bytes 3551240 | tf_op jit(solution)/shard_map/ppermute | solution.py:269
  783.4 94.5 %collective-permute-start.123 = (bf16[544,1088]{1,0:T(8,128)(2,1)}, bf16[544,1088]{1,0:T(8,128)(2,1)}, u32[]{:S(2)}, u32[]{:S(2)}) collective-permute-start(bf16[544,1088]{1,0:T(8,128)(2,1)} %convolution_convert_fusion.8), channel_id=1, source_target_pairs={{0,4},{4,0},{8,12},{12,8},{16,20},{20,16},{24,28},{28,24},{1,5},{5... | collective-permute-start | bytes 3551240 | tf_op jit(solution)/shard_map/ppermute | solution.py:269
  783.9 68.2 %collective-permute-start.117 = (bf16[544,1088]{1,0:T(8,128)(2,1)}, bf16[544,1088]{1,0:T(8,128)(2,1)}, u32[]{:S(2)}, u32[]{:S(2)}) collective-permute-start(bf16[544,1088]{1,0:T(8,128)(2,1)} %convolution_convert_fusion.11), channel_id=1, source_target_pairs={{0,4},{4,0},{8,12},{12,8},{16,20},{20,16},{24,28},{28,24},{1,5},{5... | collective-permute-start | bytes 3551240 | tf_op jit(solution)/shard_map/ppermute | solution.py:269
  811.8 121.0 %collective-permute-start.104 = (bf16[544,1088]{1,0:T(8,128)(2,1)}, bf16[544,1088]{1,0:T(8,128)(2,1)}, u32[]{:S(2)}, u32[]{:S(2)}) collective-permute-start(bf16[544,1088]{1,0:T(8,128)(2,1)} %convolution_convert_fusion.15), channel_id=1, source_target_pairs={{0,4},{4,0},{8,12},{12,8},{16,20},{20,16},{24,28},{28,24},{1,5},{5... | collective-permute-start | bytes 3551240 | tf_op jit(solution)/shard_map/ppermute | solution.py:269
  838.7 354.7 %all-gather.21.cloned.1.call-start = ((), (), s32[]{:S(2)}) async-start(), calls=%async_computation.3 | async-start | bytes 2820096 | tf_op jit(solution)/shard_map/all_gather | solution.py:394
  876.9 37.3 %collective-permute-start.93 = (bf16[544,1088]{1,0:T(8,128)(2,1)S(1)}, bf16[544,1088]{1,0:T(8,128)(2,1)S(1)}, u32[]{:S(2)}, u32[]{:S(2)}) collective-permute-start(bf16[544,1088]{1,0:T(8,128)(2,1)S(1)} %copy-done.193), channel_id=1, source_target_pairs={{0,4},{4,0},{8,12},{12,8},{16,20},{20,16},{24,28},{28,24},{1,5},{5... | collective-permute-start | bytes 3551240 | tf_op jit(solution)/shard_map/ppermute | solution.py:269
  944.5 254.6 %all-gather.17.cloned.1.call-start = ((), (), s32[]{:S(2)}) async-start(), calls=%async_computation.1 | async-start | bytes 2820096 | tf_op jit(solution)/shard_map/all_gather | solution.py:394
  944.5 44.5 %collective-permute-start.110 = (bf16[544,1088]{1,0:T(8,128)(2,1)}, bf16[544,1088]{1,0:T(8,128)(2,1)}, u32[]{:S(2)}, u32[]{:S(2)}) collective-permute-start(bf16[544,1088]{1,0:T(8,128)(2,1)} %convolution_convert_fusion.12), channel_id=1, source_target_pairs={{0,4},{4,0},{8,12},{12,8},{16,20},{20,16},{24,28},{28,24},{1,5},{5... | collective-permute-start | bytes 3551240 | tf_op jit(solution)/shard_map/ppermute | solution.py:269
  958.7 39.4 %collective-permute-start.109 = (bf16[544,1088]{1,0:T(8,128)(2,1)}, bf16[544,1088]{1,0:T(8,128)(2,1)}, u32[]{:S(2)}, u32[]{:S(2)}) collective-permute-start(bf16[544,1088]{1,0:T(8,128)(2,1)} %add_convert_fusion.24), channel_id=1, source_target_pairs={{0,16},{4,12},{8,24},{12,4},{16,0},{20,28},{24,8},{28,20},{1,17},{... | collective-permute-start | bytes 3551240 | tf_op jit(solution)/shard_map/ppermute | solution.py:269
  983.9 51.9 %collective-permute-start.143 = (bf16[544,1088]{1,0:T(8,128)(2,1)}, bf16[544,1088]{1,0:T(8,128)(2,1)}, u32[]{:S(2)}, u32[]{:S(2)}) collective-permute-start(bf16[544,1088]{1,0:T(8,128)(2,1)} %convolution_convert_fusion.3), channel_id=1, source_target_pairs={{0,4},{4,0},{8,12},{12,8},{16,20},{20,16},{24,28},{28,24},{1,5},{5... | collective-permute-start | bytes 3551240 | tf_op jit(solution)/shard_map/ppermute | solution.py:269
  988.9 222.9 %all-gather.19.cloned.1.call-start = ((), (), s32[]{:S(2)}) async-start(), calls=%async_computation.2 | async-start | bytes 2820096 | tf_op jit(solution)/shard_map/all_gather | solution.py:394
  1046.0 171.5 %all-gather.15.cloned.1.call-start = ((), (), s32[]{:S(2)}) async-start(), calls=%async_computation | async-start | bytes 2820096 | tf_op jit(solution)/shard_map/all_gather | solution.py:394
  1046.1 46.2 %collective-permute-start.149 = (bf16[544,1088]{1,0:T(8,128)(2,1)}, bf16[544,1088]{1,0:T(8,128)(2,1)}, u32[]{:S(2)}, u32[]{:S(2)}) collective-permute-start(bf16[544,1088]{1,0:T(8,128)(2,1)} %convolution_convert_fusion), channel_id=1, source_target_pairs={{0,4},{4,0},{8,12},{12,8},{16,20},{20,16},{24,28},{28,24},{1,5},{5... | collective-permute-start | bytes 3551240 | tf_op jit(solution)/shard_map/ppermute | solution.py:269
  1087.2 60.4 %collective-permute-start.136 = (bf16[544,1088]{1,0:T(8,128)(2,1)}, bf16[544,1088]{1,0:T(8,128)(2,1)}, u32[]{:S(2)}, u32[]{:S(2)}) collective-permute-start(bf16[544,1088]{1,0:T(8,128)(2,1)} %convolution_convert_fusion.4), channel_id=1, source_target_pairs={{0,4},{4,0},{8,12},{12,8},{16,20},{20,16},{24,28},{28,24},{1,5},{5... | collective-permute-start | bytes 3551240 | tf_op jit(solution)/shard_map/ppermute | solution.py:269
  1092.2 152.1 %all-gather.25.cloned.1.call-start = ((), (), s32[]{:S(2)}) async-start(), calls=%async_computation.5 | async-start | bytes 2820096 | tf_op jit(solution)/shard_map/all_gather | solution.py:394
  1144.2 100.2 %all-gather.23.cloned.1.call-start = ((), (), s32[]{:S(2)}) async-start(), calls=%async_computation.4 | async-start | bytes 2820096 | tf_op jit(solution)/shard_map/all_gather | solution.py:394
  (322 other events, 5286.2 us)
Sparse Core Ops, SparseCore 0:
  838.8 120.8 all-reduce.2
Sparse Core Ops, SparseCore 1:
  944.6 32.7 all-gather.20
  989.0 32.5 all-gather.16
  1046.1 32.1 all-gather.18
  1092.3 31.1 all-gather.14
  1144.2 27.3 all-gather.24
  1193.5 26.7 all-gather.22

commit v2 on v1

--- a/solution.py
+++ b/solution.py
@@ -176,7 +176,7 @@
     )
 
 
-def backward_layer(grad_out, weights, saved, allowed):
+def backward_layer(grad_out, weights, saved, allowed, layout, pipe, sum_group):
     small, qkv_weight, out_weight, up_weight, down_weight = weights
     (
         norm1_gain,
@@ -194,10 +194,14 @@
     )
     width = stream.shape[1]
     grad_branch = grad_out.astype(jnp.bfloat16)
+    sum_group("down", down_product(layout, activated, grad_branch))
+    grad_branch = pipe.advance(grad_branch)
     grad_down_bias = jnp.sum(grad_branch.astype(jnp.float32), axis=0)
     grad_act = jnp.einsum("td,fd->tf", grad_branch, down_weight, preferred_element_type=jnp.float32)
     gelu_value, gelu_pull = jax.vjp(gelu_tanh, hidden_pre)
     grad_pre = gelu_pull(grad_act)[0].astype(jnp.bfloat16)
+    sum_group("up", up_product(layout, normed_two, grad_pre))
+    grad_pre = pipe.advance(grad_pre)
     grad_up_bias = jnp.sum(grad_pre.astype(jnp.float32), axis=0)
     grad_normed_two = dot_columns_back(grad_pre, up_weight)
     norm_value, norm_pull = jax.vjp(
@@ -208,7 +212,10 @@
     grad_attn = grad_after.astype(jnp.bfloat16)
     grad_out_bias = jnp.sum(grad_attn.astype(jnp.float32), axis=0)
     grad_mixed = dot_columns_back(grad_attn, out_weight).astype(jnp.bfloat16)
+    grad_mixed = pipe.advance(grad_mixed)
     grad_projected = attend_back(projected, log_total, grad_mixed, allowed)
+    sum_group("first", first_product(layout, normed, grad_projected, mixed, grad_attn))
+    grad_projected = pipe.advance(grad_projected)
     grad_query_bias = jnp.sum(grad_projected[:, :width].astype(jnp.float32), axis=0)
     grad_value_bias = jnp.sum(grad_projected[:, 2 * width :].astype(jnp.float32), axis=0)
     grad_normed = dot_columns_back(grad_projected, qkv_weight)
@@ -227,17 +234,7 @@
         grad_up_bias,
         grad_down_bias,
     )
-    operands = (
-        normed,
-        grad_projected,
-        mixed,
-        grad_attn,
-        normed_two,
-        grad_pre,
-        activated,
-        grad_branch,
-    )
-    return (grad_after + grad_stream, vectors, operands)
+    return (grad_after + grad_stream, vectors)
 
 
 class Layout:
@@ -285,15 +282,14 @@
 
 
 def place_kernel(by_shard, index_ref, *refs):
-    chips_cores = (len(refs) - 2)
-    blocks, out_ref, sems = refs[:chips_cores], refs[chips_cores], refs[chips_cores + 1]
+    count = len(refs) - 2
+    blocks, out_ref, sems = refs[:count], refs[count], refs[count + 1]
     shards = blocks[0].shape[0]
     copies = []
-    for p in range(chips_cores):
+    for p in range(count):
         chip, core = index_ref[0, p], index_ref[1, p]
         for s in range(shards):
-            shard = index_ref[2, s]
-            target = out_ref.at[shard, chip, core] if by_shard else out_ref.at[chip, shard, core]
+            target = out_ref.at[s, chip, core] if by_shard else out_ref.at[chip, s, core]
             copies.append(pltpu.make_async_copy(blocks[p].at[s], target, sems.at[p * shards + s]))
             copies[-1].start()
     for copy in copies:
@@ -301,23 +297,12 @@
 
 
 def assemble(layout, blocks, by_shard):
-    _, _, core, shard = layout.place()
+    _, _, core, _ = layout.place()
     chips, shards = layout.chips, layout.shards
     own = [layout.chip_at(core, -f, -k) for f, k in layout.slots()]
     other = [layout.chip_at(1 - core, -f, -k) for f, k in layout.slots()]
     count = 2 * chips
-    width = max(count, shards)
-
-    def row(values):
-        return jnp.stack(list(values) + [jnp.int32(0)] * (width - len(values)))
-
-    index = jnp.stack(
-        [
-            row(own + other),
-            row([core] * chips + [1 - core] * chips),
-            row([(shard + s) % shards for s in range(shards)]),
-        ]
-    ).astype(jnp.int32)
+    index = jnp.stack([jnp.stack(own + other), jnp.stack([core] * chips + [1 - core] * chips)])
     _, rows, cols = blocks[0].shape
     outer = (shards, chips) if by_shard else (chips, shards)
     return pl.pallas_call(
@@ -331,22 +316,11 @@
         cost_estimate=pl.CostEstimate(
             flops=0, bytes_accessed=4 * count * shards * rows * cols, transcendentals=0
         ),
-    )(index, *blocks)
-
-
-def gather_shards(layout, piece):
-    n = layout.shards
-    _, _, _, shard = layout.place()
-    right, left = [piece], [piece]
-    for t in range(1, n):
-        right.append(lax.ppermute(right[-1], "shard", [(i, i + 1) for i in range(t - 1, n - 1)]))
-        left.append(lax.ppermute(left[-1], "shard", [(i, i - 1) for i in range(1, n - t + 1)]))
-    parts = [piece] + [jnp.where(shard + k < n, left[k], right[n - k]) for k in range(1, n)]
-    return jnp.stack(parts)
+    )(index.astype(jnp.int32), *blocks)
 
 
 def gather_group(layout, piece, by_shard):
-    block = gather_shards(layout, piece)
+    block = lax.all_gather(piece, "shard", axis=0, tiled=False)
     held = {(0, 0): block}
     held[1, 0] = layout.move(block, "first")
     for k in range(1, layout.across):
@@ -361,108 +335,185 @@
     return (left.astype(jnp.float32) + right.astype(jnp.float32)).astype(jnp.bfloat16)
 
 
-def reduce_shards(layout, parts):
-    n = layout.shards
-    right = left = None
-    for t in range(1, n):
-        right = parts[n - t] if right is None else add_low(parts[n - t], right)
-        left = parts[t] if left is None else add_low(parts[t], left)
-        right = lax.ppermute(right, "shard", [(i, i + 1) for i in range(min(t, n - 1))])
-        left = lax.ppermute(left, "shard", [(i, i - 1) for i in range(max(1, n - t), n)])
-    total = parts[0].astype(jnp.float32) + right.astype(jnp.float32) + left.astype(jnp.float32)
-    return total.astype(jnp.bfloat16)
-
-
-def reduce_group(layout, product):
+def reduce_steps(layout, product, finish):
     _, _, core, _ = layout.place()
-    n = layout.shards
+    n, last = layout.shards, layout.across - 1
+    away = {
+        (f, k): product(layout.chip_at(1 - core, f, k), 1 - core).astype(jnp.bfloat16)
+        for f, k in layout.slots()
+    }
+    came = {slot: layout.move(value, "core") for slot, value in away.items()}
+    yield list(away.values())
     sums = {}
     for f, k in layout.slots():
-        away = product(layout.chip_at(1 - core, f, k), 1 - core).astype(jnp.bfloat16)
-        came = layout.move(away, "core")
         here = product(layout.chip_at(core, f, k), core)
-        sums[f, k] = (here + came.astype(jnp.float32)).astype(jnp.bfloat16)
-    halves = []
-    for f in range(2):
-        total = sums[f, layout.across - 1]
-        for step in range(1, layout.across):
-            total = add_low(layout.move(total, "second"), sums[f, layout.across - 1 - step])
-        halves.append(total)
-    total = add_low(layout.move(halves[1], "first"), halves[0])
+        sums[f, k] = (here + came[f, k].astype(jnp.float32)).astype(jnp.bfloat16)
+    totals = [sums[f, last] for f in range(2)]
+    for step in range(1, layout.across):
+        moved = [layout.move(total, "second") for total in totals]
+        if step == 1:
+            yield list(sums.values())
+        totals = [add_low(moved[f], sums[f, last - step]) for f in range(2)]
+    moved = layout.move(totals[1], "first")
+    yield totals
+    total = add_low(moved, totals[0])
     total = total.reshape((n, total.shape[0] // n) + total.shape[1:])
-    piece = reduce_shards(layout, [total[s] for s in range(n)])
-    return lax.all_gather(piece, "replica", axis=0, tiled=False)
-
-
-def rolled(value, shift):
-    return lax.dynamic_slice_in_dim(
-        jnp.concatenate([value, value], axis=0), shift, value.shape[0], axis=0
-    )
-
-
-def by_shard_rows(layout, rows, chips):
+    piece = lax.psum_scatter(total, "shard", scatter_dimension=0, tiled=False)
+    yield [total]
+    moved = layout.move(piece, "first")
+    yield [piece]
+    held = [jnp.stack([piece, moved])]
+    for _ in range(1, layout.across):
+        held.append(layout.move(held[-1], "second"))
+    yield [held[0]]
+    own = jnp.concatenate(held, axis=0)
+    other = layout.move(own, "core")
+    yield [own]
+    finish(jnp.concatenate([own, other], axis=0))
+
+
+class Pipe:
+    def __init__(self):
+        self.running = []
+
+    def begin(self, steps):
+        self.running.append(steps)
+
+    def advance(self, value):
+        issued, kept = [], []
+        for steps in self.running:
+            try:
+                issued.extend(next(steps))
+                kept.append(steps)
+            except StopIteration:
+                pass
+        self.running = kept
+        return lax.optimization_barrier((value, issued))[0]
+
+    def drain(self):
+        while self.running:
+            self.advance(jnp.zeros((), jnp.float32))
+
+
+def by_core_rows(layout, rows, chips):
+    n = layout.shards
+    block = rows.T.reshape(n, chips, 2, rows.shape[1] // (2 * n * chips), rows.shape[0])
+    return block.transpose(1, 2, 0, 3, 4).reshape(chips, 2, -1, rows.shape[0])
+
+
+def column_chunks(layout, rows):
+    return rows.reshape(rows.shape[0], layout.chips, -1).transpose(1, 0, 2)
+
+
+def pick(value, i):
+    return lax.dynamic_index_in_dim(value, i, axis=0, keepdims=False)
+
+
+def down_product(layout, activated, grad_branch):
+    rows = by_core_rows(layout, activated, layout.chips)
+
+    def product(chip, core):
+        return jnp.dot(pick(pick(rows, chip), core), grad_branch, preferred_element_type=jnp.float32)
+
+    return product
+
+
+def up_product(layout, normed_two, grad_pre):
+    rows = by_core_rows(layout, normed_two, 1)[0]
+    chunks = column_chunks(layout, grad_pre)
+
+    def product(chip, core):
+        return jnp.dot(pick(rows, core), pick(chunks, chip), preferred_element_type=jnp.float32)
+
+    return product
+
+
+def first_product(layout, normed, grad_projected, mixed, grad_attn):
+    one_rows = by_core_rows(layout, normed, 1)[0]
+    mixed_rows = by_core_rows(layout, mixed, 1)[0]
+    chunks = column_chunks(layout, jnp.concatenate([grad_projected, grad_attn], axis=1))
+
+    def product(chip, core):
+        rows = jnp.where(
+            chip < 3 * layout.chips // 4, pick(one_rows, core), pick(mixed_rows, core)
+        )
+        return jnp.dot(rows, pick(chunks, chip), preferred_element_type=jnp.float32)
+
+    return product
+
+
+def block_order(layout):
+    _, _, core, _ = layout.place()
+    labels = [layout.chip_at(core, -f, -k) * 2 + core for f, k in layout.slots()]
+    labels += [layout.chip_at(1 - core, -f, -k) * 2 + 1 - core for f, k in layout.slots()]
+    wanted = jnp.arange(len(labels), dtype=jnp.int32)
+    return jnp.argmax(wanted[:, None] == jnp.stack(labels)[None, :], axis=1).astype(jnp.int32)
+
+
+def sum_vectors(layout, vectors):
     n = layout.shards
     _, _, _, shard = layout.place()
-    turned = rows.T.reshape(n, chips, 2, rows.shape[1] // (2 * n * chips), rows.shape[0])
-    return rolled(turned, shard).transpose(1, 2, 0, 3, 4)
-
-
-def column_chunks(layout, rows):
-    return rows.reshape(rows.shape[0], layout.chips, -1).transpose(1, 0, 2)
-
-
-def weight_sums(layout, operands):
-    normed, grad_projected, mixed, grad_attn, normed_two, grad_pre, activated, grad_branch = (
-        operands
-    )
-    chips = layout.chips
-
-    def flat(block):
-        return block.reshape(-1, block.shape[-1])
-
-    def pick(value, i):
-        return lax.dynamic_index_in_dim(value, i, axis=0, keepdims=False)
-
-    act_rows = by_shard_rows(layout, activated, chips)
-
-    def down_product(chip, core):
-        return jnp.dot(
-            flat(pick(pick(act_rows, chip), core)), grad_branch, preferred_element_type=jnp.float32
-        )
-
-    two_rows = by_shard_rows(layout, normed_two, 1)[0]
-    pre_chunks = column_chunks(layout, grad_pre)
-
-    def up_product(chip, core):
-        return jnp.dot(
-            flat(pick(two_rows, core)), pick(pre_chunks, chip), preferred_element_type=jnp.float32
-        )
-
-    one_rows = by_shard_rows(layout, normed, 1)[0]
-    mixed_rows = by_shard_rows(layout, mixed, 1)[0]
-    first_chunks = column_chunks(layout, jnp.concatenate([grad_projected, grad_attn], axis=1))
-
-    def first_product(chip, core):
-        rows = jnp.where(chip < 3 * chips // 4, pick(one_rows, core), pick(mixed_rows, core))
-        return jnp.dot(flat(rows), pick(first_chunks, chip), preferred_element_type=jnp.float32)
-
-    down = reduce_group(layout, down_product)
-    up = reduce_group(layout, up_product)
-    first = reduce_group(layout, first_product)
-
-    def columns(gathered):
-        blocks = gathered.reshape((chips, 2) + gathered.shape[1:])
-        blocks = blocks.transpose(1, 2, 0, 3)
-        return blocks.reshape(blocks.shape[0] * blocks.shape[1], -1).astype(jnp.float32)
-
-    first = columns(first)
-    width = first.shape[1] // 4
-    return (
-        first[:, : 3 * width],
-        first[:, 3 * width :],
-        columns(up),
-        flat(down).astype(jnp.float32),
-    )
+    parts = jnp.concatenate([vector.reshape(n, -1) for vector in vectors], axis=1)
+    total = pick(parts, (shard + n - 1) % n)
+    for step in range(1, n):
+        total = lax.ppermute(total, "shard", [(i, (i + 1) % n) for i in range(n)])
+        total = total + pick(parts, (shard + 2 * n - 1 - step) % n)
+    bit = 1
+    while bit < layout.copies:
+        pairs = [(i, i ^ bit) for i in range(layout.copies)]
+        total = total + lax.ppermute(total, "replica", pairs)
+        bit *= 2
+    out, at = [], 0
+    for vector in vectors:
+        size = vector.shape[0] // n
+        out.append(total[at : at + size])
+        at += size
+    return out
+
+
+def write_kernel(by_rows, splits, order_ref, blocks_ref, *refs):
+    outs = refs[-len(splits) :]
+    chips = blocks_ref.shape[0] // 2
+    rows, width = blocks_ref.shape[1:]
+    if by_rows:
+        for i in range(2 * chips):
+            outs[0][0, i * rows : (i + 1) * rows, :] = blocks_ref[order_ref[i]].astype(jnp.float32)
+        return
+    for core in range(2):
+        at = 0
+        for out, count in zip(outs, splits):
+            line = [
+                blocks_ref[order_ref[2 * (at + i) + core]].astype(jnp.float32) for i in range(count)
+            ]
+            out[0, core * rows : (core + 1) * rows, :] = jnp.concatenate(line, axis=1)
+            at += count
+
+
+def write_layer(layout, whole, layer, count, by_rows, splits, held):
+    blocks, rows, width = whole.shape
+    if by_rows:
+        shapes = [(count, blocks * rows, width)]
+    else:
+        shapes = [(count, 2 * rows, split * width) for split in splits]
+    held = [] if held is None else held
+    return pl.pallas_call(
+        functools.partial(write_kernel, by_rows, splits),
+        out_shape=[jax.ShapeDtypeStruct(shape, jnp.float32) for shape in shapes],
+        grid=(1,),
+        in_specs=[
+            pl.BlockSpec(memory_space=pltpu.SMEM),
+            pl.BlockSpec(whole.shape, lambda i: (0, 0, 0)),
+        ]
+        + [pl.BlockSpec(memory_space=pl.ANY)] * len(held),
+        out_specs=[
+            pl.BlockSpec((1,) + shape[1:], lambda i, layer=layer: (layer, 0, 0)) for shape in shapes
+        ],
+        input_output_aliases={2 + i: i for i in range(len(held))},
+        compiler_params=pltpu.CompilerParams(vmem_limit_bytes=48 << 20),
+        cost_estimate=pl.CostEstimate(
+            flops=0, bytes_accessed=6 * blocks * rows * width, transcendentals=0
+        ),
+    )(block_order(layout), whole, *held)
 
 
 def solution(mesh):
@@ -509,14 +560,24 @@
             rows, cols = weight.shape[0] // 2, weight.shape[1] // chips
             return lax.dynamic_slice(weight, (core * rows, chip * cols), (rows, cols))
 
+        def own_first(one, two):
+            cut = 3 * chips // 4
+            rows, cols = one.shape[0] // 2, one.shape[1] // cut
+            from_one = lax.dynamic_slice(
+                one, (core * rows, jnp.minimum(chip, cut - 1) * cols), (rows, cols)
+            )
+            from_two = lax.dynamic_slice(
+                two, (core * rows, jnp.maximum(chip - cut, 0) * cols), (rows, cols)
+            )
+            return jnp.where(chip < cut, from_one, from_two)
+
         def own_rows(weight):
             rows = weight.shape[0] // (2 * chips)
             return lax.dynamic_slice_in_dim(weight, (chip * 2 + core) * rows, rows, axis=0)
 
         weights = []
         for l in range(layer_count):
-            first_piece = own_columns(jnp.concatenate([qkv_weight[l], out_weight[l]], axis=1))
-            first = gather_group(layout, first_piece, False)
+            first = gather_group(layout, own_first(qkv_weight[l], out_weight[l]), False)
             up = gather_group(layout, own_columns(up_weight[l]), False)
             down = gather_group(layout, own_rows(down_weight[l]), True)
             first = first.reshape(chips, -1, first.shape[-1])
@@ -546,37 +607,52 @@
         block_out = stream.astype(jnp.bfloat16)
         grad_stream = cotangent.astype(jnp.float32)
         shares = [None] * layer_count
+        pipe = Pipe()
+        held = {"first": None, "up": None, "down": None}
+
+        def sum_group(name, l, product):
+            cut = 3 * chips // 4
+            splits = (cut, chips - cut) if name == "first" else (chips,)
+
+            def finish(whole):
+                held[name] = write_layer(
+                    layout, whole, l, layer_count, name == "down", splits, held[name]
+                )
+
+            pipe.begin(reduce_steps(layout, product, finish))
+
         for l in reversed(range(layer_count)):
-            grad_stream, vectors, operands = backward_layer(
-                grad_stream, weights[l], saved_all[l], allowed
+            grad_stream, vectors = backward_layer(
+                grad_stream,
+                weights[l],
+                saved_all[l],
+                allowed,
+                layout,
+                pipe,
+                lambda name, product, l=l: sum_group(name, l, product),
             )
-            sums = lax.psum(jnp.concatenate(vectors), ("replica", "shard"))
-            small, at = [], 0
-            for vector in vectors:
-                size = vector.shape[0] // shards
-                small.append(lax.dynamic_slice_in_dim(sums, at + shard * size, size))
-                at += vector.shape[0]
-            shares[l] = (small, weight_sums(layout, operands))
-
-        def stacked(group, i):
-            return jnp.stack([share[group][i] for share in shares])
+            shares[l] = sum_vectors(layout, vectors)
+        pipe.drain()
+
+        def stacked(i):
+            return jnp.stack([share[i] for share in shares])
 
         return (
             block_out,
             grad_stream,
-            stacked(0, 0),
-            stacked(0, 1),
-            stacked(1, 0),
-            stacked(0, 2),
-            stacked(0, 3),
-            stacked(1, 1),
-            stacked(0, 4),
-            stacked(0, 5),
-            stacked(0, 6),
-            stacked(1, 2),
-            stacked(0, 7),
-            stacked(1, 3),
-            stacked(0, 8),
+            stacked(0),
+            stacked(1),
+            held["first"][0],
+            stacked(2),
+            stacked(3),
+            held["first"][1],
+            stacked(4),
+            stacked(5),
+            stacked(6),
+            held["up"][0],
+            stacked(7),
+            held["down"][0],
+            stacked(8),
         )
 
     rows = P(("replica", "shard"), None)

time: 1280 us -> 1010 us (0.79); the launches traced: 1260 us -> 1010 us
  starting transfers between devices: 204 us -> 75.2 us
  waiting for transfers between devices: 350 us -> 266 us
  local copies, waits for them, and re-layouts: 121 us -> 77.7 us
  other arithmetic: 181 us -> 149 us
  Pallas kernels: 47 us -> 68 us
  matrix products: 327 us -> 341 us
    ppermute x72 -> x12, starting transfers between devices: 160 us -> 9.04 us  [the longest x6 4.91 us: sum_vectors(): total = total + lax.ppermute(total, 'replica', pairs)]
    ppermute x72 -> x12, waiting for transfers between devices: 120 us -> 19.2 us  [the longest x6 14 us: sum_vectors(): total = lax.ppermute(total, 'shard', [(i, (i + 1) % n) for i in range(n)])]
    all_gather x6, waiting for transfers between devices: 0.03 us -> 50.1 us  [gather_group(): block = lax.all_gather(piece, 'shard', axis=0, tiled=False)]
    ppermute x84 -> x102, waiting for transfers between devices: 230 us -> 196 us  [move(): return lax.ppermute(value, 'replica', self.pairs(way))]
    convert_element_type x8 -> x0, local copies, waits for them, and re-layouts: 33.1 us -> none  [columns(): blocks.reshape(blocks.shape[0] * blocks.shape[1], -1).astype(jnp.float32)]
    another operation x39 -> x14, other arithmetic: 32.2 us -> 8.72 us  [the longest x6 4.93 us: reduce_steps(): held = [jnp.stack([piece, moved])]]
    ppermute x84 -> x102, starting transfers between devices: 43.1 us -> 65 us  [move(): return lax.ppermute(value, 'replica', self.pairs(way))]
    pallas_call x0 -> x6, Pallas kernels: none -> 19.3 us  [write_layer(): pl.pallas_call(functools.partial(write_kernel, by_rows, splits), out_shap...]
  transfers between devices with their start and end apart: 163 -> 126, of which waited for: 62 -> 28; matrix products, arithmetic and copies ran while one was open for 31% -> 52% of each run, Pallas kernels for 3% -> 6%
where the time goes in v2:
time: 1010 us
  matrix products  341 us (34%)
  waiting for transfers between devices  266 us (26%)
  other arithmetic  149 us (15%)
  local copies, waits for them, and re-layouts  77.7 us (8%)
  starting transfers between devices  75.2 us (7%)
  Pallas kernels  68 us (7%)
  between operations  17.8 us (2%)
  blocking collectives  13.9 us (1%)
    ppermute x102, waiting for transfers between devices, move(): return lax.ppermute(value, 'replica', self.pairs(way))  196 us
    ppermute x102, starting transfers between devices, move(): return lax.ppermute(value, 'replica', self.pairs(way))  65 us
    all_gather x6, waiting for transfers between devices, gather_group(): block = lax.all_gather(piece, 'shard', axis=0, tiled=False)  50.1 us
    dot_general x16, matrix products, product(): jnp.dot(pick(pick(rows, chip), core), grad_branch, preferred_element_type...  48.8 us
    pallas_call x6, Pallas kernels, assemble(): pl.pallas_call(functools.partial(place_kernel, by_shard), out_shape=jax.S...  48.7 us
    dot_general x16, matrix products, dot_columns_back(): jnp.einsum('te,de->td', rows[:, i * width:(i + 1) * width], chunk, prefer...  39.6 us
    dot_general x16, matrix products, product(): jnp.dot(pick(rows, core), pick(chunks, chip), preferred_element_type=jnp....  39.1 us
    dot_general x16, matrix products, product(): return jnp.dot(rows, pick(chunks, chip), preferred_element_type=jnp.float32)  38.7 us
  transfers between devices with their start and end apart: 126, of which 28 were waited for; matrix products, arithmetic and copies ran while one was open for 52% of the time, Pallas kernels for 6%

profile of v2, /device:TPU:0, one launch (start us, length us, event | category | flops | bytes accessed | tf_op | source)
XLA Modules:
  0.0 1008.7 jit_solution(15726212636147610975)
XLA Ops:
  26.0 22.5 %all-gather.9.cloned.1.call-done.refs_0_ = bf16[4,136,1088]{2,1,0:T(8,128)(2,1)} async-done(((bf16[1,136,1088]{2,1,0:T(8,128)(2,1)}), bf16[4,136,1088]{2,1,0:T(8,128)(2,1)}) %all-gather.9.cloned.1.call-update) | async-done | bytes 1183760 | tf_op jit(solution)/shard_map/all_gather | solution.py:323
  53.7 27.7 %all-gather.11.cloned.1.call-done.refs_0_ = bf16[4,136,1088]{2,1,0:T(8,128)(2,1)} async-done(((bf16[1,136,1088]{2,1,0:T(8,128)(2,1)}), bf16[4,136,1088]{2,1,0:T(8,128)(2,1)}) %all-gather.11.cloned.1.call-update) | async-done | bytes 1183760 | tf_op jit(solution)/shard_map/all_gather | solution.py:323
  84.3 13.9 %all-gather.1 = bf16[4,2,3264]{2,1,0:T(2,128)(2,1)S(1)} all-gather(bf16[1,2,3264]{2,1,0:T(2,128)(2,1)S(1)} %bitcast.710), channel_id=2, replica_groups=mesh['replica'=8,'shard'=4] {'shard'}, dimensions={0}, use_global_device_ids=true | all-gather | bytes 65280 | tf_op jit(solution)/shard_map/all_gather | solution.py:557
  106.1 5.9 collective-permute-done.7.refs_1_
  118.6 5.2 collective-permute-done.8.refs_2_
  126.6 19.7 %collective-permute-done.9.refs_3_ = bf16[4,136,1088]{2,1,0:T(8,128)(2,1)} collective-permute-done((bf16[4,136,1088]{2,1,0:T(8,128)(2,1)}, bf16[4,136,1088]{2,1,0:T(8,128)(2,1)}, u32[]{:S(2)}, u32[]{:S(2)}) %collective-permute-start.9) | collective-permute-done | bytes 1183776 | tf_op jit(solution)/shard_map/ppermute | solution.py:266
  147.9 8.6 shard_map.271
  156.5 5.7 fusion.457
  171.0 7.9 fusion.2
  178.9 10.3 %fusion = f32[17,512]{1,0:T(8,128)S(1)} fusion(f32[17,512,512]{1,2,0:T(8,128)} %get-tuple-element.152, f32[17,512]{1,0:T(8,128)S(1)} %get-tuple-element.151, pred[512,512]{0,1:T(8,128)(4,1)S(1)} %fusion.167), kind=kLoop, calls=%fused_computation.12 | loop fusion | flops 22273536 | bytes 18157568 | tf_op jit(solution)/shard_map/reduce_sum | solution.py:62
  189.3 9.3 fusion.49
  207.3 8.6 shard_map.272
  215.9 4.8 fusion.456
  235.7 24.2 %collective-permute-done.16.refs_3_ = bf16[4,136,1088]{2,1,0:T(8,128)(2,1)} collective-permute-done((bf16[4,136,1088]{2,1,0:T(8,128)(2,1)}, bf16[4,136,1088]{2,1,0:T(8,128)(2,1)}, u32[]{:S(2)}, u32[]{:S(2)}) %collective-permute-start.16) | collective-permute-done | bytes 1183776 | tf_op jit(solution)/shard_map/ppermute | solution.py:266
  259.9 7.5 multiply_convert_fusion.3
  269.6 5.9 collective-permute-done.23.refs_3_
  276.0 8.6 shard_map.273
  284.6 8.0 fusion.467
  299.6 8.9 shard_map.274
  308.5 5.7 fusion.455
  324.0 8.0 fusion.3
  332.0 10.4 %fusion.1 = f32[17,512]{1,0:T(8,128)S(1)} fusion(f32[17,512,512]{1,2,0:T(8,128)} %get-tuple-element.158, f32[17,512]{1,0:T(8,128)S(1)} %get-tuple-element.157, pred[512,512]{0,1:T(8,128)(4,1)S(1)} %fusion.167), kind=kLoop, calls=%fused_computation.13 | loop fusion | flops 22273536 | bytes 18157568 | tf_op jit(solution)/shard_map/reduce_sum | solution.py:62
  342.4 9.3 fusion.48
  358.0 11.5 %collective-permute-done.37.refs_3_ = bf16[4,136,1088]{2,1,0:T(8,128)(2,1)S(1)} collective-permute-done((bf16[4,136,1088]{2,1,0:T(8,128)(2,1)}, bf16[4,136,1088]{2,1,0:T(8,128)(2,1)S(1)}, u32[]{:S(2)}, u32[]{:S(2)}) %collective-permute-start.37) | collective-permute-done | bytes 1183776 | tf_op jit(solution)/shard_map/ppermute | solution.py:266
  369.6 7.4 shard_map.275
  377.0 4.8 fusion.454
  395.0 8.1 multiply_convert_fusion.2
  414.8 6.6 shard_map.276
  421.5 19.1 %fusion.17 = bf16[512,4352]{0,1:T(8,128)(2,1)} fusion(f32[512,1088]{0,1:T(8,128)} %fusion.482, f32[512,1088]{0,1:T(8,128)} %fusion.481, f32[512,1088]{0,1:T(8,128)} %fusion.480, f32[512,1088]{0,1:T(8,128)} %fusion.479, f32[4352]{0:T(1024)S(1)} %copy-done.158, bf16[4352,1088]{1,0:T(8,128)(2,1)} %bitcast.518, bf16[512,1088]{0,1:T(8,128)(2,1)S(1)} %copy-done.34), kind=kOutput, calls=%fused_computation.33 | convolution fusion | flops 4902092800 | bytes 23970816 | tf_op jit(solution)/shard_map/td,fd->tf/dot_general | solution.py:200
  504.1 29.8 %collective-permute-done.54 = bf16[544,1088]{1,0:T(8,128)(2,1)S(1)} collective-permute-done((bf16[544,1088]{1,0:T(8,128)(2,1)S(1)}, bf16[544,1088]{1,0:T(8,128)(2,1)S(1)}, u32[]{:S(2)}, u32[]{:S(2)}) %collective-permute-start.54) | collective-permute-done | bytes 1183776 | tf_op jit(solution)/shard_map/ppermute | solution.py:266
  536.4 8.7 fusion.50
  545.1 12.9 %multiply_reduce_fusion.1 = (f32[17,512]{1,0:T(8,128)S(1)}, f32[17,512,512]{1,2,0:T(8,128)}) fusion(f32[17,512]{1,0:T(8,128)S(1)} %log_add_fusion.1, f32[17,512,512]{1,2,0:T(8,128)} %get-tuple-element.158, pred[512,512]{0,1:T(8,128)(4,1)S(1)} %fusion.167, bf16[512,17,64]{0,2,1:T(8,128)(2,1)S(1)} %bitcast.716, bf16[512,17,64]{0,2,1:T(8,128)(2,1)S(1)} %bitcast.673), kind=kOutput, calls=%fused_computation.4 | convolution fusion | flops 597155328 | bytes 38211584 | tf_op jit(solution)/shard_map/qhd,khd->hqk/dot_general | solution.py:82
  558.0 13.4 %multiply_convert_fusion.1 = bf16[17,512,512]{1,2,0:T(8,128)(2,1)S(1)} fusion(f32[17,512,512]{1,2,0:T(8,128)} %get-tuple-element.163, f32[17,512]{1,0:T(8,128)S(1)} %get-tuple-element.162, f32[17,512]{1,0:T(8,128)S(1)} %log_add_fusion.1, f32[17,512,512]{1,2,0:T(8,128)} %get-tuple-element.158, pred[512,512]{0,1:T(8,128)(4,1)S(1)} %fusion.167), kind=kLoop, calls=%fused_computation.3 | loop fusion | flops 31195136 | bytes 44896256 | tf_op jit(solution)/shard_map/convert_element_type | solution.py:86
  602.0 5.7 fusion.448
  610.8 5.1 fusion.452
  622.2 10.3 %fusion.40 = bf16[512,1088]{0,1:T(8,128)(2,1)} fusion(f32[512,1088]{0,1:T(8,128)S(1)} %copy-done.16, bf16[512,4352]{0,1:T(8,128)(2,1)S(1)} %bitcast.504, bf16[4352,1088]{1,0:T(8,128)(2,1)} %bitcast.519, f32[1088]{0:T(1024)S(1)} %copy-done.178), kind=kOutput, calls=%fused_computation.108 | convolution fusion | flops 4850286592 | bytes 17273088 | tf_op jit(solution)/shard_map/dot_general | solution.py:160
  678.3 17.6 %fusion.10 = bf16[512,4352]{0,1:T(8,128)(2,1)S(1)} fusion(f32[512,1088]{0,1:T(8,128)} %copy-done.113, f32[512,1088]{0,1:T(8,128)} %copy-done.114, f32[512,1088]{0,1:T(8,128)} %copy-done.115, f32[512,1088]{0,1:T(8,128)} %copy-done.116, f32[4352]{0:T(1024)S(1)} %copy-done.157, bf16[4352,1088]{1,0:T(8,128)(2,1)} %bitcast.517, bf16[512,1088]{0,1:T(8,128)(2,1)S(1)} %copy-done.63), kind=kOutput, calls=%fused_computation.26 | convolution fusion | flops 4902092800 | bytes 23970816 | tf_op jit(solution)/shard_map/td,fd->tf/dot_general | solution.py:200
  715.5 6.4 collective-permute-done.67
  737.9 14.5 %collective-permute-done.61 = bf16[544,1088]{1,0:T(8,128)(2,1)S(1)} collective-permute-done((bf16[544,1088]{1,0:T(8,128)(2,1)S(1)}, bf16[544,1088]{1,0:T(8,128)(2,1)S(1)}, u32[]{:S(2)}, u32[]{:S(2)}) %collective-permute-start.61) | collective-permute-done | bytes 1183776 | tf_op jit(solution)/shard_map/ppermute | solution.py:266
  769.8 8.3 collective-permute-done.70
  782.1 9.7 fusion.53
  791.8 13.0 %multiply_reduce_fusion = (f32[17,512]{1,0:T(8,128)S(1)}, f32[17,512,512]{1,2,0:T(8,128)}) fusion(f32[17,512]{1,0:T(8,128)S(1)} %log_add_fusion, f32[17,512,512]{1,2,0:T(8,128)} %get-tuple-element.152, pred[512,512]{0,1:T(8,128)(4,1)S(1)} %fusion.167, bf16[512,17,64]{0,2,1:T(8,128)(2,1)S(1)} %bitcast.718, bf16[512,17,64]{0,2,1:T(8,128)(2,1)S(1)} %bitcast.671), kind=kOutput, calls=%fused_computation.1 | convolution fusion | flops 597155328 | bytes 38211584 | tf_op jit(solution)/shard_map/qhd,khd->hqk/dot_general | solution.py:82
  804.9 13.7 %multiply_convert_fusion = bf16[17,512,512]{1,2,0:T(8,128)(2,1)S(1)} fusion(f32[17,512,512]{1,2,0:T(8,128)} %get-tuple-element.167, f32[17,512]{1,0:T(8,128)S(1)} %get-tuple-element.166, f32[17,512]{1,0:T(8,128)S(1)} %log_add_fusion, f32[17,512,512]{1,2,0:T(8,128)} %get-tuple-element.152, pred[512,512]{0,1:T(8,128)(4,1)S(1)} %fusion.167), kind=kLoop, calls=%fused_computation | loop fusion | flops 31195136 | bytes 44896256 | tf_op jit(solution)/shard_map/convert_element_type | solution.py:86
  855.8 31.7 %collective-permute-done.93 = bf16[544,1088]{1,0:T(8,128)(2,1)S(1)} collective-permute-done((bf16[544,1088]{1,0:T(8,128)(2,1)S(1)}, bf16[544,1088]{1,0:T(8,128)(2,1)S(1)}, u32[]{:S(2)}, u32[]{:S(2)}) %collective-permute-start.93) | collective-permute-done | bytes 1183776 | tf_op jit(solution)/shard_map/ppermute | solution.py:266
  938.5 5.2 collective-permute-done.84
  953.0 4.7 collective-permute-done.110
  965.4 5.7 collective-permute-done.99
  979.6 5.5 collective-permute-done.100
  (952 shorter events, 465.3 us)
Async XLA Ops:
  13.9 67.5 %all-gather.11.cloned.1.call-start = ((), (), s32[]{:S(2)}) async-start(), calls=%async_computation.7 | async-start | bytes 1566720 | tf_op jit(solution)/shard_map/all_gather | solution.py:323
  17.6 107.6 %all-gather.13.cloned.1.call-start = ((), (), s32[]{:S(2)}) async-start(), calls=%async_computation.8 | async-start | bytes 1566720 | tf_op jit(solution)/shard_map/all_gather | solution.py:323
  22.8 181.4 %all-gather.15.cloned.1.call-start = ((), (), s32[]{:S(2)}) async-start(), calls=%async_computation.9 | async-start | bytes 1566720 | tf_op jit(solution)/shard_map/all_gather | solution.py:323
  25.0 243.0 %all-gather.17.cloned.1.call-start = ((), (), s32[]{:S(2)}) async-start(), calls=%async_computation.10 | async-start | bytes 1566720 | tf_op jit(solution)/shard_map/all_gather | solution.py:323
  25.9 270.0 %all-gather.19.cloned.1.call-start = ((), (), s32[]{:S(2)}) async-start(), calls=%async_computation.11 | async-start | bytes 1566720 | tf_op jit(solution)/shard_map/all_gather | solution.py:323
  51.7 626.1 %reduce-scatter.19.cloned.1.call-start = ((), (), s32[]{:S(2)}) async-start(), calls=%async_computation.12 | async-start | bytes 1566720
  52.2 53.4 %collective-permute-start.1 = (bf16[4,136,1088]{2,1,0:T(8,128)(2,1)}, bf16[4,136,1088]{2,1,0:T(8,128)(2,1)}, u32[]{:S(2)}, u32[]{:S(2)}) collective-permute-start(bf16[4,136,1088]{2,1,0:T(8,128)(2,1)} %all-gather.9.cloned.1.call-done.refs_0_), channel_id=1, source_target_pairs={{0,16},{4,12},{8,24},{12,4},{16,0},{20,28},{24,8},{28,20},{1,17},{... | collective-permute-start | bytes 3551240 | tf_op jit(solution)/shard_map/ppermute | solution.py:266
  53.7 51.9 %collective-permute-start.3 = (bf16[4,136,1088]{2,1,0:T(8,128)(2,1)}, bf16[4,136,1088]{2,1,0:T(8,128)(2,1)}, u32[]{:S(2)}, u32[]{:S(2)}) collective-permute-start(bf16[4,136,1088]{2,1,0:T(8,128)(2,1)} %all-gather.9.cloned.1.call-done.refs_0_), channel_id=1, source_target_pairs={{0,4},{4,0},{8,12},{12,8},{16,20},{20,16},{24,28},{28,24},{1,5},{5... | collective-permute-start | bytes 3551240 | tf_op jit(solution)/shard_map/ppermute | solution.py:266
  123.8 76.9 %collective-permute-start.10 = (bf16[4,136,1088]{2,1,0:T(8,128)(2,1)S(1)}, bf16[4,136,1088]{2,1,0:T(8,128)(2,1)}, u32[]{:S(2)}, u32[]{:S(2)}) collective-permute-start(bf16[4,136,1088]{2,1,0:T(8,128)(2,1)S(1)} %copy-done.4), channel_id=1, source_target_pairs={{0,4},{4,0},{8,12},{12,8},{16,20},{20,16},{24,28},{28,24},{1,5},{5... | collective-permute-start | bytes 3551240 | tf_op jit(solution)/shard_map/ppermute | solution.py:266
  125.1 78.6 %collective-permute-start.14 = (bf16[4,136,1088]{2,1,0:T(8,128)(2,1)}, bf16[4,136,1088]{2,1,0:T(8,128)(2,1)}, u32[]{:S(2)}, u32[]{:S(2)}) collective-permute-start(bf16[4,136,1088]{2,1,0:T(8,128)(2,1)} %all-gather.13.cloned.1.call-done.refs_0_), channel_id=1, source_target_pairs={{0,8},{4,20},{8,0},{12,28},{16,24},{20,4},{24,16},{28,12},{1,9},{5... | collective-permute-start | bytes 3551240 | tf_op jit(solution)/shard_map/ppermute | solution.py:266
  126.6 77.6 %collective-permute-start.11 = (bf16[4,136,1088]{2,1,0:T(8,128)(2,1)}, bf16[4,136,1088]{2,1,0:T(8,128)(2,1)}, u32[]{:S(2)}, u32[]{:S(2)}) collective-permute-start(bf16[4,136,1088]{2,1,0:T(8,128)(2,1)} %collective-permute-done.7.refs_1_), channel_id=1, source_target_pairs={{0,4},{4,0},{8,12},{12,8},{16,20},{20,16},{24,28},{28,24},{1,5},{5... | collective-permute-start | bytes 3551240 | tf_op jit(solution)/shard_map/ppermute | solution.py:266
  146.3 59.0 %collective-permute-start.12 = (bf16[4,136,1088]{2,1,0:T(8,128)(2,1)}, bf16[4,136,1088]{2,1,0:T(8,128)(2,1)}, u32[]{:S(2)}, u32[]{:S(2)}) collective-permute-start(bf16[4,136,1088]{2,1,0:T(8,128)(2,1)} %collective-permute-done.8.refs_2_), channel_id=1, source_target_pairs={{0,4},{4,0},{8,12},{12,8},{16,20},{20,16},{24,28},{28,24},{1,5},{5... | collective-permute-start | bytes 3551240 | tf_op jit(solution)/shard_map/ppermute | solution.py:266
  147.9 58.2 %collective-permute-start.13 = (bf16[4,136,1088]{2,1,0:T(8,128)(2,1)}, bf16[4,136,1088]{2,1,0:T(8,128)(2,1)}, u32[]{:S(2)}, u32[]{:S(2)}) collective-permute-start(bf16[4,136,1088]{2,1,0:T(8,128)(2,1)} %collective-permute-done.9.refs_3_), channel_id=1, source_target_pairs={{0,4},{4,0},{8,12},{12,8},{16,20},{20,16},{24,28},{28,24},{1,5},{5... | collective-permute-start | bytes 3551240 | tf_op jit(solution)/shard_map/ppermute | solution.py:266
  205.3 62.2 %collective-permute-start.22 = (bf16[4,136,1088]{2,1,0:T(8,128)(2,1)}, bf16[4,136,1088]{2,1,0:T(8,128)(2,1)}, u32[]{:S(2)}, u32[]{:S(2)}) collective-permute-start(bf16[4,136,1088]{2,1,0:T(8,128)(2,1)} %all-gather.15.cloned.1.call-done.refs_0_), channel_id=1, source_target_pairs={{0,16},{4,12},{8,24},{12,4},{16,0},{20,28},{24,8},{28,20},{1,17},{... | collective-permute-start | bytes 3551240 | tf_op jit(solution)/shard_map/ppermute | solution.py:266
  206.1 53.8 %collective-permute-start.16 = (bf16[4,136,1088]{2,1,0:T(8,128)(2,1)}, bf16[4,136,1088]{2,1,0:T(8,128)(2,1)}, u32[]{:S(2)}, u32[]{:S(2)}) collective-permute-start(bf16[4,136,1088]{2,1,0:T(8,128)(2,1)} %collective-permute-done.14.refs_1_), channel_id=1, source_target_pairs={{0,16},{4,12},{8,24},{12,4},{16,0},{20,28},{24,8},{28,20},{1,17},{... | collective-permute-start | bytes 3551240 | tf_op jit(solution)/shard_map/ppermute | solution.py:266
  294.8 57.0 %collective-permute-start.29 = (bf16[4,136,1088]{2,1,0:T(8,128)(2,1)S(1)}, bf16[4,136,1088]{2,1,0:T(8,128)(2,1)}, u32[]{:S(2)}, u32[]{:S(2)}) collective-permute-start(bf16[4,136,1088]{2,1,0:T(8,128)(2,1)S(1)} %copy-done.1), channel_id=1, source_target_pairs={{0,16},{4,12},{8,24},{12,4},{16,0},{20,28},{24,8},{28,20},{1,17},{... | collective-permute-start | bytes 3551240 | tf_op jit(solution)/shard_map/ppermute | solution.py:266
  296.0 55.9 %collective-permute-start.31 = (bf16[4,136,1088]{2,1,0:T(8,128)(2,1)S(1)}, bf16[4,136,1088]{2,1,0:T(8,128)(2,1)}, u32[]{:S(2)}, u32[]{:S(2)}) collective-permute-start(bf16[4,136,1088]{2,1,0:T(8,128)(2,1)S(1)} %copy-done.1), channel_id=1, source_target_pairs={{0,4},{4,0},{8,12},{12,8},{16,20},{20,16},{24,28},{28,24},{1,5},{5... | collective-permute-start | bytes 3551240 | tf_op jit(solution)/shard_map/ppermute | solution.py:266
  296.0 56.3 %collective-permute-start.35 = (bf16[4,136,1088]{2,1,0:T(8,128)(2,1)}, bf16[4,136,1088]{2,1,0:T(8,128)(2,1)}, u32[]{:S(2)}, u32[]{:S(2)}) collective-permute-start(bf16[4,136,1088]{2,1,0:T(8,128)(2,1)} %all-gather.19.cloned.1.call-done.refs_0_), channel_id=1, source_target_pairs={{0,8},{4,20},{8,0},{12,28},{16,24},{20,4},{24,16},{28,12},{1,9},{5... | collective-permute-start | bytes 3551240 | tf_op jit(solution)/shard_map/ppermute | solution.py:266
  297.5 58.7 %collective-permute-start.36 = (bf16[4,136,1088]{2,1,0:T(8,128)(2,1)}, bf16[4,136,1088]{2,1,0:T(8,128)(2,1)}, u32[]{:S(2)}, u32[]{:S(2)}) collective-permute-start(bf16[4,136,1088]{2,1,0:T(8,128)(2,1)} %all-gather.19.cloned.1.call-done.refs_0_), channel_id=1, source_target_pairs={{0,16},{4,12},{8,24},{12,4},{16,0},{20,28},{24,8},{28,20},{1,17},{... | collective-permute-start | bytes 3551240 | tf_op jit(solution)/shard_map/ppermute | solution.py:266
  298.4 54.8 %collective-permute-start.30 = (bf16[4,136,1088]{2,1,0:T(8,128)(2,1)}, bf16[4,136,1088]{2,1,0:T(8,128)(2,1)}, u32[]{:S(2)}, u32[]{:S(2)}) collective-permute-start(bf16[4,136,1088]{2,1,0:T(8,128)(2,1)} %collective-permute-done.28.refs_1_), channel_id=1, source_target_pairs={{0,16},{4,12},{8,24},{12,4},{16,0},{20,28},{24,8},{28,20},{1,17},{... | collective-permute-start | bytes 3551240 | tf_op jit(solution)/shard_map/ppermute | solution.py:266
  357.0 57.2 %collective-permute-start.38 = (bf16[4,136,1088]{2,1,0:T(8,128)(2,1)S(1)}, bf16[4,136,1088]{2,1,0:T(8,128)(2,1)S(1)}, u32[]{:S(2)}, u32[]{:S(2)}) collective-permute-start(bf16[4,136,1088]{2,1,0:T(8,128)(2,1)S(1)} %copy-done), channel_id=1, source_target_pairs={{0,4},{4,0},{8,12},{12,8},{16,20},{20,16},{24,28},{28,24},{1,5},{5... | collective-permute-start | bytes 3551240 | tf_op jit(solution)/shard_map/ppermute | solution.py:266
  357.5 56.7 %collective-permute-start.39 = (bf16[4,136,1088]{2,1,0:T(8,128)(2,1)}, bf16[4,136,1088]{2,1,0:T(8,128)(2,1)S(1)}, u32[]{:S(2)}, u32[]{:S(2)}) collective-permute-start(bf16[4,136,1088]{2,1,0:T(8,128)(2,1)} %collective-permute-done.35.refs_1_), channel_id=1, source_target_pairs={{0,4},{4,0},{8,12},{12,8},{16,20},{20,16},{24,28},{28,24},{1,5},{5... | collective-permute-start | bytes 3551240 | tf_op jit(solution)/shard_map/ppermute | solution.py:266
  357.5 57.2 %collective-permute-start.40 = (bf16[4,136,1088]{2,1,0:T(8,128)(2,1)}, bf16[4,136,1088]{2,1,0:T(8,128)(2,1)S(1)}, u32[]{:S(2)}, u32[]{:S(2)}) collective-permute-start(bf16[4,136,1088]{2,1,0:T(8,128)(2,1)} %collective-permute-done.36.refs_2_), channel_id=1, source_target_pairs={{0,4},{4,0},{8,12},{12,8},{16,20},{20,16},{24,28},{28,24},{1,5},{5... | collective-permute-start | bytes 3551240 | tf_op jit(solution)/shard_map/ppermute | solution.py:266
  369.5 45.3 %collective-permute-start.41 = (bf16[4,136,1088]{2,1,0:T(8,128)(2,1)S(1)}, bf16[4,136,1088]{2,1,0:T(8,128)(2,1)S(1)}, u32[]{:S(2)}, u32[]{:S(2)}) collective-permute-start(bf16[4,136,1088]{2,1,0:T(8,128)(2,1)S(1)} %collective-permute-done.37.refs_3_), channel_id=1, source_target_pairs={{0,4},{4,0},{8,12},{12,8},{16,20},{20,16},{24,28},{28,24},{1,5},{5... | collective-permute-start | bytes 3551240 | tf_op jit(solution)/shard_map/ppermute | solution.py:266
  407.8 48.0 %collective-permute-start.42 = (bf16[544,1088]{1,0:T(8,128)(2,1)}, bf16[544,1088]{1,0:T(8,128)(2,1)}, u32[]{:S(2)}, u32[]{:S(2)}) collective-permute-start(bf16[544,1088]{1,0:T(8,128)(2,1)} %convolution_convert_fusion.23), channel_id=1, source_target_pairs={{0,4},{4,0},{8,12},{12,8},{16,20},{20,16},{24,28},{28,24},{1,5},{5... | collective-permute-start | bytes 3551240 | tf_op jit(solution)/shard_map/ppermute | solution.py:266
  414.2 49.7 %collective-permute-start.43 = (bf16[544,1088]{1,0:T(8,128)(2,1)}, bf16[544,1088]{1,0:T(8,128)(2,1)}, u32[]{:S(2)}, u32[]{:S(2)}) collective-permute-start(bf16[544,1088]{1,0:T(8,128)(2,1)} %convolution_convert_fusion.22), channel_id=1, source_target_pairs={{0,4},{4,0},{8,12},{12,8},{16,20},{20,16},{24,28},{28,24},{1,5},{5... | collective-permute-start | bytes 3551240 | tf_op jit(solution)/shard_map/ppermute | solution.py:266
  414.2 53.5 %collective-permute-start.44 = (bf16[544,1088]{1,0:T(8,128)(2,1)}, bf16[544,1088]{1,0:T(8,128)(2,1)}, u32[]{:S(2)}, u32[]{:S(2)}) collective-permute-start(bf16[544,1088]{1,0:T(8,128)(2,1)} %convolution_convert_fusion.21), channel_id=1, source_target_pairs={{0,4},{4,0},{8,12},{12,8},{16,20},{20,16},{24,28},{28,24},{1,5},{5... | collective-permute-start | bytes 3551240 | tf_op jit(solution)/shard_map/ppermute | solution.py:266
  414.7 45.5 %collective-permute-start.45 = (bf16[544,1088]{1,0:T(8,128)(2,1)}, bf16[544,1088]{1,0:T(8,128)(2,1)}, u32[]{:S(2)}, u32[]{:S(2)}) collective-permute-start(bf16[544,1088]{1,0:T(8,128)(2,1)} %convolution_convert_fusion.20), channel_id=1, source_target_pairs={{0,4},{4,0},{8,12},{12,8},{16,20},{20,16},{24,28},{28,24},{1,5},{5... | collective-permute-start | bytes 3551240 | tf_op jit(solution)/shard_map/ppermute | solution.py:266
  450.6 43.1 %collective-permute-start.48 = (bf16[544,1088]{1,0:T(8,128)(2,1)}, bf16[544,1088]{1,0:T(8,128)(2,1)}, u32[]{:S(2)}, u32[]{:S(2)}) collective-permute-start(bf16[544,1088]{1,0:T(8,128)(2,1)} %convolution_convert_fusion.19), channel_id=1, source_target_pairs={{0,4},{4,0},{8,12},{12,8},{16,20},{20,16},{24,28},{28,24},{1,5},{5... | collective-permute-start | bytes 3551240 | tf_op jit(solution)/shard_map/ppermute | solution.py:266
  455.9 44.4 %collective-permute-start.49 = (bf16[544,1088]{1,0:T(8,128)(2,1)}, bf16[544,1088]{1,0:T(8,128)(2,1)}, u32[]{:S(2)}, u32[]{:S(2)}) collective-permute-start(bf16[544,1088]{1,0:T(8,128)(2,1)} %convolution_convert_fusion.18), channel_id=1, source_target_pairs={{0,4},{4,0},{8,12},{12,8},{16,20},{20,16},{24,28},{28,24},{1,5},{5... | collective-permute-start | bytes 3551240 | tf_op jit(solution)/shard_map/ppermute | solution.py:266
  485.3 49.6 %collective-permute-start.46 = (bf16[544,1088]{1,0:T(8,128)(2,1)}, bf16[544,1088]{1,0:T(8,128)(2,1)S(1)}, u32[]{:S(2)}, u32[]{:S(2)}) collective-permute-start(bf16[544,1088]{1,0:T(8,128)(2,1)} %add_convert_fusion.39), channel_id=1, source_target_pairs={{0,16},{4,12},{8,24},{12,4},{16,0},{20,28},{24,8},{28,20},{1,17},{... | collective-permute-start | bytes 3551240 | tf_op jit(solution)/shard_map/ppermute | solution.py:266
  489.2 44.8 %collective-permute-start.54 = (bf16[544,1088]{1,0:T(8,128)(2,1)S(1)}, bf16[544,1088]{1,0:T(8,128)(2,1)S(1)}, u32[]{:S(2)}, u32[]{:S(2)}) collective-permute-start(bf16[544,1088]{1,0:T(8,128)(2,1)S(1)} %add_convert_fusion.32), channel_id=1, source_target_pairs={{0,16},{4,12},{8,24},{12,4},{16,0},{20,28},{24,8},{28,20},{1,17},{... | collective-permute-start | bytes 3551240 | tf_op jit(solution)/shard_map/ppermute | solution.py:266
  493.7 94.2 %collective-permute-start.53 = (bf16[544,1088]{1,0:T(8,128)(2,1)}, bf16[544,1088]{1,0:T(8,128)(2,1)}, u32[]{:S(2)}, u32[]{:S(2)}) collective-permute-start(bf16[544,1088]{1,0:T(8,128)(2,1)} %add_convert_fusion.33), channel_id=1, source_target_pairs={{0,16},{4,12},{8,24},{12,4},{16,0},{20,28},{24,8},{28,20},{1,17},{... | collective-permute-start | bytes 3551240 | tf_op jit(solution)/shard_map/ppermute | solution.py:266
  534.3 53.6 %collective-permute-start.55 = (bf16[544,1088]{1,0:T(8,128)(2,1)S(1)}, bf16[544,1088]{1,0:T(8,128)(2,1)S(1)}, u32[]{:S(2)}, u32[]{:S(2)}) collective-permute-start(bf16[544,1088]{1,0:T(8,128)(2,1)S(1)} %add_convert_fusion.29), channel_id=1, source_target_pairs={{0,8},{4,20},{8,0},{12,28},{16,24},{20,4},{24,16},{28,12},{1,9},{5... | collective-permute-start | bytes 3551240 | tf_op jit(solution)/shard_map/ppermute | solution.py:266
  599.7 102.2 %reduce-scatter.21.cloned.1.call-start = ((), (), s32[]{:S(2)}) async-start(), calls=%async_computation.13 | async-start | bytes 1566720
  647.4 247.2 %reduce-scatter.23.cloned.1.call-start = ((), (), s32[]{:S(2)}) async-start(), calls=%async_computation.14 | async-start | bytes 1566720
  660.7 46.6 %collective-permute-start.62 = (bf16[544,1088]{1,0:T(8,128)(2,1)}, bf16[544,1088]{1,0:T(8,128)(2,1)}, u32[]{:S(2)}, u32[]{:S(2)}) collective-permute-start(bf16[544,1088]{1,0:T(8,128)(2,1)} %add_convert_fusion.24), channel_id=1, source_target_pairs={{0,16},{4,12},{8,24},{12,4},{16,0},{20,28},{24,8},{28,20},{1,17},{... | collective-permute-start | bytes 3551240 | tf_op jit(solution)/shard_map/ppermute | solution.py:266
  665.2 46.4 %collective-permute-start.71 = (bf16[544,1088]{1,0:T(8,128)(2,1)}, bf16[544,1088]{1,0:T(8,128)(2,1)}, u32[]{:S(2)}, u32[]{:S(2)}) collective-permute-start(bf16[544,1088]{1,0:T(8,128)(2,1)} %add_convert_fusion.18), channel_id=1, source_target_pairs={{0,16},{4,12},{8,24},{12,4},{16,0},{20,28},{24,8},{28,20},{1,17},{... | collective-permute-start | bytes 3551240 | tf_op jit(solution)/shard_map/ppermute | solution.py:266
  728.2 49.8 %collective-permute-start.70 = (bf16[544,1088]{1,0:T(8,128)(2,1)S(1)}, bf16[544,1088]{1,0:T(8,128)(2,1)S(1)}, u32[]{:S(2)}, u32[]{:S(2)}) collective-permute-start(bf16[544,1088]{1,0:T(8,128)(2,1)S(1)} %copy-done.191), channel_id=1, source_target_pairs={{0,16},{4,12},{8,24},{12,4},{16,0},{20,28},{24,8},{28,20},{1,17},{... | collective-permute-start | bytes 3551240 | tf_op jit(solution)/shard_map/ppermute | solution.py:266
  731.2 49.3 %collective-permute-start.77 = (bf16[544,1088]{1,0:T(8,128)(2,1)S(1)}, bf16[544,1088]{1,0:T(8,128)(2,1)S(1)}, u32[]{:S(2)}, u32[]{:S(2)}) collective-permute-start(bf16[544,1088]{1,0:T(8,128)(2,1)S(1)} %add_convert_fusion.15), channel_id=1, source_target_pairs={{0,8},{4,20},{8,0},{12,28},{16,24},{20,4},{24,16},{28,12},{1,9},{5... | collective-permute-start | bytes 3551240 | tf_op jit(solution)/shard_map/ppermute | solution.py:266
  734.7 92.6 %collective-permute-start.76 = (bf16[2,136,1088]{2,1,0:T(8,128)(2,1)}, bf16[2,136,1088]{2,1,0:T(8,128)(2,1)}, u32[]{:S(2)}, u32[]{:S(2)}) collective-permute-start(bf16[2,136,1088]{2,1,0:T(8,128)(2,1)} %pad_maximum_fusion.17), channel_id=1, source_target_pairs={{0,16},{4,12},{8,24},{12,4},{16,0},{20,28},{24,8},{28,20},{1,17},{... | collective-permute-start | bytes 1775624 | tf_op jit(solution)/shard_map/ppermute | solution.py:266
  804.8 142.3 %reduce-scatter.29.cloned.1.call-start = ((), (), s32[]{:S(2)}) async-start(), calls=%async_computation.17 | async-start | bytes 1566720
  830.7 60.3 %collective-permute-start.78 = (bf16[544,1088]{1,0:T(8,128)(2,1)}, bf16[544,1088]{1,0:T(8,128)(2,1)}, u32[]{:S(2)}, u32[]{:S(2)}) collective-permute-start(bf16[544,1088]{1,0:T(8,128)(2,1)} %add_convert_fusion.12), channel_id=1, source_target_pairs={{0,16},{4,12},{8,24},{12,4},{16,0},{20,28},{24,8},{28,20},{1,17},{... | collective-permute-start | bytes 3551240 | tf_op jit(solution)/shard_map/ppermute | solution.py:266
  839.1 113.0 %reduce-scatter.27.cloned.1.call-start = ((), (), s32[]{:S(2)}) async-start(), calls=%async_computation.16 | async-start | bytes 1566720
  845.9 41.5 %collective-permute-start.93 = (bf16[544,1088]{1,0:T(8,128)(2,1)S(1)}, bf16[544,1088]{1,0:T(8,128)(2,1)S(1)}, u32[]{:S(2)}, u32[]{:S(2)}) collective-permute-start(bf16[544,1088]{1,0:T(8,128)(2,1)S(1)} %add_convert_fusion.7), channel_id=1, source_target_pairs={{0,16},{4,12},{8,24},{12,4},{16,0},{20,28},{24,8},{28,20},{1,17},{... | collective-permute-start | bytes 3551240 | tf_op jit(solution)/shard_map/ppermute | solution.py:266
  851.9 66.0 %collective-permute-start.109 = (bf16[4,136,1088]{2,1,0:T(8,128)(2,1)}, bf16[4,136,1088]{2,1,0:T(8,128)(2,1)}, u32[]{:S(2)}, u32[]{:S(2)}) collective-permute-start(bf16[4,136,1088]{2,1,0:T(8,128)(2,1)} %pad_maximum_fusion.11), channel_id=1, source_target_pairs={{0,4},{4,0},{8,12},{12,8},{16,20},{20,16},{24,28},{28,24},{1,5},{5... | collective-permute-start | bytes 3551240 | tf_op jit(solution)/shard_map/ppermute | solution.py:266
  855.3 68.9 %collective-permute-start.98 = (bf16[544,1088]{1,0:T(8,128)(2,1)}, bf16[544,1088]{1,0:T(8,128)(2,1)}, u32[]{:S(2)}, u32[]{:S(2)}) collective-permute-start(bf16[544,1088]{1,0:T(8,128)(2,1)} %convolution_convert_fusion.3), channel_id=1, source_target_pairs={{0,4},{4,0},{8,12},{12,8},{16,20},{20,16},{24,28},{28,24},{1,5},{5... | collective-permute-start | bytes 3551240 | tf_op jit(solution)/shard_map/ppermute | solution.py:266
  894.6 65.8 %reduce-scatter.25.cloned.1.call-start = ((), (), s32[]{:S(2)}) async-start(), calls=%async_computation.15 | async-start | bytes 1566720
  (287 other events, 3968.7 us)
Sparse Core Ops, SparseCore 0:
  14.0 34.3 all-gather.8
  50.6 30.7 all-gather.10
  83.5 30.9 all-gather.12
  116.0 30.6 all-gather.14
  148.1 30.7 all-gather.16
  180.3 30.7 all-gather.18
  599.8 30.0 reduce-scatter.18
  647.5 30.4 reduce-scatter.20
  804.9 29.9 reduce-scatter.22
  839.3 29.9 reduce-scatter.28
  894.7 32.1 reduce-scatter.26
  929.7 29.1 reduce-scatter.24

commit v3 on v2

--- a/solution.py
+++ b/solution.py
@@ -26,81 +26,151 @@
     return jax.nn.gelu(values, approximate=True)
 
 
-def causal_mask(lengths, count):
+def sequence_starts(lengths, count):
     seq_ends = jnp.cumsum(lengths[0])
     positions = jnp.arange(count, dtype=jnp.int32)
-    segment = jnp.sum((positions[:, None] >= seq_ends[None, :]).astype(jnp.int32), axis=1)
-    return (segment[:, None] == segment[None, :]) & (positions[:, None] >= positions[None, :])
-
-
-def split_heads(rows):
-    return rows.reshape(rows.shape[0], HEADS, HEAD)
-
-
-def three_parts(projected):
-    width = projected.shape[1] // 3
-    return (
-        split_heads(projected[:, :width]),
-        split_heads(projected[:, width : 2 * width]),
-        split_heads(projected[:, 2 * width :]),
-    )
-
-
-def scores_of(queries, key_rows, allowed):
-    scores = (
-        jnp.einsum("qhd,khd->hqk", queries, key_rows, preferred_element_type=jnp.float32)
-        * score_scale
-    )
-    return jnp.where(allowed[None], scores, masked_fill)
-
-
-def attend(projected, allowed):
-    queries, key_rows, value_rows = three_parts(projected)
-    scores = scores_of(queries, key_rows, allowed)
-    row_max = jnp.max(scores, axis=-1, keepdims=True)
-    exponent = jnp.where(allowed[None], jnp.exp(scores - row_max), 0.0)
-    totals = jnp.sum(exponent, axis=-1, keepdims=True)
-    attn_probs = (exponent / totals).astype(jnp.bfloat16)
-    mixed = jnp.einsum("hqk,khd->qhd", attn_probs, value_rows, preferred_element_type=jnp.float32)
-    mixed = mixed.reshape(projected.shape[0], projected.shape[1] // 3)
-    return (mixed.astype(jnp.bfloat16), row_max + jnp.log(totals))
-
-
-def attend_back(projected, log_total, grad_mixed, allowed):
-    count = projected.shape[0]
-    width = projected.shape[1] // 3
-    queries, key_rows, value_rows = three_parts(projected)
-    grad_heads = split_heads(grad_mixed)
-    scores = scores_of(queries, key_rows, allowed)
-    attn_probs = jnp.where(allowed[None], jnp.exp(scores - log_total), 0.0)
-    grad_values = jnp.einsum(
-        "hqk,qhd->khd",
-        attn_probs.astype(jnp.bfloat16),
-        grad_heads,
-        preferred_element_type=jnp.float32,
-    )
-    grad_probs = jnp.einsum(
-        "qhd,khd->hqk", grad_heads, value_rows, preferred_element_type=jnp.float32
-    )
-    row_dot = jnp.sum(attn_probs * grad_probs, axis=-1, keepdims=True)
-    grad_scores = (attn_probs * (grad_probs - row_dot)).astype(jnp.bfloat16)
-    grad_queries = (
-        jnp.einsum("hqk,khd->qhd", grad_scores, key_rows, preferred_element_type=jnp.float32)
-        * score_scale
-    )
-    grad_keys = (
-        jnp.einsum("hqk,qhd->khd", grad_scores, queries, preferred_element_type=jnp.float32)
-        * score_scale
-    )
-    joined = jnp.concatenate(
-        [
-            grad_queries.reshape(count, width),
-            grad_keys.reshape(count, width),
-            grad_values.reshape(count, width),
-        ],
-        axis=1,
-    )
-    return joined.astype(jnp.bfloat16)
+    passed = positions[:, None] >= seq_ends[None, :]
+    return jnp.max(jnp.where(passed, seq_ends[None, :], 0), axis=1, keepdims=True)
+
+
+def rows_at_once(count):
+    return 256 if count % 256 == 0 else count
+
+
+def mask_add(starts_ref, first, rows, keys):
+    at = lax.broadcasted_iota(jnp.int32, (rows, keys), 0) + first
+    key = lax.broadcasted_iota(jnp.int32, (rows, keys), 1)
+    allowed = (key <= at) & (key >= starts_ref[first : first + rows, :])
+    return jnp.where(allowed, 0.0, masked_fill)
+
+
+def across(left, right):
+    return lax.dot_general(
+        left, right, (((1,), (1,)), ((), ())), preferred_element_type=jnp.float32
+    )
+
+
+def down(left, right):
+    return lax.dot_general(
+        left, right, (((0,), (0,)), ((), ())), preferred_element_type=jnp.float32
+    )
+
+
+def over_heads(step):
+    def pair(i, _):
+        step(pl.multiple_of(i * 2 * HEAD, 2 * HEAD), 2, i)
+        return 0
+
+    lax.fori_loop(0, HEADS // 2, pair, 0)
+    if HEADS % 2:
+        step((HEADS - 1) * HEAD, 1, HEADS // 2)
+
+
+def side_by_side(parts):
+    return parts[0] if len(parts) == 1 else jnp.concatenate(parts, axis=1)
+
+
+def attend_kernel(starts_ref, q_ref, k_ref, v_ref, mixed_ref, log_ref):
+    count = q_ref.shape[0]
+    rows = rows_at_once(count)
+    for first in range(0, count, rows):
+        keys = first + rows
+        mask = mask_add(starts_ref, first, rows, keys)
+
+        def step(at, heads, pair, first=first, keys=keys, mask=mask):
+            cols = pl.ds(at, heads * HEAD)
+            queries = q_ref[first:keys, cols]
+            key_rows = k_ref[0:keys, cols]
+            value_rows = v_ref[0:keys, cols]
+            mixed = []
+            for h in range(heads):
+                own = slice(h * HEAD, (h + 1) * HEAD)
+                scores = across(queries[:, own], key_rows[:, own]) * score_scale + mask
+                row_max = jnp.max(scores, axis=1, keepdims=True)
+                exponent = jnp.exp(scores - row_max)
+                totals = jnp.sum(exponent, axis=1, keepdims=True)
+                probs = (exponent * (1.0 / totals)).astype(jnp.bfloat16)
+                mixed.append(
+                    jnp.dot(probs, value_rows[:, own], preferred_element_type=jnp.float32)
+                )
+                log_ref[pair * 2 + h, first:keys, :] = row_max + jnp.log(totals)
+            mixed_ref[first:keys, cols] = side_by_side(mixed).astype(jnp.bfloat16)
+
+        over_heads(step)
+
+
+def attend(queries, key_rows, value_rows, starts):
+    count, width = queries.shape
+    return pl.pallas_call(
+        attend_kernel,
+        out_shape=(
+            jax.ShapeDtypeStruct((count, width), jnp.bfloat16),
+            jax.ShapeDtypeStruct((HEADS, count, 1), jnp.float32),
+        ),
+        compiler_params=pltpu.CompilerParams(vmem_limit_bytes=48 << 20),
+        cost_estimate=pl.CostEstimate(
+            flops=4 * count * count * width,
+            bytes_accessed=8 * count * width,
+            transcendentals=HEADS * count * count,
+        ),
+    )(starts, queries, key_rows, value_rows)
+
+
+def attend_back_kernel(
+    starts_ref, q_ref, k_ref, v_ref, log_ref, g_ref, gq_ref, gk_ref, gv_ref, key_sum, value_sum
+):
+    count = q_ref.shape[0]
+    rows = rows_at_once(count)
+    masks = [mask_add(starts_ref, first, rows, first + rows) for first in range(0, count, rows)]
+
+    def step(at, heads, pair):
+        cols = pl.ds(at, heads * HEAD)
+        key_sum[...] = jnp.zeros_like(key_sum)
+        value_sum[...] = jnp.zeros_like(value_sum)
+        for first, mask in zip(range(0, count, rows), masks):
+            keys = first + rows
+            queries, grads = q_ref[first:keys, cols], g_ref[first:keys, cols]
+            key_rows, value_rows = k_ref[0:keys, cols], v_ref[0:keys, cols]
+            query_parts, key_parts, value_parts = [], [], []
+            for h in range(heads):
+                own = slice(h * HEAD, (h + 1) * HEAD)
+                scores = across(queries[:, own], key_rows[:, own]) * score_scale + mask
+                probs = jnp.exp(scores - log_ref[pair * 2 + h, first:keys, :])
+                value_parts.append(down(probs.astype(jnp.bfloat16), grads[:, own]))
+                grad_probs = across(grads[:, own], value_rows[:, own])
+                row_dot = jnp.sum(probs * grad_probs, axis=1, keepdims=True)
+                grad_scores = (probs * (grad_probs - row_dot)).astype(jnp.bfloat16)
+                query_parts.append(
+                    jnp.dot(grad_scores, key_rows[:, own], preferred_element_type=jnp.float32)
+                )
+                key_parts.append(down(grad_scores, queries[:, own]))
+            width = heads * HEAD
+            gq_ref[first:keys, cols] = (side_by_side(query_parts) * score_scale).astype(
+                jnp.bfloat16
+            )
+            key_sum[0:keys, 0:width] += side_by_side(key_parts)
+            value_sum[0:keys, 0:width] += side_by_side(value_parts)
+        width = heads * HEAD
+        gk_ref[:, cols] = (key_sum[:, 0:width] * score_scale).astype(jnp.bfloat16)
+        gv_ref[:, cols] = value_sum[:, 0:width].astype(jnp.bfloat16)
+
+    over_heads(step)
+
+
+def attend_back(queries, key_rows, value_rows, log_total, grad_mixed, starts):
+    count, width = queries.shape
+    shape = jax.ShapeDtypeStruct((count, width), jnp.bfloat16)
+    return pl.pallas_call(
+        attend_back_kernel,
+        out_shape=(shape, shape, shape),
+        scratch_shapes=[pltpu.VMEM((count, 2 * HEAD), jnp.float32)] * 2,
+        compiler_params=pltpu.CompilerParams(vmem_limit_bytes=48 << 20),
+        cost_estimate=pl.CostEstimate(
+            flops=10 * count * count * width,
+            bytes_accessed=14 * count * width,
+            transcendentals=HEADS * count * count,
+        ),
+    )(starts, queries, key_rows, value_rows, log_total, grad_mixed)
 
 
 def dot_columns(rows, chunks):
@@ -122,7 +192,7 @@
     )
 
 
-def forward_layer(stream, weights, allowed):
+def forward_layer(stream, weights, starts, layout):
     small, qkv_weight, out_weight, up_weight, down_weight = weights
     (
         norm1_gain,
@@ -138,13 +208,13 @@
     normed = layer_norm(
         stream, norm1_gain.astype(jnp.float32), norm1_shift.astype(jnp.float32)
     ).astype(jnp.bfloat16)
-    qkv_bias = jnp.concatenate([query_bias, jnp.zeros_like(query_bias), value_bias]).astype(
-        jnp.float32
-    )
-    projected = (dot_columns(normed, qkv_weight) + qkv_bias).astype(
-        jnp.bfloat16
-    )
-    mixed, log_total = attend(projected, allowed)
+    joined = dot_columns(normed, qkv_weight)
+    width = stream.shape[1]
+    queries = (joined[:, :width] + query_bias.astype(jnp.float32)).astype(jnp.bfloat16)
+    key_rows = joined[:, width : 2 * width].astype(jnp.bfloat16)
+    value_rows = (joined[:, 2 * width :] + value_bias.astype(jnp.float32)).astype(jnp.bfloat16)
+    projected = (queries, key_rows, value_rows)
+    mixed, log_total = attend(queries, key_rows, value_rows, starts)
     after_attn = (
         stream
         + dot_columns(mixed, out_weight)
@@ -176,7 +246,7 @@
     )
 
 
-def backward_layer(grad_out, weights, saved, allowed, layout, pipe, sum_group):
+def backward_layer(grad_out, weights, saved, starts, layout, pipe, sum_group):
     small, qkv_weight, out_weight, up_weight, down_weight = weights
     (
         norm1_gain,
@@ -192,7 +262,6 @@
     stream, normed, projected, mixed, log_total, after_attn, normed_two, hidden_pre, activated = (
         saved
     )
-    width = stream.shape[1]
     grad_branch = grad_out.astype(jnp.bfloat16)
     sum_group("down", down_product(layout, activated, grad_branch))
     grad_branch = pipe.advance(grad_branch)
@@ -213,12 +282,21 @@
     grad_out_bias = jnp.sum(grad_attn.astype(jnp.float32), axis=0)
     grad_mixed = dot_columns_back(grad_attn, out_weight).astype(jnp.bfloat16)
     grad_mixed = pipe.advance(grad_mixed)
-    grad_projected = attend_back(projected, log_total, grad_mixed, allowed)
-    sum_group("first", first_product(layout, normed, grad_projected, mixed, grad_attn))
-    grad_projected = pipe.advance(grad_projected)
-    grad_query_bias = jnp.sum(grad_projected[:, :width].astype(jnp.float32), axis=0)
-    grad_value_bias = jnp.sum(grad_projected[:, 2 * width :].astype(jnp.float32), axis=0)
-    grad_normed = dot_columns_back(grad_projected, qkv_weight)
+    thirds = attend_back(*projected, log_total, grad_mixed, starts)
+    sum_group("first", first_product(layout, normed, thirds, mixed, grad_attn))
+    thirds = pipe.advance(thirds)
+    grad_query_bias = jnp.sum(thirds[0].astype(jnp.float32), axis=0)
+    grad_value_bias = jnp.sum(thirds[2].astype(jnp.float32), axis=0)
+    if len(qkv_weight) == 3:
+        pieces = list(thirds)
+    else:
+        cols = qkv_weight[0].shape[1]
+        whole = jnp.concatenate(thirds, axis=1)
+        pieces = [whole[:, i * cols : (i + 1) * cols] for i in range(len(qkv_weight))]
+    grad_normed = sum(
+        jnp.einsum("te,de->td", piece, chunk, preferred_element_type=jnp.float32)
+        for piece, chunk in zip(pieces, qkv_weight)
+    )
     first_value, first_pull = jax.vjp(
         layer_norm, stream, norm1_gain.astype(jnp.float32), norm1_shift.astype(jnp.float32)
     )
@@ -319,16 +397,21 @@
     )(index.astype(jnp.int32), *blocks)
 
 
-def gather_group(layout, piece, by_shard):
+def gather_group(layout, piece, by_shard, before):
     block = lax.all_gather(piece, "shard", axis=0, tiled=False)
-    held = {(0, 0): block}
-    held[1, 0] = layout.move(block, "first")
+    if before is not None:
+        block = lax.optimization_barrier((block, before[0]))[0]
+    moved = layout.move(block, "first")
+    starts = (block, moved)
+    if before is not None:
+        starts = lax.optimization_barrier((starts, before[1]))[0]
+    held = {(0, 0): starts[0], (1, 0): starts[1]}
     for k in range(1, layout.across):
         for f in range(2):
             held[f, k] = layout.move(held[f, k - 1], "second")
     own = [held[slot] for slot in layout.slots()]
     other = [layout.move(block, "core") for block in own]
-    return assemble(layout, own + other, by_shard)
+    return assemble(layout, own + other, by_shard), (moved, own[2:])
 
 
 def add_low(left, right):
@@ -428,10 +511,13 @@
     return product
 
 
-def first_product(layout, normed, grad_projected, mixed, grad_attn):
+def first_product(layout, normed, thirds, mixed, grad_attn):
     one_rows = by_core_rows(layout, normed, 1)[0]
     mixed_rows = by_core_rows(layout, mixed, 1)[0]
-    chunks = column_chunks(layout, jnp.concatenate([grad_projected, grad_attn], axis=1))
+    if layout.chips == 4:
+        chunks = jnp.stack(list(thirds) + [grad_attn])
+    else:
+        chunks = column_chunks(layout, jnp.concatenate(list(thirds) + [grad_attn], axis=1))
 
     def product(chip, core):
         rows = jnp.where(
@@ -537,7 +623,7 @@
         down_bias,
         cotangent,
     ):
-        allowed = causal_mask(lengths, tokens_in.shape[0])
+        starts = sequence_starts(lengths, tokens_in.shape[0])
         layer_count = ln1_gain.shape[0]
         chips, shards = layout.chips, layout.shards
         a, b, core, shard = layout.place()
@@ -575,11 +661,13 @@
             rows = weight.shape[0] // (2 * chips)
             return lax.dynamic_slice_in_dim(weight, (chip * 2 + core) * rows, rows, axis=0)
 
-        weights = []
+        weights, before = [], None
         for l in range(layer_count):
-            first = gather_group(layout, own_first(qkv_weight[l], out_weight[l]), False)
-            up = gather_group(layout, own_columns(up_weight[l]), False)
-            down = gather_group(layout, own_rows(down_weight[l]), True)
+            first, before = gather_group(
+                layout, own_first(qkv_weight[l], out_weight[l]), False, before
+            )
+            up, before = gather_group(layout, own_columns(up_weight[l]), False, before)
+            down, before = gather_group(layout, own_rows(down_weight[l]), True, before)
             first = first.reshape(chips, -1, first.shape[-1])
             up = up.reshape(chips, -1, up.shape[-1])
             down = down.reshape(-1, down.shape[-1])
@@ -602,7 +690,7 @@
         stream = tokens_in.astype(jnp.float32)
         saved_all = []
         for l in range(layer_count):
-            stream, saved = forward_layer(stream, weights[l], allowed)
+            stream, saved = forward_layer(stream, weights[l], starts, layout)
             saved_all.append(saved)
         block_out = stream.astype(jnp.bfloat16)
         grad_stream = cotangent.astype(jnp.float32)
@@ -626,7 +714,7 @@
                 grad_stream,
                 weights[l],
                 saved_all[l],
-                allowed,
+                starts,
                 layout,
                 pipe,
                 lambda name, product, l=l: sum_group(name, l, product),

time: 1010 us -> 952 us (0.943)
  Pallas kernels: 68 us -> 161 us
  waiting for transfers between devices: 266 us -> 178 us
  matrix products: 341 us -> 266 us
  local copies, waits for them, and re-layouts: 77.7 us -> 109 us
  other arithmetic: 149 us -> 122 us
    pallas_call x0 -> x4, Pallas kernels: none -> 91.5 us  [the longest x2 51.2 us: attend_back(): pl.pallas_call(attend_back_kernel, out_shape=(shape, shape, shape), scrat...]
    dot_general x12 -> x6, matrix products: 87.4 us -> 15.6 us  [backward_layer(): jnp.einsum('te,de->td', piece, chunk, preferred_element_type=jnp.float32)]
    ppermute x102, waiting for transfers between devices: 196 us -> 129 us  [move(): return lax.ppermute(value, 'replica', self.pairs(way))]
    convert_element_type x6 -> x0, other arithmetic: 32.9 us -> none  [the longest x2 27 us: attend_back(): grad_scores = (attn_probs * (grad_probs - row_dot)).astype(jnp.bfloat16)]
    all_gather x6, waiting for transfers between devices: 50.1 us -> 21.7 us  [gather_group(): block = lax.all_gather(piece, 'shard', axis=0, tiled=False)]
    reduce_sum x5 -> x2, other arithmetic: 24.8 us -> 0.78 us  [backward_layer(): grad_value_bias = jnp.sum(thirds[2].astype(jnp.float32), axis=0)]
    ppermute x6, waiting for transfers between devices: 5.19 us -> 18.3 us  [sum_vectors(): total = total + lax.ppermute(total, 'replica', pairs)]
    transpose x0 -> x6, local copies, waits for them, and re-layouts: none -> 13.1 us  [by_core_rows(): rows.T.reshape(n, chips, 2, rows.shape[1] // (2 * n * chips), rows.shape[0])]
  transfers between devices with their start and end apart: 126 -> 126, of which waited for: 28 -> 23; matrix products, arithmetic and copies ran while one was open for 52% -> 49% of each run, Pallas kernels for 6% -> 17%
where the time goes in v3:
time: 952 us; the launch traced here: 946 us
  matrix products  266 us (28%)
  waiting for transfers between devices  178 us (19%)
  Pallas kernels  161 us (17%)
  other arithmetic  122 us (13%)
  local copies, waits for them, and re-layouts  109 us (11%)
  starting transfers between devices  78.2 us (8%)
  between operations  17.7 us (2%)
  blocking collectives  13.8 us (1%)
    ppermute x102, waiting for transfers between devices, move(): return lax.ppermute(value, 'replica', self.pairs(way))  129 us
    ppermute x102, starting transfers between devices, move(): return lax.ppermute(value, 'replica', self.pairs(way))  66.7 us
    pallas_call x2, Pallas kernels, attend_back(): pl.pallas_call(attend_back_kernel, out_shape=(shape, shape, shape), scrat...  51.2 us
    pallas_call x6, Pallas kernels, assemble(): pl.pallas_call(functools.partial(place_kernel, by_shard), out_shape=jax.S...  50.2 us
    dot_general x16, matrix products, product(): return jnp.dot(rows, pick(chunks, chip), preferred_element_type=jnp.float32)  45.6 us
    dot_general x16, matrix products, product(): jnp.dot(pick(rows, core), pick(chunks, chip), preferred_element_type=jnp....  44.6 us
    dot_general x16, matrix products, product(): jnp.dot(pick(pick(rows, chip), core), grad_branch, preferred_element_type...  42 us
    pallas_call x2, Pallas kernels, attend(): pl.pallas_call(attend_kernel, out_shape=(jax.ShapeDtypeStruct((count, wid...  40.2 us
  transfers between devices with their start and end apart: 126, of which 23 were waited for; matrix products, arithmetic and copies ran while one was open for 49% of the time, Pallas kernels for 17%

profile of v3, /device:TPU:0, one launch (start us, length us, event | category | flops | bytes accessed | tf_op | source)
XLA Modules:
  0.0 946.4 jit_solution(8484790323120827788)
XLA Ops:
  13.1 4.1 fusion.427
  26.0 21.7 %all-gather.9.cloned.1.call-done.refs_0_ = bf16[4,136,1088]{2,1,0:T(8,128)(2,1)} async-done(((bf16[1,136,1088]{2,1,0:T(8,128)(2,1)}), bf16[4,136,1088]{2,1,0:T(8,128)(2,1)}) %all-gather.9.cloned.1.call-update) | async-done | bytes 1183760 | tf_op jit(solution)/shard_map/all_gather | solution.py:401
  50.6 27.7 %collective-permute-done.refs_1_ = bf16[4,136,1088]{2,1,0:T(8,128)(2,1)} collective-permute-done((bf16[4,136,1088]{2,1,0:T(8,128)(2,1)}, bf16[4,136,1088]{2,1,0:T(8,128)(2,1)}, u32[]{:S(2)}, u32[]{:S(2)}) %collective-permute-start) | collective-permute-done | bytes 1183776 | tf_op jit(solution)/shard_map/ppermute | solution.py:344
  79.6 13.8 %all-gather.1 = bf16[4,2,3264]{2,1,0:T(2,128)(2,1)S(1)} all-gather(bf16[1,2,3264]{2,1,0:T(2,128)(2,1)S(1)} %bitcast.632), channel_id=2, replica_groups=mesh['replica'=8,'shard'=4] {'shard'}, dimensions={0}, use_global_device_ids=true | all-gather | bytes 65280 | tf_op jit(solution)/shard_map/all_gather | solution.py:643
  111.4 3.6 collective-permute-done.7.refs_1_
  119.2 8.8 shard_map.271
  128.0 7.0 fusion.425
  138.1 4.8 collective-permute-done.8.refs_2_
  142.9 16.1 %collective-permute-done.9.refs_3_ = bf16[4,136,1088]{2,1,0:T(8,128)(2,1)} collective-permute-done((bf16[4,136,1088]{2,1,0:T(8,128)(2,1)}, bf16[4,136,1088]{2,1,0:T(8,128)(2,1)}, u32[]{:S(2)}, u32[]{:S(2)}) %collective-permute-start.9) | collective-permute-done | bytes 1183776 | tf_op jit(solution)/shard_map/ppermute | solution.py:344
  160.9 4.2 fusion.28.q_ref
  167.2 20.2 %shard_map.272 = (bf16[512,1088]{1,0:T(8,128)(2,1)S(1)}, f32[17,512,1]{2,1,0:T(8,128)}) custom-call(s32[512,1]{1,0:T(8,128)S(1)} %copy.177.starts_ref, bf16[512,1088]{1,0:T(8,128)(2,1)S(1)} %fusion.28.q_ref, bf16[512,1088]{1,0:T(8,128)(2,1)S(1)} %copy-done.9, bf16[512,1088]{1,0:T(8,128)(2,1)S(1)} %fusion.29.v_ref), custom_call_target="tpu_custom_call" | custom-call | flops 1140850688 | bytes 4456448 | tf_op jit(solution)/shard_map/pallas_call | solution.py:104
  204.7 8.6 shard_map.273
  213.3 7.4 fusion.424
  234.9 17.5 %collective-permute-done.22.refs_2_ = bf16[4,136,1088]{2,1,0:T(8,128)(2,1)} collective-permute-done((bf16[4,136,1088]{2,1,0:T(8,128)(2,1)}, bf16[4,136,1088]{2,1,0:T(8,128)(2,1)}, u32[]{:S(2)}, u32[]{:S(2)}) %collective-permute-start.22) | collective-permute-done | bytes 1183776 | tf_op jit(solution)/shard_map/ppermute | solution.py:344
  252.4 14.0 %collective-permute-done.23.refs_3_ = bf16[4,136,1088]{2,1,0:T(8,128)(2,1)} collective-permute-done((bf16[4,136,1088]{2,1,0:T(8,128)(2,1)}, bf16[4,136,1088]{2,1,0:T(8,128)(2,1)}, u32[]{:S(2)}, u32[]{:S(2)}) %collective-permute-start.23) | collective-permute-done | bytes 1183776 | tf_op jit(solution)/shard_map/ppermute | solution.py:344
  266.4 12.2 %multiply_convert_fusion.1 = bf16[512,4352]{0,1:T(8,128)(2,1)S(1)} fusion(f32[512,1088]{0,1:T(8,128)S(1)} %fusion.438, f32[512,1088]{0,1:T(8,128)S(1)} %fusion.437, f32[512,1088]{0,1:T(8,128)S(1)} %fusion.436, f32[512,1088]{0,1:T(8,128)S(1)} %fusion.435, f32[4352]{0:T(1024)S(1)} %reshape.598), kind=kLoop, calls=%fused_computation.23 | loop fusion | flops 28966912 | bytes 13386752 | tf_op jit(solution)/shard_map/convert_element_type | solution.py:227
  282.2 7.9 shard_map.274
  290.1 10.1 %fusion.433 = (f32[512]{0:T(512)S(1)}, f32[512,1088]{1,0:T(8,128)S(1)}) fusion(f32[1088]{0:T(1024)S(1)} %reshape.599, f32[512,1088]{1,0:T(8,128)S(1)} %copy-done.20, bf16[512,4352]{0,1:T(8,128)(2,1)S(1)} %multiply_convert_fusion.1, bf16[4352,1088]{1,0:T(8,128)(2,1)} %bitcast.470), kind=kOutput, calls=%fused_computation.588 | convolution fusion | flops 4850286080 | bytes 18389248 | tf_op jit(solution)/shard_map/dot_general | solution.py:230
  314.6 8.4 shard_map.275
  323.0 4.8 fusion.423
  333.8 20.0 %shard_map.276 = (bf16[512,1088]{1,0:T(8,128)(2,1)S(1)}, f32[17,512,1]{2,1,0:T(8,128)}) custom-call(s32[512,1]{1,0:T(8,128)S(1)} %copy.177.starts_ref, bf16[512,1088]{1,0:T(8,128)(2,1)S(1)} %fusion.30.q_ref, bf16[512,1088]{1,0:T(8,128)(2,1)S(1)} %convolution_convert_fusion.26.k_ref, bf16[512,1088]{1,0:T(8,128)(2,1)S(1)} %fusion.31.v_ref), custom_call_target="tpu_custom_call" | custom-call | flops 1140850688 | bytes 4456448 | tf_op jit(solution)/shard_map/pallas_call | solution.py:104
  372.3 8.4 shard_map.277
  380.7 4.6 fusion.422
  392.7 12.2 %multiply_convert_fusion = bf16[512,4352]{0,1:T(8,128)(2,1)S(1)} fusion(f32[512,1088]{0,1:T(8,128)S(1)} %fusion.442, f32[512,1088]{0,1:T(8,128)S(1)} %fusion.441, f32[512,1088]{0,1:T(8,128)S(1)} %fusion.440, f32[512,1088]{0,1:T(8,128)S(1)} %fusion.439, f32[4352]{0:T(1024)S(1)} %reshape.607), kind=kLoop, calls=%fused_computation.22 | loop fusion | flops 28966912 | bytes 13386752 | tf_op jit(solution)/shard_map/convert_element_type | solution.py:227
  416.8 8.1 shard_map.278
  424.9 18.2 %fusion.13 = bf16[512,4352]{0,1:T(8,128)(2,1)S(1)} fusion(f32[512,1088]{0,1:T(8,128)} %copy-done.104, f32[512,1088]{0,1:T(8,128)} %copy-done.105, f32[512,1088]{0,1:T(8,128)} %copy-done.106, f32[512,1088]{0,1:T(8,128)} %copy-done.107, f32[4352]{0:T(1024)S(1)} %reshape.607, bf16[4352,1088]{1,0:T(8,128)(2,1)} %bitcast.472, bf16[512,1088]{0,1:T(8,128)(2,1)} %param.31), kind=kOutput, calls=%fused_computation.17 | convolution fusion | flops 4902092800 | bytes 23970816 | tf_op jit(solution)/shard_map/td,fd->tf/dot_general | solution.py:269
  475.1 7.4 fusion.32
  482.5 4.5 multiply_reduce_fusion
  514.3 12.1 %collective-permute-done.52 = bf16[544,1088]{1,0:T(8,128)(2,1)} collective-permute-done((bf16[544,1088]{1,0:T(8,128)(2,1)}, bf16[544,1088]{1,0:T(8,128)(2,1)}, u32[]{:S(2)}, u32[]{:S(2)}) %collective-permute-start.52) | collective-permute-done | bytes 1183776 | tf_op jit(solution)/shard_map/ppermute | solution.py:344
  532.3 25.7 %shard_map.279 = (bf16[512,1088]{1,0:T(8,128)(2,1)S(1)}, bf16[512,1088]{1,0:T(8,128)(2,1)S(1)}, bf16[512,1088]{1,0:T(8,128)(2,1)S(1)}) custom-call(s32[512,1]{1,0:T(8,128)S(1)} %copy.177.starts_ref, bf16[512,1088]{1,0:T(8,128)(2,1)S(1)} %copy-done.17, bf16[512,1088]{1,0:T(8,128)(2,1)S(1)} %copy-done.15, bf16[512,1088]{1,0:T(8,128)(2,1)} %copy-done.18, ...), custom_call_target="tpu_custom_call" | custom-call | flops 2852126720 | bytes 7798784 | tf_op jit(solution)/shard_map/pallas_call | solution.py:163
  577.8 3.7 multiply_reduce_fusion.1
  619.6 8.0 collective-permute-done.91
  656.6 19.1 %fusion.6 = bf16[512,4352]{0,1:T(8,128)(2,1)} fusion(f32[512,1088]{0,1:T(8,128)} %copy-done.100, f32[512,1088]{0,1:T(8,128)} %copy-done.101, f32[512,1088]{0,1:T(8,128)} %copy-done.102, f32[512,1088]{0,1:T(8,128)} %copy-done.103, f32[4352]{0:T(1024)} %copy-done.134, bf16[512,1088]{1,0:T(8,128)(2,1)S(1)} %copy-done.55, bf16[4352,1088]{1,0:T(8,128)(2,1)} %bitcast.471), kind=kOutput, calls=%fused_computation.10 | convolution fusion | flops 4902092800 | bytes 23970816 | tf_op jit(solution)/shard_map/td,fd->tf/dot_general | solution.py:269
  689.6 3.6 collective-permute-done.67
  703.4 4.1 fusion.127
  739.6 8.6 collective-permute-done.68
  754.1 25.6 %shard_map.280 = (bf16[512,1088]{1,0:T(8,128)(2,1)S(1)}, bf16[512,1088]{1,0:T(8,128)(2,1)S(1)}, bf16[512,1088]{1,0:T(8,128)(2,1)S(1)}) custom-call(s32[512,1]{1,0:T(8,128)S(1)} %copy-done.8, bf16[512,1088]{1,0:T(8,128)(2,1)S(1)} %copy-done.12, bf16[512,1088]{1,0:T(8,128)(2,1)S(1)} %copy-done.10, bf16[512,1088]{1,0:T(8,128)(2,1)} %copy-done.13, ...), custom_call_target="tpu_custom_call" | custom-call | flops 2852126720 | bytes 7798784 | tf_op jit(solution)/shard_map/pallas_call | solution.py:163
  796.5 3.7 convolution_convert_fusion.3
  800.2 3.7 convolution_convert_fusion.2
  818.0 3.8 fusion.446
  829.5 4.1 add_convert_fusion.4
  858.3 10.3 %collective-permute-done.84 = f32[3264]{0:T(1024)S(1)} collective-permute-done((f32[3264]{0:T(1024)S(1)}, f32[3264]{0:T(1024)S(1)}, u32[]{:S(2)}, u32[]{:S(2)}) %collective-permute-start.84) | collective-permute-done | bytes 13088 | tf_op jit(solution)/shard_map/ppermute | solution.py:550
  871.9 4.0 add_add_fusion.4
  888.6 5.0 collective-permute-done.110
  896.4 5.0 reduce-scatter.25.cloned.1.call-done
  905.8 3.8 collective-permute-done.99
  912.1 3.9 collective-permute-done.107
  916.8 5.9 collective-permute-done.100
  (923 shorter events, 458.8 us)
Async XLA Ops:
  7.2 40.5 %all-gather.9.cloned.1.call-start = ((), (), s32[]{:S(2)}) async-start(), calls=%async_computation.6 | async-start | bytes 1566720 | tf_op jit(solution)/shard_map/all_gather | solution.py:401
  13.1 84.5 %all-gather.11.cloned.1.call-start = ((), (), s32[]{:S(2)}) async-start(), calls=%async_computation.7 | async-start | bytes 1566720 | tf_op jit(solution)/shard_map/all_gather | solution.py:401
  18.2 98.7 %all-gather.13.cloned.1.call-start = ((), (), s32[]{:S(2)}) async-start(), calls=%async_computation.8 | async-start | bytes 1566720 | tf_op jit(solution)/shard_map/all_gather | solution.py:401
  22.0 138.9 %all-gather.15.cloned.1.call-start = ((), (), s32[]{:S(2)}) async-start(), calls=%async_computation.9 | async-start | bytes 1566720 | tf_op jit(solution)/shard_map/all_gather | solution.py:401
  24.0 200.3 %all-gather.17.cloned.1.call-start = ((), (), s32[]{:S(2)}) async-start(), calls=%async_computation.10 | async-start | bytes 1566720 | tf_op jit(solution)/shard_map/all_gather | solution.py:401
  25.9 276.1 %all-gather.19.cloned.1.call-start = ((), (), s32[]{:S(2)}) async-start(), calls=%async_computation.11 | async-start | bytes 1566720 | tf_op jit(solution)/shard_map/all_gather | solution.py:401
  49.1 50.6 %collective-permute-start.1 = (bf16[4,136,1088]{2,1,0:T(8,128)(2,1)}, bf16[4,136,1088]{2,1,0:T(8,128)(2,1)}, u32[]{:S(2)}, u32[]{:S(2)}) collective-permute-start(bf16[4,136,1088]{2,1,0:T(8,128)(2,1)} %all-gather.9.cloned.1.call-done.refs_0_), channel_id=1, source_target_pairs={{0,16},{4,12},{8,24},{12,4},{16,0},{20,28},{24,8},{28,20},{1,17},{... | collective-permute-start | bytes 3551240 | tf_op jit(solution)/shard_map/ppermute | solution.py:344
  79.1 576.6 %reduce-scatter.19.cloned.1.call-start = ((), (), s32[]{:S(2)}) async-start(), calls=%async_computation.12 | async-start | bytes 1566720
  116.9 74.9 %collective-permute-start.10 = (bf16[4,136,1088]{2,1,0:T(8,128)(2,1)S(1)}, bf16[4,136,1088]{2,1,0:T(8,128)(2,1)}, u32[]{:S(2)}, u32[]{:S(2)}) collective-permute-start(bf16[4,136,1088]{2,1,0:T(8,128)(2,1)S(1)} %copy-done.3), channel_id=1, source_target_pairs={{0,4},{4,0},{8,12},{12,8},{16,20},{20,16},{24,28},{28,24},{1,5},{5... | collective-permute-start | bytes 3551240 | tf_op jit(solution)/shard_map/ppermute | solution.py:344
  116.9 42.0 %collective-permute-start.9 = (bf16[4,136,1088]{2,1,0:T(8,128)(2,1)}, bf16[4,136,1088]{2,1,0:T(8,128)(2,1)}, u32[]{:S(2)}, u32[]{:S(2)}) collective-permute-start(bf16[4,136,1088]{2,1,0:T(8,128)(2,1)} %collective-permute-done.7.refs_1_), channel_id=1, source_target_pairs={{0,16},{4,12},{8,24},{12,4},{16,0},{20,28},{24,8},{28,20},{1,17},{... | collective-permute-start | bytes 3551240 | tf_op jit(solution)/shard_map/ppermute | solution.py:344
  117.7 74.3 %collective-permute-start.11 = (bf16[4,136,1088]{2,1,0:T(8,128)(2,1)}, bf16[4,136,1088]{2,1,0:T(8,128)(2,1)}, u32[]{:S(2)}, u32[]{:S(2)}) collective-permute-start(bf16[4,136,1088]{2,1,0:T(8,128)(2,1)} %collective-permute-done.7.refs_1_), channel_id=1, source_target_pairs={{0,4},{4,0},{8,12},{12,8},{16,20},{20,16},{24,28},{28,24},{1,5},{5... | collective-permute-start | bytes 3551240 | tf_op jit(solution)/shard_map/ppermute | solution.py:344
  118.6 40.3 %collective-permute-start.14 = (bf16[4,136,1088]{2,1,0:T(8,128)(2,1)}, bf16[4,136,1088]{2,1,0:T(8,128)(2,1)}, u32[]{:S(2)}, u32[]{:S(2)}) collective-permute-start(bf16[4,136,1088]{2,1,0:T(8,128)(2,1)} %all-gather.13.cloned.1.call-done.refs_0_), channel_id=1, source_target_pairs={{0,8},{4,20},{8,0},{12,28},{16,24},{20,4},{24,16},{28,12},{1,9},{5... | collective-permute-start | bytes 3551240 | tf_op jit(solution)/shard_map/ppermute | solution.py:344
  159.0 61.7 %collective-permute-start.15 = (bf16[4,136,1088]{2,1,0:T(8,128)(2,1)S(1)}, bf16[4,136,1088]{2,1,0:T(8,128)(2,1)}, u32[]{:S(2)}, u32[]{:S(2)}) collective-permute-start(bf16[4,136,1088]{2,1,0:T(8,128)(2,1)S(1)} %copy-done.2), channel_id=1, source_target_pairs={{0,16},{4,12},{8,24},{12,4},{16,0},{20,28},{24,8},{28,20},{1,17},{... | collective-permute-start | bytes 3551240 | tf_op jit(solution)/shard_map/ppermute | solution.py:344
  204.2 77.4 %collective-permute-start.17 = (bf16[4,136,1088]{2,1,0:T(8,128)(2,1)S(1)}, bf16[4,136,1088]{2,1,0:T(8,128)(2,1)}, u32[]{:S(2)}, u32[]{:S(2)}) collective-permute-start(bf16[4,136,1088]{2,1,0:T(8,128)(2,1)S(1)} %copy-done.2), channel_id=1, source_target_pairs={{0,4},{4,0},{8,12},{12,8},{16,20},{20,16},{24,28},{28,24},{1,5},{5... | collective-permute-start | bytes 3551240 | tf_op jit(solution)/shard_map/ppermute | solution.py:344
  204.2 77.5 %collective-permute-start.18 = (bf16[4,136,1088]{2,1,0:T(8,128)(2,1)}, bf16[4,136,1088]{2,1,0:T(8,128)(2,1)}, u32[]{:S(2)}, u32[]{:S(2)}) collective-permute-start(bf16[4,136,1088]{2,1,0:T(8,128)(2,1)} %collective-permute-done.14.refs_1_), channel_id=1, source_target_pairs={{0,4},{4,0},{8,12},{12,8},{16,20},{20,16},{24,28},{28,24},{1,5},{5... | collective-permute-start | bytes 3551240 | tf_op jit(solution)/shard_map/ppermute | solution.py:344
  222.8 43.6 %collective-permute-start.23 = (bf16[4,136,1088]{2,1,0:T(8,128)(2,1)}, bf16[4,136,1088]{2,1,0:T(8,128)(2,1)}, u32[]{:S(2)}, u32[]{:S(2)}) collective-permute-start(bf16[4,136,1088]{2,1,0:T(8,128)(2,1)} %collective-permute-done.21.refs_1_), channel_id=1, source_target_pairs={{0,16},{4,12},{8,24},{12,4},{16,0},{20,28},{24,8},{28,20},{1,17},{... | collective-permute-start | bytes 3551240 | tf_op jit(solution)/shard_map/ppermute | solution.py:344
  224.3 56.8 %collective-permute-start.28 = (bf16[4,136,1088]{2,1,0:T(8,128)(2,1)}, bf16[4,136,1088]{2,1,0:T(8,128)(2,1)}, u32[]{:S(2)}, u32[]{:S(2)}) collective-permute-start(bf16[4,136,1088]{2,1,0:T(8,128)(2,1)} %all-gather.17.cloned.1.call-done.refs_0_), channel_id=1, source_target_pairs={{0,8},{4,20},{8,0},{12,28},{16,24},{20,4},{24,16},{28,12},{1,9},{5... | collective-permute-start | bytes 3551240 | tf_op jit(solution)/shard_map/ppermute | solution.py:344
  281.7 74.6 %collective-permute-start.29 = (bf16[4,136,1088]{2,1,0:T(8,128)(2,1)S(1)}, bf16[4,136,1088]{2,1,0:T(8,128)(2,1)}, u32[]{:S(2)}, u32[]{:S(2)}) collective-permute-start(bf16[4,136,1088]{2,1,0:T(8,128)(2,1)S(1)} %copy-done.1), channel_id=1, source_target_pairs={{0,16},{4,12},{8,24},{12,4},{16,0},{20,28},{24,8},{28,20},{1,17},{... | collective-permute-start | bytes 3551240 | tf_op jit(solution)/shard_map/ppermute | solution.py:344
  312.1 58.7 %collective-permute-start.31 = (bf16[4,136,1088]{2,1,0:T(8,128)(2,1)S(1)}, bf16[4,136,1088]{2,1,0:T(8,128)(2,1)}, u32[]{:S(2)}, u32[]{:S(2)}) collective-permute-start(bf16[4,136,1088]{2,1,0:T(8,128)(2,1)S(1)} %copy-done.1), channel_id=1, source_target_pairs={{0,4},{4,0},{8,12},{12,8},{16,20},{20,16},{24,28},{28,24},{1,5},{5... | collective-permute-start | bytes 3551240 | tf_op jit(solution)/shard_map/ppermute | solution.py:344
  312.5 43.7 %collective-permute-start.30 = (bf16[4,136,1088]{2,1,0:T(8,128)(2,1)}, bf16[4,136,1088]{2,1,0:T(8,128)(2,1)}, u32[]{:S(2)}, u32[]{:S(2)}) collective-permute-start(bf16[4,136,1088]{2,1,0:T(8,128)(2,1)} %collective-permute-done.28.refs_1_), channel_id=1, source_target_pairs={{0,16},{4,12},{8,24},{12,4},{16,0},{20,28},{24,8},{28,20},{1,17},{... | collective-permute-start | bytes 3551240 | tf_op jit(solution)/shard_map/ppermute | solution.py:344
  313.3 57.5 %collective-permute-start.32 = (bf16[4,136,1088]{2,1,0:T(8,128)(2,1)}, bf16[4,136,1088]{2,1,0:T(8,128)(2,1)}, u32[]{:S(2)}, u32[]{:S(2)}) collective-permute-start(bf16[4,136,1088]{2,1,0:T(8,128)(2,1)} %collective-permute-done.28.refs_1_), channel_id=1, source_target_pairs={{0,4},{4,0},{8,12},{12,8},{16,20},{20,16},{24,28},{28,24},{1,5},{5... | collective-permute-start | bytes 3551240 | tf_op jit(solution)/shard_map/ppermute | solution.py:344
  313.4 42.9 %collective-permute-start.35 = (bf16[4,136,1088]{2,1,0:T(8,128)(2,1)S(1)}, bf16[4,136,1088]{2,1,0:T(8,128)(2,1)}, u32[]{:S(2)}, u32[]{:S(2)}) collective-permute-start(bf16[4,136,1088]{2,1,0:T(8,128)(2,1)S(1)} %copy-done), channel_id=1, source_target_pairs={{0,8},{4,20},{8,0},{12,28},{16,24},{20,4},{24,16},{28,12},{1,9},{5... | collective-permute-start | bytes 3551240 | tf_op jit(solution)/shard_map/ppermute | solution.py:344
  356.3 50.7 %collective-permute-start.36 = (bf16[4,136,1088]{2,1,0:T(8,128)(2,1)S(1)}, bf16[4,136,1088]{2,1,0:T(8,128)(2,1)}, u32[]{:S(2)}, u32[]{:S(2)}) collective-permute-start(bf16[4,136,1088]{2,1,0:T(8,128)(2,1)S(1)} %copy-done), channel_id=1, source_target_pairs={{0,16},{4,12},{8,24},{12,4},{16,0},{20,28},{24,8},{28,20},{1,17},{... | collective-permute-start | bytes 3551240 | tf_op jit(solution)/shard_map/ppermute | solution.py:344
  370.8 45.2 %collective-permute-start.38 = (bf16[4,136,1088]{2,1,0:T(8,128)(2,1)S(1)}, bf16[4,136,1088]{2,1,0:T(8,128)(2,1)}, u32[]{:S(2)}, u32[]{:S(2)}) collective-permute-start(bf16[4,136,1088]{2,1,0:T(8,128)(2,1)S(1)} %copy-done), channel_id=1, source_target_pairs={{0,4},{4,0},{8,12},{12,8},{16,20},{20,16},{24,28},{28,24},{1,5},{5... | collective-permute-start | bytes 3551240 | tf_op jit(solution)/shard_map/ppermute | solution.py:344
  372.0 44.2 %collective-permute-start.39 = (bf16[4,136,1088]{2,1,0:T(8,128)(2,1)}, bf16[4,136,1088]{2,1,0:T(8,128)(2,1)}, u32[]{:S(2)}, u32[]{:S(2)}) collective-permute-start(bf16[4,136,1088]{2,1,0:T(8,128)(2,1)} %collective-permute-done.35.refs_1_), channel_id=1, source_target_pairs={{0,4},{4,0},{8,12},{12,8},{16,20},{20,16},{24,28},{28,24},{1,5},{5... | collective-permute-start | bytes 3551240 | tf_op jit(solution)/shard_map/ppermute | solution.py:344
  409.4 42.2 %collective-permute-start.42 = (bf16[544,1088]{1,0:T(8,128)(2,1)}, bf16[544,1088]{1,0:T(8,128)(2,1)}, u32[]{:S(2)}, u32[]{:S(2)}) collective-permute-start(bf16[544,1088]{1,0:T(8,128)(2,1)} %convolution_convert_fusion.23), channel_id=1, source_target_pairs={{0,4},{4,0},{8,12},{12,8},{16,20},{20,16},{24,28},{28,24},{1,5},{5... | collective-permute-start | bytes 3551240 | tf_op jit(solution)/shard_map/ppermute | solution.py:344
  416.0 42.3 %collective-permute-start.43 = (bf16[544,1088]{1,0:T(8,128)(2,1)}, bf16[544,1088]{1,0:T(8,128)(2,1)}, u32[]{:S(2)}, u32[]{:S(2)}) collective-permute-start(bf16[544,1088]{1,0:T(8,128)(2,1)} %convolution_convert_fusion.22), channel_id=1, source_target_pairs={{0,4},{4,0},{8,12},{12,8},{16,20},{20,16},{24,28},{28,24},{1,5},{5... | collective-permute-start | bytes 3551240 | tf_op jit(solution)/shard_map/ppermute | solution.py:344
  416.3 45.3 %collective-permute-start.44 = (bf16[544,1088]{1,0:T(8,128)(2,1)}, bf16[544,1088]{1,0:T(8,128)(2,1)}, u32[]{:S(2)}, u32[]{:S(2)}) collective-permute-start(bf16[544,1088]{1,0:T(8,128)(2,1)} %convolution_convert_fusion.21), channel_id=1, source_target_pairs={{0,4},{4,0},{8,12},{12,8},{16,20},{20,16},{24,28},{28,24},{1,5},{5... | collective-permute-start | bytes 3551240 | tf_op jit(solution)/shard_map/ppermute | solution.py:344
  473.3 40.9 %collective-permute-start.46 = (bf16[544,1088]{1,0:T(8,128)(2,1)}, bf16[544,1088]{1,0:T(8,128)(2,1)}, u32[]{:S(2)}, u32[]{:S(2)}) collective-permute-start(bf16[544,1088]{1,0:T(8,128)(2,1)} %add_convert_fusion.39), channel_id=1, source_target_pairs={{0,16},{4,12},{8,24},{12,4},{16,0},{20,28},{24,8},{28,20},{1,17},{... | collective-permute-start | bytes 3551240 | tf_op jit(solution)/shard_map/ppermute | solution.py:344
  507.7 60.7 %collective-permute-start.53 = (bf16[544,1088]{1,0:T(8,128)(2,1)}, bf16[544,1088]{1,0:T(8,128)(2,1)}, u32[]{:S(2)}, u32[]{:S(2)}) collective-permute-start(bf16[544,1088]{1,0:T(8,128)(2,1)} %add_convert_fusion.33), channel_id=1, source_target_pairs={{0,16},{4,12},{8,24},{12,4},{16,0},{20,28},{24,8},{28,20},{1,17},{... | collective-permute-start | bytes 3551240 | tf_op jit(solution)/shard_map/ppermute | solution.py:344
  532.3 171.2 %reduce-scatter.21.cloned.1.call-start = ((), (), s32[]{:S(2)}) async-start(), calls=%async_computation.13 | async-start | bytes 1566720
  561.9 41.6 %collective-permute-start.56 = (bf16[544,1088]{1,0:T(8,128)(2,1)}, bf16[544,1088]{1,0:T(8,128)(2,1)}, u32[]{:S(2)}, u32[]{:S(2)}) collective-permute-start(bf16[544,1088]{1,0:T(8,128)(2,1)} %convolution_convert_fusion.15), channel_id=1, source_target_pairs={{0,4},{4,0},{8,12},{12,8},{16,20},{20,16},{24,28},{28,24},{1,5},{5... | collective-permute-start | bytes 3551240 | tf_op jit(solution)/shard_map/ppermute | solution.py:344
  563.9 47.8 %collective-permute-start.57 = (bf16[544,1088]{1,0:T(8,128)(2,1)}, bf16[544,1088]{1,0:T(8,128)(2,1)}, u32[]{:S(2)}, u32[]{:S(2)}) collective-permute-start(bf16[544,1088]{1,0:T(8,128)(2,1)} %convolution_convert_fusion.14), channel_id=1, source_target_pairs={{0,4},{4,0},{8,12},{12,8},{16,20},{20,16},{24,28},{28,24},{1,5},{5... | collective-permute-start | bytes 3551240 | tf_op jit(solution)/shard_map/ppermute | solution.py:344
  596.7 39.7 %collective-permute-start.62 = (bf16[544,1088]{1,0:T(8,128)(2,1)}, bf16[544,1088]{1,0:T(8,128)(2,1)}, u32[]{:S(2)}, u32[]{:S(2)}) collective-permute-start(bf16[544,1088]{1,0:T(8,128)(2,1)} %add_convert_fusion.24), channel_id=1, source_target_pairs={{0,16},{4,12},{8,24},{12,4},{16,0},{20,28},{24,8},{28,20},{1,17},{... | collective-permute-start | bytes 3551240 | tf_op jit(solution)/shard_map/ppermute | solution.py:344
  602.1 93.8 %collective-permute-start.61 = (bf16[544,1088]{1,0:T(8,128)(2,1)}, bf16[544,1088]{1,0:T(8,128)(2,1)}, u32[]{:S(2)}, u32[]{:S(2)}) collective-permute-start(bf16[544,1088]{1,0:T(8,128)(2,1)} %add_convert_fusion.25), channel_id=1, source_target_pairs={{0,16},{4,12},{8,24},{12,4},{16,0},{20,28},{24,8},{28,20},{1,17},{... | collective-permute-start | bytes 3551240 | tf_op jit(solution)/shard_map/ppermute | solution.py:344
  603.5 40.8 %collective-permute-start.65 = (bf16[544,1088]{1,0:T(8,128)(2,1)}, bf16[544,1088]{1,0:T(8,128)(2,1)}, u32[]{:S(2)}, u32[]{:S(2)}) collective-permute-start(bf16[544,1088]{1,0:T(8,128)(2,1)} %convolution_convert_fusion.9), channel_id=1, source_target_pairs={{0,4},{4,0},{8,12},{12,8},{16,20},{20,16},{24,28},{28,24},{1,5},{5... | collective-permute-start | bytes 3551240 | tf_op jit(solution)/shard_map/ppermute | solution.py:344
  619.6 198.4 %reduce-scatter.23.cloned.1.call-start = ((), (), s32[]{:S(2)}) async-start(), calls=%async_computation.14 | async-start | bytes 1566720
  639.6 56.5 %collective-permute-start.69 = (bf16[544,1088]{1,0:T(8,128)(2,1)}, bf16[544,1088]{1,0:T(8,128)(2,1)}, u32[]{:S(2)}, u32[]{:S(2)}) collective-permute-start(bf16[544,1088]{1,0:T(8,128)(2,1)} %add_convert_fusion.22), channel_id=1, source_target_pairs={{0,8},{4,20},{8,0},{12,28},{16,24},{20,4},{24,16},{28,12},{1,9},{5... | collective-permute-start | bytes 3551240 | tf_op jit(solution)/shard_map/ppermute | solution.py:344
  644.2 56.0 %collective-permute-start.71 = (bf16[544,1088]{1,0:T(8,128)(2,1)}, bf16[544,1088]{1,0:T(8,128)(2,1)}, u32[]{:S(2)}, u32[]{:S(2)}) collective-permute-start(bf16[544,1088]{1,0:T(8,128)(2,1)} %add_convert_fusion.18), channel_id=1, source_target_pairs={{0,16},{4,12},{8,24},{12,4},{16,0},{20,28},{24,8},{28,20},{1,17},{... | collective-permute-start | bytes 3551240 | tf_op jit(solution)/shard_map/ppermute | solution.py:344
  648.8 101.7 %collective-permute-start.70 = (bf16[544,1088]{1,0:T(8,128)(2,1)}, bf16[544,1088]{1,0:T(8,128)(2,1)}, u32[]{:S(2)}, u32[]{:S(2)}) collective-permute-start(bf16[544,1088]{1,0:T(8,128)(2,1)} %add_convert_fusion.19), channel_id=1, source_target_pairs={{0,16},{4,12},{8,24},{12,4},{16,0},{20,28},{24,8},{28,20},{1,17},{... | collective-permute-start | bytes 3551240 | tf_op jit(solution)/shard_map/ppermute | solution.py:344
  699.8 185.5 %reduce-scatter.29.cloned.1.call-start = ((), (), s32[]{:S(2)}) async-start(), calls=%async_computation.17 | async-start | bytes 1566720
  727.5 111.2 %collective-permute-start.113 = (bf16[4,136,1088]{2,1,0:T(8,128)(2,1)}, bf16[4,136,1088]{2,1,0:T(8,128)(2,1)}, u32[]{:S(2)}, u32[]{:S(2)}) collective-permute-start(bf16[4,136,1088]{2,1,0:T(8,128)(2,1)} %pad_maximum_fusion.8), channel_id=1, source_target_pairs={{0,4},{4,0},{8,12},{12,8},{16,20},{20,16},{24,28},{28,24},{1,5},{5... | collective-permute-start | bytes 3551240 | tf_op jit(solution)/shard_map/ppermute | solution.py:344
  735.4 47.8 %collective-permute-start.79 = (bf16[544,1088]{1,0:T(8,128)(2,1)}, bf16[544,1088]{1,0:T(8,128)(2,1)}, u32[]{:S(2)}, u32[]{:S(2)}) collective-permute-start(bf16[544,1088]{1,0:T(8,128)(2,1)} %add_convert_fusion.11), channel_id=1, source_target_pairs={{0,16},{4,12},{8,24},{12,4},{16,0},{20,28},{24,8},{28,20},{1,17},{... | collective-permute-start | bytes 3551240 | tf_op jit(solution)/shard_map/ppermute | solution.py:344
  748.3 65.0 %collective-permute-start.78 = (bf16[544,1088]{1,0:T(8,128)(2,1)}, bf16[544,1088]{1,0:T(8,128)(2,1)}, u32[]{:S(2)}, u32[]{:S(2)}) collective-permute-start(bf16[544,1088]{1,0:T(8,128)(2,1)} %add_convert_fusion.12), channel_id=1, source_target_pairs={{0,16},{4,12},{8,24},{12,4},{16,0},{20,28},{24,8},{28,20},{1,17},{... | collective-permute-start | bytes 3551240 | tf_op jit(solution)/shard_map/ppermute | solution.py:344
  750.5 43.2 %collective-permute-start.76 = (bf16[2,136,1088]{2,1,0:T(8,128)(2,1)}, bf16[2,136,1088]{2,1,0:T(8,128)(2,1)}, u32[]{:S(2)}, u32[]{:S(2)}) collective-permute-start(bf16[2,136,1088]{2,1,0:T(8,128)(2,1)} %pad_maximum_fusion.15), channel_id=1, source_target_pairs={{0,16},{4,12},{8,24},{12,4},{16,0},{20,28},{24,8},{28,20},{1,17},{... | collective-permute-start | bytes 1775624 | tf_op jit(solution)/shard_map/ppermute | solution.py:344
  796.2 54.3 %collective-permute-start.109 = (bf16[4,136,1088]{2,1,0:T(8,128)(2,1)}, bf16[4,136,1088]{2,1,0:T(8,128)(2,1)}, u32[]{:S(2)}, u32[]{:S(2)}) collective-permute-start(bf16[4,136,1088]{2,1,0:T(8,128)(2,1)} %pad_maximum_fusion.9), channel_id=1, source_target_pairs={{0,4},{4,0},{8,12},{12,8},{16,20},{20,16},{24,28},{28,24},{1,5},{5... | collective-permute-start | bytes 3551240 | tf_op jit(solution)/shard_map/ppermute | solution.py:344
  796.2 91.1 %reduce-scatter.27.cloned.1.call-start = ((), (), s32[]{:S(2)}) async-start(), calls=%async_computation.16 | async-start | bytes 1566720
  833.6 67.7 %reduce-scatter.25.cloned.1.call-start = ((), (), s32[]{:S(2)}) async-start(), calls=%async_computation.15 | async-start | bytes 1566720
  (276 other events, 4617.3 us)
Sparse Core Ops, SparseCore 0:
  13.2 34.3 all-gather.8
  49.8 30.7 all-gather.10
  82.7 30.8 all-gather.12
  115.0 30.6 all-gather.14
  147.2 30.7 all-gather.16
  179.4 30.7 all-gather.18
  532.4 28.0 reduce-scatter.18
  619.7 40.7 reduce-scatter.20
  699.9 30.5 reduce-scatter.22
  796.3 30.2 reduce-scatter.28
  833.8 30.6 reduce-scatter.26
  871.8 29.4 reduce-scatter.24

commit v4 on v3

--- a/solution.py
+++ b/solution.py
@@ -22,8 +22,13 @@
     return center * lax.rsqrt(spread + norm_eps) * norm_gain + norm_shift
 
 
-def gelu_tanh(values):
-    return jax.nn.gelu(values, approximate=True)
+def gelu_and_slope(values):
+    inner = 0.7978845608028654 * (values + 0.044715 * values * values * values)
+    bend = jnp.tanh(inner)
+    value = 0.5 * values * (1.0 + bend)
+    rate = 0.7978845608028654 * (1.0 + 0.134145 * values * values)
+    slope = 0.5 * (1.0 + bend) + 0.5 * values * (1.0 - bend * bend) * rate
+    return value, slope
 
 
 def sequence_starts(lengths, count):
@@ -224,7 +229,8 @@
         after_attn, norm2_gain.astype(jnp.float32), norm2_shift.astype(jnp.float32)
     ).astype(jnp.bfloat16)
     hidden_pre = dot_columns(normed_two, up_weight) + up_bias.astype(jnp.float32)
-    activated = gelu_tanh(hidden_pre).astype(jnp.bfloat16)
+    activated, slope = gelu_and_slope(hidden_pre)
+    activated, slope = lax.optimization_barrier((activated.astype(jnp.bfloat16), slope))
     result = (
         after_attn
         + jnp.dot(activated, down_weight, preferred_element_type=jnp.float32)
@@ -240,7 +246,7 @@
             log_total,
             after_attn,
             normed_two,
-            hidden_pre,
+            slope,
             activated,
         ),
     )
@@ -259,17 +265,16 @@
         up_bias,
         down_bias,
     ) = small
-    stream, normed, projected, mixed, log_total, after_attn, normed_two, hidden_pre, activated = (
+    stream, normed, projected, mixed, log_total, after_attn, normed_two, slope, activated = (
         saved
     )
     grad_branch = grad_out.astype(jnp.bfloat16)
-    sum_group("down", down_product(layout, activated, grad_branch))
+    sum_group("down", down_group(layout, activated, grad_branch))
     grad_branch = pipe.advance(grad_branch)
     grad_down_bias = jnp.sum(grad_branch.astype(jnp.float32), axis=0)
     grad_act = jnp.einsum("td,fd->tf", grad_branch, down_weight, preferred_element_type=jnp.float32)
-    gelu_value, gelu_pull = jax.vjp(gelu_tanh, hidden_pre)
-    grad_pre = gelu_pull(grad_act)[0].astype(jnp.bfloat16)
-    sum_group("up", up_product(layout, normed_two, grad_pre))
+    grad_pre = (grad_act * slope).astype(jnp.bfloat16)
+    sum_group("up", up_group(layout, normed_two, grad_pre))
     grad_pre = pipe.advance(grad_pre)
     grad_up_bias = jnp.sum(grad_pre.astype(jnp.float32), axis=0)
     grad_normed_two = dot_columns_back(grad_pre, up_weight)
@@ -283,7 +288,7 @@
     grad_mixed = dot_columns_back(grad_attn, out_weight).astype(jnp.bfloat16)
     grad_mixed = pipe.advance(grad_mixed)
     thirds = attend_back(*projected, log_total, grad_mixed, starts)
-    sum_group("first", first_product(layout, normed, thirds, mixed, grad_attn))
+    sum_group("first", first_group(layout, normed, thirds, mixed, grad_attn))
     thirds = pipe.advance(thirds)
     grad_query_bias = jnp.sum(thirds[0].astype(jnp.float32), axis=0)
     grad_value_bias = jnp.sum(thirds[2].astype(jnp.float32), axis=0)
@@ -418,28 +423,73 @@
     return (left.astype(jnp.float32) + right.astype(jnp.float32)).astype(jnp.bfloat16)
 
 
-def reduce_steps(layout, product, finish):
+def product_kernel(index_ref, rows_ref, cols_ref, *refs):
+    total = jnp.dot(rows_ref[0, 0], cols_ref[0], preferred_element_type=jnp.float32)
+    if len(refs) == 2:
+        total = total + refs[0][0].astype(jnp.float32)
+    refs[-1][0] = total.astype(jnp.bfloat16)
+
+
+def products(rows, cols, index, came=None, skip=0):
+    steps = index.shape[1]
+    height, width = rows.shape[2], cols.shape[2]
+    in_specs = [
+        pl.BlockSpec((1, 1) + rows.shape[2:], lambda i, at: (at[0, i], at[1, i], 0, 0)),
+        pl.BlockSpec((1,) + cols.shape[1:], lambda i, at: (at[2, i], 0, 0)),
+    ]
+    operands = [rows, cols]
+    if came is not None:
+        in_specs.append(pl.BlockSpec((1, height, width), lambda i, at: (i + skip, 0, 0)))
+        operands.append(came)
+    return pl.pallas_call(
+        product_kernel,
+        out_shape=jax.ShapeDtypeStruct((steps, height, width), jnp.bfloat16),
+        grid_spec=pltpu.PrefetchScalarGridSpec(
+            num_scalar_prefetch=1,
+            grid=(steps,),
+            in_specs=in_specs,
+            out_specs=pl.BlockSpec((1, height, width), lambda i, at: (i, 0, 0)),
+        ),
+        compiler_params=pltpu.CompilerParams(vmem_limit_bytes=40 << 20),
+        cost_estimate=pl.CostEstimate(
+            flops=2 * steps * height * width * rows.shape[3],
+            bytes_accessed=4 * steps * height * width,
+            transcendentals=0,
+        ),
+    )(index, *operands)
+
+
+def reduce_steps(layout, group, finish):
+    rows, cols, blocks_of = group
     _, _, core, _ = layout.place()
     n, last = layout.shards, layout.across - 1
-    away = {
-        (f, k): product(layout.chip_at(1 - core, f, k), 1 - core).astype(jnp.bfloat16)
-        for f, k in layout.slots()
-    }
-    came = {slot: layout.move(value, "core") for slot, value in away.items()}
-    yield list(away.values())
-    sums = {}
-    for f, k in layout.slots():
-        here = product(layout.chip_at(core, f, k), core)
-        sums[f, k] = (here + came[f, k].astype(jnp.float32)).astype(jnp.bfloat16)
-    totals = [sums[f, last] for f in range(2)]
-    for step in range(1, layout.across):
-        moved = [layout.move(total, "second") for total in totals]
-        if step == 1:
-            yield list(sums.values())
-        totals = [add_low(moved[f], sums[f, last - step]) for f in range(2)]
-    moved = layout.move(totals[1], "first")
-    yield totals
-    total = add_low(moved, totals[0])
+    slots = layout.slots()
+
+    def index(side, wanted):
+        places = [blocks_of(layout.chip_at(side, f, k)) for f, k in wanted]
+        return jnp.stack(
+            [
+                jnp.stack([jnp.asarray(i, jnp.int32) for i, _ in places]),
+                jnp.stack([side] * len(places)).astype(jnp.int32),
+                jnp.stack([jnp.asarray(i, jnp.int32) for _, i in places]),
+            ]
+        )
+
+    away = products(rows, cols, index(1 - core, slots))
+    came = layout.move(away, "core")
+    yield [away]
+    total = products(rows, cols, index(core, slots[2 * last :]), came, 2 * last)
+    moved = layout.move(total, "second")
+    kept = products(rows, cols, index(core, slots[: 2 * last]), came, 0)
+    yield [total, kept]
+    for step in range(1, last):
+        total = add_low(moved, kept[2 * (last - step) : 2 * (last - step) + 2])
+        moved = layout.move(total, "second")
+    sent = add_low(moved[1], kept[1])
+    held = add_low(moved[0], kept[0])
+    moved = layout.move(sent, "first")
+    yield [sent, held]
+    total = add_low(moved, held)
     total = total.reshape((n, total.shape[0] // n) + total.shape[1:])
     piece = lax.psum_scatter(total, "shard", scatter_dimension=0, tiled=False)
     yield [total]
@@ -492,40 +542,22 @@
     return lax.dynamic_index_in_dim(value, i, axis=0, keepdims=False)
 
 
-def down_product(layout, activated, grad_branch):
-    rows = by_core_rows(layout, activated, layout.chips)
-
-    def product(chip, core):
-        return jnp.dot(pick(pick(rows, chip), core), grad_branch, preferred_element_type=jnp.float32)
-
-    return product
-
-
-def up_product(layout, normed_two, grad_pre):
-    rows = by_core_rows(layout, normed_two, 1)[0]
-    chunks = column_chunks(layout, grad_pre)
-
-    def product(chip, core):
-        return jnp.dot(pick(rows, core), pick(chunks, chip), preferred_element_type=jnp.float32)
-
-    return product
-
-
-def first_product(layout, normed, thirds, mixed, grad_attn):
-    one_rows = by_core_rows(layout, normed, 1)[0]
-    mixed_rows = by_core_rows(layout, mixed, 1)[0]
+def down_group(layout, activated, grad_branch):
+    return by_core_rows(layout, activated, layout.chips), grad_branch[None], lambda chip: (chip, 0)
+
+
+def up_group(layout, normed_two, grad_pre):
+    return by_core_rows(layout, normed_two, 1), column_chunks(layout, grad_pre), lambda chip: (0, chip)
+
+
+def first_group(layout, normed, thirds, mixed, grad_attn):
+    rows = jnp.concatenate([by_core_rows(layout, normed, 1), by_core_rows(layout, mixed, 1)])
     if layout.chips == 4:
-        chunks = jnp.stack(list(thirds) + [grad_attn])
+        cols = jnp.stack(list(thirds) + [grad_attn])
     else:
-        chunks = column_chunks(layout, jnp.concatenate(list(thirds) + [grad_attn], axis=1))
-
-    def product(chip, core):
-        rows = jnp.where(
-            chip < 3 * layout.chips // 4, pick(one_rows, core), pick(mixed_rows, core)
-        )
-        return jnp.dot(rows, pick(chunks, chip), preferred_element_type=jnp.float32)
-
-    return product
+        cols = column_chunks(layout, jnp.concatenate(list(thirds) + [grad_attn], axis=1))
+    cut = 3 * layout.chips // 4
+    return rows, cols, lambda chip: ((chip >= cut).astype(jnp.int32), chip)
 
 
 def block_order(layout):
@@ -698,7 +730,7 @@
         pipe = Pipe()
         held = {"first": None, "up": None, "down": None}
 
-        def sum_group(name, l, product):
+        def sum_group(name, l, group):
             cut = 3 * chips // 4
             splits = (cut, chips - cut) if name == "first" else (chips,)
 
@@ -707,7 +739,7 @@
                     layout, whole, l, layer_count, name == "down", splits, held[name]
                 )
 
-            pipe.begin(reduce_steps(layout, product, finish))
+            pipe.begin(reduce_steps(layout, group, finish))
 
         for l in reversed(range(layer_count)):
             grad_stream, vectors = backward_layer(
@@ -717,7 +749,7 @@
                 starts,
                 layout,
                 pipe,
-                lambda name, product, l=l: sum_group(name, l, product),
+                lambda name, group, l=l: sum_group(name, l, group),
             )
             shares[l] = sum_vectors(layout, vectors)
         pipe.drain()

time: 952 us -> 1020 us (1.071)
  matrix products: 266 us -> 130 us
  waiting for transfers between devices: 178 us -> 268 us
  Pallas kernels: 161 us -> 241 us
  local copies, waits for them, and re-layouts: 109 us -> 139 us
  other arithmetic: 122 us -> 142 us
  starting transfers between devices: 78.2 us -> 62.8 us
    dot_general x48 -> x0, matrix products: 132 us -> none  [the longest x16 45.6 us: product(): return jnp.dot(rows, pick(chunks, chip), preferred_element_type=jnp.float32)]
    pallas_call x0 -> x18, Pallas kernels: none -> 82 us  [products(): pl.pallas_call(product_kernel, out_shape=jax.ShapeDtypeStruct((steps, hei...]
    ppermute x102 -> x78, waiting for transfers between devices: 129 us -> 191 us  [move(): return lax.ppermute(value, 'replica', self.pairs(way))]
    add x0 -> x2, other arithmetic: none -> 29.4 us  [gelu_and_slope(): slope = 0.5 * (1.0 + bend) + 0.5 * values * (1.0 - bend * bend) * rate]
    unnamed x400 -> x436, local copies, waits for them, and re-layouts: 24 us -> 50.2 us
    convert_element_type x2 -> x0, other arithmetic: 24.4 us -> none  [forward_layer(): activated = gelu_tanh(hidden_pre).astype(jnp.bfloat16)]
    ppermute x6, waiting for transfers between devices: 3.83 us -> 24.9 us  [sum_vectors(): total = lax.ppermute(total, 'shard', [(i, (i + 1) % n) for i in range(n)])]
    reshape x0 -> x2, local copies, waits for them, and re-layouts: none -> 13.1 us  [column_chunks(): return rows.reshape(rows.shape[0], layout.chips, -1).transpose(1, 0, 2)]
  transfers between devices with their start and end apart: 126 -> 102, of which waited for: 23 -> 36; matrix products, arithmetic and copies ran while one was open for 49% -> 35% of each run, Pallas kernels for 17% -> 20%
where the time goes in v4:
time: 1020 us; the launch traced here: 1010 us
  waiting for transfers between devices  268 us (26%)
  Pallas kernels  241 us (24%)
  other arithmetic  142 us (14%)
  local copies, waits for them, and re-layouts  139 us (14%)
  matrix products  130 us (13%)
  starting transfers between devices  62.8 us (6%)
  between operations  17.7 us (2%)
  blocking collectives  13.4 us (1%)
    ppermute x78, waiting for transfers between devices, move(): return lax.ppermute(value, 'replica', self.pairs(way))  191 us
    pallas_call x18, Pallas kernels, products(): pl.pallas_call(product_kernel, out_shape=jax.ShapeDtypeStruct((steps, hei...  82 us
    ppermute x78, starting transfers between devices, move(): return lax.ppermute(value, 'replica', self.pairs(way))  58.1 us
    pallas_call x2, Pallas kernels, attend_back(): pl.pallas_call(attend_back_kernel, out_shape=(shape, shape, shape), scrat...  51.8 us
    unnamed x436, local copies, waits for them, and re-layouts  50.2 us
    pallas_call x6, Pallas kernels, assemble(): pl.pallas_call(functools.partial(place_kernel, by_shard), out_shape=jax.S...  47.7 us
    pallas_call x2, Pallas kernels, attend(): pl.pallas_call(attend_kernel, out_shape=(jax.ShapeDtypeStruct((count, wid...  40.2 us
    convert_element_type x12, other arithmetic, add_low(): (left.astype(jnp.float32) + right.astype(jnp.float32)).astype(jnp.bfloat16)  37.4 us
  transfers between devices with their start and end apart: 102, of which 36 were waited for; matrix products, arithmetic and copies ran while one was open for 35% of the time, Pallas kernels for 20%

profile of v4, /device:TPU:0, one launch (start us, length us, event | category | flops | bytes accessed | tf_op | source)
XLA Modules:
  0.0 1013.9 jit_solution(15139853253622093656)
XLA Ops:
  24.0 23.6 %all-gather.9.cloned.1.call-done.refs_0_ = bf16[4,136,1088]{2,1,0:T(8,128)(2,1)} async-done(((bf16[1,136,1088]{2,1,0:T(8,128)(2,1)}), bf16[4,136,1088]{2,1,0:T(8,128)(2,1)}) %all-gather.9.cloned.1.call-update) | async-done | bytes 1183760 | tf_op jit(solution)/shard_map/all_gather | solution.py:406
  52.6 24.3 %collective-permute-done.refs_1_ = bf16[4,136,1088]{2,1,0:T(8,128)(2,1)} collective-permute-done((bf16[4,136,1088]{2,1,0:T(8,128)(2,1)}, bf16[4,136,1088]{2,1,0:T(8,128)(2,1)}, u32[]{:S(2)}, u32[]{:S(2)}) %collective-permute-start) | collective-permute-done | bytes 1183776 | tf_op jit(solution)/shard_map/ppermute | solution.py:349
  80.6 13.4 %all-gather.1 = bf16[4,2,3264]{2,1,0:T(2,128)(2,1)S(1)} all-gather(bf16[1,2,3264]{2,1,0:T(2,128)(2,1)S(1)} %bitcast.369), channel_id=2, replica_groups=mesh['replica'=8,'shard'=4] {'shard'}, dimensions={0}, use_global_device_ids=true | all-gather | bytes 65280 | tf_op jit(solution)/shard_map/all_gather | solution.py:675
  117.2 8.7 shard_map.271
  126.0 5.8 fusion.109
  131.8 10.3 %collective-permute-done.8.refs_2_ = bf16[4,136,1088]{2,1,0:T(8,128)(2,1)} collective-permute-done((bf16[4,136,1088]{2,1,0:T(8,128)(2,1)}, bf16[4,136,1088]{2,1,0:T(8,128)(2,1)}, u32[]{:S(2)}, u32[]{:S(2)}) %collective-permute-start.8) | collective-permute-done | bytes 1183776 | tf_op jit(solution)/shard_map/ppermute | solution.py:349
  142.1 14.3 %collective-permute-done.9.refs_3_ = bf16[4,136,1088]{2,1,0:T(8,128)(2,1)S(1)} collective-permute-done((bf16[4,136,1088]{2,1,0:T(8,128)(2,1)}, bf16[4,136,1088]{2,1,0:T(8,128)(2,1)S(1)}, u32[]{:S(2)}, u32[]{:S(2)}) %collective-permute-start.9) | collective-permute-done | bytes 1183776 | tf_op jit(solution)/shard_map/ppermute | solution.py:349
  163.2 20.2 %shard_map.272 = (bf16[512,1088]{1,0:T(8,128)(2,1)S(1)}, f32[17,512,1]{2,1,0:T(8,128)}) custom-call(s32[512,1]{1,0:T(8,128)S(1)} %copy.186.starts_ref, bf16[512,1088]{1,0:T(8,128)(2,1)S(1)} %fusion.26.q_ref, bf16[512,1088]{1,0:T(8,128)(2,1)S(1)} %convolution_convert_fusion.3.k_ref, bf16[512,1088]{1,0:T(8,128)(2,1)S(1)} %fusion.27.v_ref), custom_call_target="tpu_custom_call" | custom-call | flops 1140850688 | bytes 4456448 | tf_op jit(solution)/shard_map/pallas_call | solution.py:109
  195.4 7.7 shard_map.273
  203.0 7.4 fusion.108
  210.4 11.0 %collective-permute-done.16.refs_3_ = bf16[4,136,1088]{2,1,0:T(8,128)(2,1)} collective-permute-done((bf16[4,136,1088]{2,1,0:T(8,128)(2,1)}, bf16[4,136,1088]{2,1,0:T(8,128)(2,1)}, u32[]{:S(2)}, u32[]{:S(2)}) %collective-permute-start.16) | collective-permute-done | bytes 1183776 | tf_op jit(solution)/shard_map/ppermute | solution.py:349
  233.5 18.0 %collective-permute-done.22.refs_2_ = bf16[4,136,1088]{2,1,0:T(8,128)(2,1)} collective-permute-done((bf16[4,136,1088]{2,1,0:T(8,128)(2,1)}, bf16[4,136,1088]{2,1,0:T(8,128)(2,1)}, u32[]{:S(2)}, u32[]{:S(2)}) %collective-permute-start.22) | collective-permute-done | bytes 1183776 | tf_op jit(solution)/shard_map/ppermute | solution.py:349
  251.6 14.0 %collective-permute-done.23.refs_3_ = bf16[4,136,1088]{2,1,0:T(8,128)(2,1)} collective-permute-done((bf16[4,136,1088]{2,1,0:T(8,128)(2,1)}, bf16[4,136,1088]{2,1,0:T(8,128)(2,1)}, u32[]{:S(2)}, u32[]{:S(2)}) %collective-permute-start.23) | collective-permute-done | bytes 1183776 | tf_op jit(solution)/shard_map/ppermute | solution.py:349
  265.6 14.9 %fusion.5 = (f32[512,4352]{0,1:T(8,128)}, bf16[512,4352]{0,1:T(8,128)(2,1)S(1)}) fusion(f32[512,1088]{0,1:T(8,128)S(1)} %fusion.122, f32[512,1088]{0,1:T(8,128)S(1)} %fusion.121, f32[512,1088]{0,1:T(8,128)S(1)} %fusion.120, f32[512,1088]{0,1:T(8,128)S(1)} %fusion.119, f32[4352]{0:T(1024)S(1)} %reshape.594), kind=kLoop, calls=%fused_computation.9 | loop fusion | flops 51249152 | bytes 22299648 | tf_op jit(solution)/shard_map/add | solution.py:30
  283.5 7.9 shard_map.274
  291.4 11.4 %fusion.117 = (f32[512]{0:T(512)S(1)}, f32[512,1088]{1,0:T(8,128)}) fusion(f32[1088]{0:T(1024)S(1)} %reshape.595, f32[512,1088]{1,0:T(8,128)S(1)} %copy-done.73, bf16[512,4352]{0,1:T(8,128)(2,1)S(1)} %get-tuple-element.65, bf16[4352,1088]{1,0:T(8,128)(2,1)} %bitcast.294), kind=kOutput, calls=%fused_computation.288 | convolution fusion | flops 4850286080 | bytes 18389248 | tf_op jit(solution)/shard_map/dot_general | solution.py:236
  310.0 7.7 shard_map.275
  317.8 5.7 fusion.107
  323.6 12.4 %collective-permute-done.30.refs_3_ = bf16[4,136,1088]{2,1,0:T(8,128)(2,1)S(1)} collective-permute-done((bf16[4,136,1088]{2,1,0:T(8,128)(2,1)}, bf16[4,136,1088]{2,1,0:T(8,128)(2,1)S(1)}, u32[]{:S(2)}, u32[]{:S(2)}) %collective-permute-start.30) | collective-permute-done | bytes 1183776 | tf_op jit(solution)/shard_map/ppermute | solution.py:349
  342.4 20.0 %shard_map.276 = (bf16[512,1088]{1,0:T(8,128)(2,1)S(1)}, f32[17,512,1]{2,1,0:T(8,128)}) custom-call(s32[512,1]{1,0:T(8,128)S(1)} %copy-done.53, bf16[512,1088]{1,0:T(8,128)(2,1)S(1)} %fusion.28.q_ref, bf16[512,1088]{1,0:T(8,128)(2,1)S(1)} %convolution_convert_fusion.2.k_ref, bf16[512,1088]{1,0:T(8,128)(2,1)S(1)} %fusion.29.v_ref), custom_call_target="tpu_custom_call" | custom-call | flops 1140850688 | bytes 4456448 | tf_op jit(solution)/shard_map/pallas_call | solution.py:109
  372.8 6.6 shard_map.277
  391.9 14.5 %fusion.11 = (f32[512,4352]{0,1:T(8,128)}, bf16[512,4352]{0,1:T(8,128)(2,1)S(1)}) fusion(f32[512,1088]{0,1:T(8,128)S(1)} %fusion.126, f32[512,1088]{0,1:T(8,128)S(1)} %fusion.125, f32[512,1088]{0,1:T(8,128)S(1)} %fusion.124, f32[512,1088]{0,1:T(8,128)S(1)} %fusion.123, f32[4352]{0:T(1024)S(1)} %copy-done.149), kind=kLoop, calls=%fused_computation.15 | loop fusion | flops 51249152 | bytes 22299648 | tf_op jit(solution)/shard_map/add | solution.py:30
  408.4 5.4 shard_map.279
  419.3 9.1 shard_map.278
  428.5 12.1 %multiply_convert_fusion.1 = bf16[512,4352]{0,1:T(8,128)(2,1)} fusion(f32[512,4352]{0,1:T(8,128)S(1)} %bitcast.303, bf16[4352,1088]{1,0:T(8,128)(2,1)} %bitcast.292, bf16[512,1088]{0,1:T(8,128)(2,1)S(1)} %copy-done.104), kind=kOutput, calls=%fused_computation.21 | convolution fusion | flops 4853071872 | bytes 23953408 | tf_op jit(solution)/shard_map/td,fd->tf/dot_general | solution.py:275
  440.6 6.6 copy.201
  449.5 5.4 shard_map.282
  500.3 8.6 collective-permute-done.43
  522.8 19.6 %collective-permute-done.45 = bf16[544,1088]{1,0:T(8,128)(2,1)} collective-permute-done((bf16[544,1088]{1,0:T(8,128)(2,1)}, bf16[544,1088]{1,0:T(8,128)(2,1)}, u32[]{:S(2)}, u32[]{:S(2)}) %collective-permute-start.45) | collective-permute-done | bytes 1183776 | tf_op jit(solution)/shard_map/ppermute | solution.py:349
  553.5 26.1 %shard_map.285 = (bf16[512,1088]{1,0:T(8,128)(2,1)S(1)}, bf16[512,1088]{1,0:T(8,128)(2,1)S(1)}, bf16[512,1088]{1,0:T(8,128)(2,1)S(1)}) custom-call(s32[512,1]{1,0:T(8,128)S(1)} %copy-done.54, bf16[512,1088]{1,0:T(8,128)(2,1)S(1)} %copy-done.67, bf16[512,1088]{1,0:T(8,128)(2,1)S(1)} %copy-done.65, bf16[512,1088]{1,0:T(8,128)(2,1)} %copy-done.68, ...), custom_call_target="tpu_custom_call" | custom-call | flops 2852126720 | bytes 7798784 | tf_op jit(solution)/shard_map/pallas_call | solution.py:168
  580.5 5.4 shard_map.286
  599.8 5.6 shard_map.289
  628.1 5.4 reduce-scatter.21.cloned.1.call-done
  641.6 15.3 %collective-permute-done.52 = bf16[2,136,1088]{2,1,0:T(8,128)(2,1)} collective-permute-done((bf16[2,136,1088]{2,1,0:T(8,128)(2,1)}, bf16[2,136,1088]{2,1,0:T(8,128)(2,1)}, u32[]{:S(2)}, u32[]{:S(2)}) %collective-permute-start.52) | collective-permute-done | bytes 591904 | tf_op jit(solution)/shard_map/ppermute | solution.py:349
  678.1 12.9 %multiply_convert_fusion = bf16[512,4352]{0,1:T(8,128)(2,1)} fusion(f32[512,4352]{0,1:T(8,128)} %get-tuple-element.92, bf16[512,1088]{1,0:T(8,128)(2,1)S(1)} %copy-done.12, bf16[4352,1088]{1,0:T(8,128)(2,1)} %bitcast.295), kind=kOutput, calls=%fused_computation.20 | convolution fusion | flops 4853071872 | bytes 23953408 | tf_op jit(solution)/shard_map/td,fd->tf/dot_general | solution.py:275
  691.0 6.5 copy.219
  701.1 5.4 shard_map.292
  757.1 25.7 %shard_map.295 = (bf16[512,1088]{1,0:T(8,128)(2,1)S(1)}, bf16[512,1088]{1,0:T(8,128)(2,1)S(1)}, bf16[512,1088]{1,0:T(8,128)(2,1)S(1)}) custom-call(s32[512,1]{1,0:T(8,128)S(1)} %copy-done.55, bf16[512,1088]{1,0:T(8,128)(2,1)S(1)} %copy-done.62, bf16[512,1088]{1,0:T(8,128)(2,1)S(1)} %copy-done.60, bf16[512,1088]{1,0:T(8,128)(2,1)} %copy-done.63, ...), custom_call_target="tpu_custom_call" | custom-call | flops 2852126720 | bytes 7798784 | tf_op jit(solution)/shard_map/pallas_call | solution.py:168
  784.7 5.4 shard_map.296
  798.8 5.6 collective-permute-done.66
  804.4 5.9 collective-permute-done.67
  810.3 6.1 collective-permute-done.68
  822.7 12.0 %fusion.30 = bf16[512,1088]{1,0:T(8,128)(2,1)} fusion(f32[512,1088]{1,0:T(8,128)} %copy-done.69, bf16[512,4352]{0,1:T(8,128)(2,1)} %copy-done.89, bf16[4352,1088]{1,0:T(8,128)(2,1)} %bitcast.293, f32[1088]{0:T(1024)S(1)} %reshape.604), kind=kOutput, calls=%fused_computation.66 | convolution fusion | flops 4850286592 | bytes 17273088 | tf_op jit(solution)/shard_map/dot_general | solution.py:236
  837.0 15.6 %collective-permute-done.71 = f32[3264]{0:T(1024)S(1)} collective-permute-done((f32[3264]{0:T(1024)S(1)}, f32[3264]{0:T(1024)S(1)}, u32[]{:S(2)}, u32[]{:S(2)}) %collective-permute-start.71) | collective-permute-done | bytes 13088 | tf_op jit(solution)/shard_map/ppermute | solution.py:582
  864.9 5.3 collective-permute-done.57
  895.2 5.5 fusion.130
  908.1 8.4 collective-permute-done.73
  986.6 5.9 collective-permute-done.76
  (899 shorter events, 465.7 us)
Async XLA Ops:
  7.2 40.5 %all-gather.9.cloned.1.call-start = ((), (), s32[]{:S(2)}) async-start(), calls=%async_computation.6 | async-start | bytes 1566720 | tf_op jit(solution)/shard_map/all_gather | solution.py:406
  13.1 81.3 %all-gather.11.cloned.1.call-start = ((), (), s32[]{:S(2)}) async-start(), calls=%async_computation.7 | async-start | bytes 1566720 | tf_op jit(solution)/shard_map/all_gather | solution.py:406
  18.2 95.6 %all-gather.13.cloned.1.call-start = ((), (), s32[]{:S(2)}) async-start(), calls=%async_computation.8 | async-start | bytes 1566720 | tf_op jit(solution)/shard_map/all_gather | solution.py:406
  22.0 163.5 %all-gather.15.cloned.1.call-start = ((), (), s32[]{:S(2)}) async-start(), calls=%async_computation.9 | async-start | bytes 1566720 | tf_op jit(solution)/shard_map/all_gather | solution.py:406
  24.0 199.5 %all-gather.17.cloned.1.call-start = ((), (), s32[]{:S(2)}) async-start(), calls=%async_computation.10 | async-start | bytes 1566720 | tf_op jit(solution)/shard_map/all_gather | solution.py:406
  51.0 251.8 %all-gather.19.cloned.1.call-start = ((), (), s32[]{:S(2)}) async-start(), calls=%async_computation.11 | async-start | bytes 1566720 | tf_op jit(solution)/shard_map/all_gather | solution.py:406
  51.1 46.1 %collective-permute-start.1 = (bf16[4,136,1088]{2,1,0:T(8,128)(2,1)}, bf16[4,136,1088]{2,1,0:T(8,128)(2,1)}, u32[]{:S(2)}, u32[]{:S(2)}) collective-permute-start(bf16[4,136,1088]{2,1,0:T(8,128)(2,1)} %all-gather.9.cloned.1.call-done.refs_0_), channel_id=1, source_target_pairs={{0,16},{4,12},{8,24},{12,4},{16,0},{20,28},{24,8},{28,20},{1,17},{... | collective-permute-start | bytes 3551240 | tf_op jit(solution)/shard_map/ppermute | solution.py:349
  80.2 534.2 %reduce-scatter.19.cloned.1.call-start = ((), (), s32[]{:S(2)}) async-start(), calls=%async_computation.12 | async-start | bytes 1566720
  113.8 42.6 %collective-permute-start.9 = (bf16[4,136,1088]{2,1,0:T(8,128)(2,1)}, bf16[4,136,1088]{2,1,0:T(8,128)(2,1)S(1)}, u32[]{:S(2)}, u32[]{:S(2)}) collective-permute-start(bf16[4,136,1088]{2,1,0:T(8,128)(2,1)} %collective-permute-done.7.refs_1_), channel_id=1, source_target_pairs={{0,16},{4,12},{8,24},{12,4},{16,0},{20,28},{24,8},{28,20},{1,17},{... | collective-permute-start | bytes 3551240 | tf_op jit(solution)/shard_map/ppermute | solution.py:349
  115.1 41.2 %collective-permute-start.14 = (bf16[4,136,1088]{2,1,0:T(8,128)(2,1)}, bf16[4,136,1088]{2,1,0:T(8,128)(2,1)}, u32[]{:S(2)}, u32[]{:S(2)}) collective-permute-start(bf16[4,136,1088]{2,1,0:T(8,128)(2,1)} %all-gather.13.cloned.1.call-done.refs_0_), channel_id=1, source_target_pairs={{0,8},{4,20},{8,0},{12,28},{16,24},{20,4},{24,16},{28,12},{1,9},{5... | collective-permute-start | bytes 3551240 | tf_op jit(solution)/shard_map/ppermute | solution.py:349
  116.6 74.3 %collective-permute-start.10 = (bf16[4,136,1088]{2,1,0:T(8,128)(2,1)}, bf16[4,136,1088]{2,1,0:T(8,128)(2,1)}, u32[]{:S(2)}, u32[]{:S(2)}) collective-permute-start(bf16[4,136,1088]{2,1,0:T(8,128)(2,1)} %all-gather.11.cloned.1.call-done.refs_0_), channel_id=1, source_target_pairs={{0,4},{4,0},{8,12},{12,8},{16,20},{20,16},{24,28},{28,24},{1,5},{5... | collective-permute-start | bytes 3551240 | tf_op jit(solution)/shard_map/ppermute | solution.py:349
  116.7 75.7 %collective-permute-start.11 = (bf16[4,136,1088]{2,1,0:T(8,128)(2,1)}, bf16[4,136,1088]{2,1,0:T(8,128)(2,1)}, u32[]{:S(2)}, u32[]{:S(2)}) collective-permute-start(bf16[4,136,1088]{2,1,0:T(8,128)(2,1)} %collective-permute-done.7.refs_1_), channel_id=1, source_target_pairs={{0,4},{4,0},{8,12},{12,8},{16,20},{20,16},{24,28},{28,24},{1,5},{5... | collective-permute-start | bytes 3551240 | tf_op jit(solution)/shard_map/ppermute | solution.py:349
  156.4 54.0 %collective-permute-start.15 = (bf16[4,136,1088]{2,1,0:T(8,128)(2,1)S(1)}, bf16[4,136,1088]{2,1,0:T(8,128)(2,1)}, u32[]{:S(2)}, u32[]{:S(2)}) collective-permute-start(bf16[4,136,1088]{2,1,0:T(8,128)(2,1)S(1)} %copy-done.40), channel_id=1, source_target_pairs={{0,16},{4,12},{8,24},{12,4},{16,0},{20,28},{24,8},{28,20},{1,17},{... | collective-permute-start | bytes 3551240 | tf_op jit(solution)/shard_map/ppermute | solution.py:349
  194.8 86.3 %collective-permute-start.17 = (bf16[4,136,1088]{2,1,0:T(8,128)(2,1)S(1)}, bf16[4,136,1088]{2,1,0:T(8,128)(2,1)}, u32[]{:S(2)}, u32[]{:S(2)}) collective-permute-start(bf16[4,136,1088]{2,1,0:T(8,128)(2,1)S(1)} %copy-done.40), channel_id=1, source_target_pairs={{0,4},{4,0},{8,12},{12,8},{16,20},{20,16},{24,28},{28,24},{1,5},{5... | collective-permute-start | bytes 3551240 | tf_op jit(solution)/shard_map/ppermute | solution.py:349
  194.9 87.2 %collective-permute-start.18 = (bf16[4,136,1088]{2,1,0:T(8,128)(2,1)}, bf16[4,136,1088]{2,1,0:T(8,128)(2,1)}, u32[]{:S(2)}, u32[]{:S(2)}) collective-permute-start(bf16[4,136,1088]{2,1,0:T(8,128)(2,1)} %collective-permute-done.14.refs_1_), channel_id=1, source_target_pairs={{0,4},{4,0},{8,12},{12,8},{16,20},{20,16},{24,28},{28,24},{1,5},{5... | collective-permute-start | bytes 3551240 | tf_op jit(solution)/shard_map/ppermute | solution.py:349
  222.8 42.8 %collective-permute-start.23 = (bf16[4,136,1088]{2,1,0:T(8,128)(2,1)}, bf16[4,136,1088]{2,1,0:T(8,128)(2,1)}, u32[]{:S(2)}, u32[]{:S(2)}) collective-permute-start(bf16[4,136,1088]{2,1,0:T(8,128)(2,1)} %collective-permute-done.21.refs_1_), channel_id=1, source_target_pairs={{0,16},{4,12},{8,24},{12,4},{16,0},{20,28},{24,8},{28,20},{1,17},{... | collective-permute-start | bytes 3551240 | tf_op jit(solution)/shard_map/ppermute | solution.py:349
  223.4 57.1 %collective-permute-start.28 = (bf16[4,136,1088]{2,1,0:T(8,128)(2,1)}, bf16[4,136,1088]{2,1,0:T(8,128)(2,1)S(1)}, u32[]{:S(2)}, u32[]{:S(2)}) collective-permute-start(bf16[4,136,1088]{2,1,0:T(8,128)(2,1)} %all-gather.17.cloned.1.call-done.refs_0_), channel_id=1, source_target_pairs={{0,8},{4,20},{8,0},{12,28},{16,24},{20,4},{24,16},{28,12},{1,9},{5... | collective-permute-start | bytes 3551240 | tf_op jit(solution)/shard_map/ppermute | solution.py:349
  251.6 31.9 %collective-permute-start.19 = (bf16[4,136,1088]{2,1,0:T(8,128)(2,1)}, bf16[4,136,1088]{2,1,0:T(8,128)(2,1)S(1)}, u32[]{:S(2)}, u32[]{:S(2)}) collective-permute-start(bf16[4,136,1088]{2,1,0:T(8,128)(2,1)} %collective-permute-done.15.refs_2_), channel_id=1, source_target_pairs={{0,4},{4,0},{8,12},{12,8},{16,20},{20,16},{24,28},{28,24},{1,5},{5... | collective-permute-start | bytes 3551240 | tf_op jit(solution)/shard_map/ppermute | solution.py:349
  282.0 41.5 %collective-permute-start.29 = (bf16[4,136,1088]{2,1,0:T(8,128)(2,1)}, bf16[4,136,1088]{2,1,0:T(8,128)(2,1)}, u32[]{:S(2)}, u32[]{:S(2)}) collective-permute-start(bf16[4,136,1088]{2,1,0:T(8,128)(2,1)} %all-gather.17.cloned.1.call-done.refs_0_), channel_id=1, source_target_pairs={{0,16},{4,12},{8,24},{12,4},{16,0},{20,28},{24,8},{28,20},{1,17},{... | collective-permute-start | bytes 3551240 | tf_op jit(solution)/shard_map/ppermute | solution.py:349
  309.5 58.5 %collective-permute-start.31 = (bf16[4,136,1088]{2,1,0:T(8,128)(2,1)}, bf16[4,136,1088]{2,1,0:T(8,128)(2,1)S(1)}, u32[]{:S(2)}, u32[]{:S(2)}) collective-permute-start(bf16[4,136,1088]{2,1,0:T(8,128)(2,1)} %all-gather.17.cloned.1.call-done.refs_0_), channel_id=1, source_target_pairs={{0,4},{4,0},{8,12},{12,8},{16,20},{20,16},{24,28},{28,24},{1,5},{5... | collective-permute-start | bytes 3551240 | tf_op jit(solution)/shard_map/ppermute | solution.py:349
  309.6 58.6 %collective-permute-start.32 = (bf16[4,136,1088]{2,1,0:T(8,128)(2,1)S(1)}, bf16[4,136,1088]{2,1,0:T(8,128)(2,1)S(1)}, u32[]{:S(2)}, u32[]{:S(2)}) collective-permute-start(bf16[4,136,1088]{2,1,0:T(8,128)(2,1)S(1)} %copy-done.43), channel_id=1, source_target_pairs={{0,4},{4,0},{8,12},{12,8},{16,20},{20,16},{24,28},{28,24},{1,5},{5... | collective-permute-start | bytes 3551240 | tf_op jit(solution)/shard_map/ppermute | solution.py:349
  336.0 49.8 %collective-permute-start.36 = (bf16[4,136,1088]{2,1,0:T(8,128)(2,1)S(1)}, bf16[4,136,1088]{2,1,0:T(8,128)(2,1)}, u32[]{:S(2)}, u32[]{:S(2)}) collective-permute-start(bf16[4,136,1088]{2,1,0:T(8,128)(2,1)S(1)} %copy-done.39), channel_id=1, source_target_pairs={{0,16},{4,12},{8,24},{12,4},{16,0},{20,28},{24,8},{28,20},{1,17},{... | collective-permute-start | bytes 3551240 | tf_op jit(solution)/shard_map/ppermute | solution.py:349
  368.0 51.3 %collective-permute-start.38 = (bf16[4,136,1088]{2,1,0:T(8,128)(2,1)S(1)}, bf16[4,136,1088]{2,1,0:T(8,128)(2,1)}, u32[]{:S(2)}, u32[]{:S(2)}) collective-permute-start(bf16[4,136,1088]{2,1,0:T(8,128)(2,1)S(1)} %copy-done.39), channel_id=1, source_target_pairs={{0,4},{4,0},{8,12},{12,8},{16,20},{20,16},{24,28},{28,24},{1,5},{5... | collective-permute-start | bytes 3551240 | tf_op jit(solution)/shard_map/ppermute | solution.py:349
  370.8 48.5 %collective-permute-start.39 = (bf16[4,136,1088]{2,1,0:T(8,128)(2,1)}, bf16[4,136,1088]{2,1,0:T(8,128)(2,1)}, u32[]{:S(2)}, u32[]{:S(2)}) collective-permute-start(bf16[4,136,1088]{2,1,0:T(8,128)(2,1)} %collective-permute-done.35.refs_1_), channel_id=1, source_target_pairs={{0,4},{4,0},{8,12},{12,8},{16,20},{20,16},{24,28},{28,24},{1,5},{5... | collective-permute-start | bytes 3551240 | tf_op jit(solution)/shard_map/ppermute | solution.py:349
  385.7 33.6 %collective-permute-start.40 = (bf16[4,136,1088]{2,1,0:T(8,128)(2,1)}, bf16[4,136,1088]{2,1,0:T(8,128)(2,1)}, u32[]{:S(2)}, u32[]{:S(2)}) collective-permute-start(bf16[4,136,1088]{2,1,0:T(8,128)(2,1)} %collective-permute-done.36.refs_2_), channel_id=1, source_target_pairs={{0,4},{4,0},{8,12},{12,8},{16,20},{20,16},{24,28},{28,24},{1,5},{5... | collective-permute-start | bytes 3551240 | tf_op jit(solution)/shard_map/ppermute | solution.py:349
  413.8 56.3 %collective-permute-start.42 = (bf16[4,544,1088]{2,1,0:T(8,128)(2,1)}, bf16[4,544,1088]{2,1,0:T(8,128)(2,1)}, u32[]{:S(2)}, u32[]{:S(2)}) collective-permute-start(bf16[4,544,1088]{2,1,0:T(8,128)(2,1)} %shard_map.279), channel_id=1, source_target_pairs={{0,4},{4,0},{8,12},{12,8},{16,20},{20,16},{24,28},{28,24},{1,5},{5... | collective-permute-start | bytes 14204936 | tf_op jit(solution)/shard_map/ppermute | solution.py:349
  454.9 39.7 %collective-permute-start.44 = (bf16[4,544,1088]{2,1,0:T(8,128)(2,1)}, bf16[4,544,1088]{2,1,0:T(8,128)(2,1)}, u32[]{:S(2)}, u32[]{:S(2)}) collective-permute-start(bf16[4,544,1088]{2,1,0:T(8,128)(2,1)} %shard_map.282), channel_id=1, source_target_pairs={{0,4},{4,0},{8,12},{12,8},{16,20},{20,16},{24,28},{28,24},{1,5},{5... | collective-permute-start | bytes 14204936 | tf_op jit(solution)/shard_map/ppermute | solution.py:349
  499.6 49.6 %collective-permute-start.46 = (bf16[2,544,1088]{2,1,0:T(8,128)(2,1)}, bf16[2,544,1088]{2,1,0:T(8,128)(2,1)}, u32[]{:S(2)}, u32[]{:S(2)}) collective-permute-start(bf16[2,544,1088]{2,1,0:T(8,128)(2,1)} %shard_map.283), channel_id=1, source_target_pairs={{0,16},{4,12},{8,24},{12,4},{16,0},{20,28},{24,8},{28,20},{1,17},{... | collective-permute-start | bytes 7102472 | tf_op jit(solution)/shard_map/ppermute | solution.py:349
  545.5 88.0 %reduce-scatter.21.cloned.1.call-start = ((), (), s32[]{:S(2)}) async-start(), calls=%async_computation.13 | async-start | bytes 1566720
  552.3 33.5 %collective-permute-start.47 = (bf16[544,1088]{1,0:T(8,128)(2,1)}, bf16[544,1088]{1,0:T(8,128)(2,1)}, u32[]{:S(2)}, u32[]{:S(2)}) collective-permute-start(bf16[544,1088]{1,0:T(8,128)(2,1)} %fusion.42), channel_id=1, source_target_pairs={{0,8},{4,20},{8,0},{12,28},{16,24},{20,4},{24,16},{28,12},{1,9},{5... | collective-permute-start | bytes 3551240 | tf_op jit(solution)/shard_map/ppermute | solution.py:349
  605.5 62.6 %collective-permute-start.51 = (bf16[4,544,1088]{2,1,0:T(8,128)(2,1)}, bf16[4,544,1088]{2,1,0:T(8,128)(2,1)}, u32[]{:S(2)}, u32[]{:S(2)}) collective-permute-start(bf16[4,544,1088]{2,1,0:T(8,128)(2,1)} %shard_map.289), channel_id=1, source_target_pairs={{0,4},{4,0},{8,12},{12,8},{16,20},{20,16},{24,28},{28,24},{1,5},{5... | collective-permute-start | bytes 14204936 | tf_op jit(solution)/shard_map/ppermute | solution.py:349
  605.9 254.1 %reduce-scatter.23.cloned.1.call-start = ((), (), s32[]{:S(2)}) async-start(), calls=%async_computation.14 | async-start | bytes 1566720
  613.1 61.3 %collective-permute-start.50 = (bf16[2,544,1088]{2,1,0:T(8,128)(2,1)}, bf16[2,544,1088]{2,1,0:T(8,128)(2,1)}, u32[]{:S(2)}, u32[]{:S(2)}) collective-permute-start(bf16[2,544,1088]{2,1,0:T(8,128)(2,1)} %shard_map.287), channel_id=1, source_target_pairs={{0,16},{4,12},{8,24},{12,4},{16,0},{20,28},{24,8},{28,20},{1,17},{... | collective-permute-start | bytes 7102472 | tf_op jit(solution)/shard_map/ppermute | solution.py:349
  673.1 44.2 %collective-permute-start.55 = (bf16[2,544,1088]{2,1,0:T(8,128)(2,1)}, bf16[2,544,1088]{2,1,0:T(8,128)(2,1)}, u32[]{:S(2)}, u32[]{:S(2)}) collective-permute-start(bf16[2,544,1088]{2,1,0:T(8,128)(2,1)} %shard_map.290), channel_id=1, source_target_pairs={{0,16},{4,12},{8,24},{12,4},{16,0},{20,28},{24,8},{28,20},{1,17},{... | collective-permute-start | bytes 7102472 | tf_op jit(solution)/shard_map/ppermute | solution.py:349
  677.1 33.6 %collective-permute-start.54 = (bf16[544,1088]{1,0:T(8,128)(2,1)}, bf16[544,1088]{1,0:T(8,128)(2,1)}, u32[]{:S(2)}, u32[]{:S(2)}) collective-permute-start(bf16[544,1088]{1,0:T(8,128)(2,1)} %fusion.44), channel_id=1, source_target_pairs={{0,8},{4,20},{8,0},{12,28},{16,24},{20,4},{24,16},{28,12},{1,9},{5... | collective-permute-start | bytes 3551240 | tf_op jit(solution)/shard_map/ppermute | solution.py:349
  706.5 32.0 %collective-permute-start.56 = (bf16[4,544,1088]{2,1,0:T(8,128)(2,1)}, bf16[4,544,1088]{2,1,0:T(8,128)(2,1)S(1)}, u32[]{:S(2)}, u32[]{:S(2)}) collective-permute-start(bf16[4,544,1088]{2,1,0:T(8,128)(2,1)} %shard_map.292), channel_id=1, source_target_pairs={{0,4},{4,0},{8,12},{12,8},{16,20},{20,16},{24,28},{28,24},{1,5},{5... | collective-permute-start | bytes 14204936 | tf_op jit(solution)/shard_map/ppermute | solution.py:349
  720.0 31.3 %collective-permute-start.58 = (bf16[544,1088]{1,0:T(8,128)(2,1)}, bf16[544,1088]{1,0:T(8,128)(2,1)}, u32[]{:S(2)}, u32[]{:S(2)}) collective-permute-start(bf16[544,1088]{1,0:T(8,128)(2,1)} %fusion.46), channel_id=1, source_target_pairs={{0,8},{4,20},{8,0},{12,28},{16,24},{20,4},{24,16},{28,12},{1,9},{5... | collective-permute-start | bytes 3551240 | tf_op jit(solution)/shard_map/ppermute | solution.py:349
  790.1 85.2 %collective-permute-start.72 = (bf16[4,544,1088]{2,1,0:T(8,128)(2,1)}, bf16[4,544,1088]{2,1,0:T(8,128)(2,1)}, u32[]{:S(2)}, u32[]{:S(2)}) collective-permute-start(bf16[4,544,1088]{2,1,0:T(8,128)(2,1)} %shard_map.296), channel_id=1, source_target_pairs={{0,4},{4,0},{8,12},{12,8},{16,20},{20,16},{24,28},{28,24},{1,5},{5... | collective-permute-start | bytes 14204936 | tf_op jit(solution)/shard_map/ppermute | solution.py:349
  795.2 95.3 %reduce-scatter.29.cloned.1.call-start = ((), (), s32[]{:S(2)}) async-start(), calls=%async_computation.17 | async-start | bytes 1566720
  818.7 42.2 %collective-permute-start.59 = (bf16[2,544,1088]{2,1,0:T(8,128)(2,1)}, bf16[2,544,1088]{2,1,0:T(8,128)(2,1)}, u32[]{:S(2)}, u32[]{:S(2)}) collective-permute-start(bf16[2,544,1088]{2,1,0:T(8,128)(2,1)} %copy-done.38), channel_id=1, source_target_pairs={{0,16},{4,12},{8,24},{12,4},{16,0},{20,28},{24,8},{28,20},{1,17},{... | collective-permute-start | bytes 7102472 | tf_op jit(solution)/shard_map/ppermute | solution.py:349
  822.7 32.0 %collective-permute-start.89 = (bf16[4,136,1088]{2,1,0:T(8,128)(2,1)}, bf16[4,136,1088]{2,1,0:T(8,128)(2,1)}, u32[]{:S(2)}, u32[]{:S(2)}) collective-permute-start(bf16[4,136,1088]{2,1,0:T(8,128)(2,1)} %pad_maximum_fusion.10), channel_id=1, source_target_pairs={{0,4},{4,0},{8,12},{12,8},{16,20},{20,16},{24,28},{28,24},{1,5},{5... | collective-permute-start | bytes 3551240 | tf_op jit(solution)/shard_map/ppermute | solution.py:349
  854.7 112.4 %reduce-scatter.27.cloned.1.call-start = ((), (), s32[]{:S(2)}) async-start(), calls=%async_computation.16 | async-start | bytes 1566720
  872.6 69.3 %collective-permute-start.85 = (bf16[4,136,1088]{2,1,0:T(8,128)(2,1)}, bf16[4,136,1088]{2,1,0:T(8,128)(2,1)}, u32[]{:S(2)}, u32[]{:S(2)}) collective-permute-start(bf16[4,136,1088]{2,1,0:T(8,128)(2,1)} %pad_maximum_fusion.11), channel_id=1, source_target_pairs={{0,4},{4,0},{8,12},{12,8},{16,20},{20,16},{24,28},{28,24},{1,5},{5... | collective-permute-start | bytes 3551240 | tf_op jit(solution)/shard_map/ppermute | solution.py:349
  882.4 34.1 %collective-permute-start.73 = (bf16[2,544,1088]{2,1,0:T(8,128)(2,1)}, bf16[2,544,1088]{2,1,0:T(8,128)(2,1)}, u32[]{:S(2)}, u32[]{:S(2)}) collective-permute-start(bf16[2,544,1088]{2,1,0:T(8,128)(2,1)} %shard_map.297), channel_id=1, source_target_pairs={{0,16},{4,12},{8,24},{12,4},{16,0},{20,28},{24,8},{28,20},{1,17},{... | collective-permute-start | bytes 7102472 | tf_op jit(solution)/shard_map/ppermute | solution.py:349
  888.8 58.3 %collective-permute-start.80 = (bf16[4,136,1088]{2,1,0:T(8,128)(2,1)}, bf16[4,136,1088]{2,1,0:T(8,128)(2,1)}, u32[]{:S(2)}, u32[]{:S(2)}) collective-permute-start(bf16[4,136,1088]{2,1,0:T(8,128)(2,1)} %pad_maximum_fusion.13), channel_id=1, source_target_pairs={{0,4},{4,0},{8,12},{12,8},{16,20},{20,16},{24,28},{28,24},{1,5},{5... | collective-permute-start | bytes 3551240 | tf_op jit(solution)/shard_map/ppermute | solution.py:349
  890.5 38.0 %collective-permute-start.86 = (bf16[136,1088]{1,0:T(8,128)(2,1)}, bf16[136,1088]{1,0:T(8,128)(2,1)}, u32[]{:S(2)}, u32[]{:S(2)}) collective-permute-start(bf16[136,1088]{1,0:T(8,128)(2,1)} %bitcast.331), channel_id=1, source_target_pairs={{0,8},{4,20},{8,0},{12,28},{16,24},{20,4},{24,16},{28,12},{1,9},{5... | collective-permute-start | bytes 887816 | tf_op jit(solution)/shard_map/ppermute | solution.py:349
  895.2 75.3 %reduce-scatter.25.cloned.1.call-start = ((), (), s32[]{:S(2)}) async-start(), calls=%async_computation.15 | async-start | bytes 1566720
  959.5 35.1 %collective-permute-start.88 = (bf16[4,136,1088]{2,1,0:T(8,128)(2,1)}, bf16[4,136,1088]{2,1,0:T(8,128)(2,1)}, u32[]{:S(2)}, u32[]{:S(2)}) collective-permute-start(bf16[4,136,1088]{2,1,0:T(8,128)(2,1)} %pad_maximum_fusion.15), channel_id=1, source_target_pairs={{0,4},{4,0},{8,12},{12,8},{16,20},{20,16},{24,28},{28,24},{1,5},{5... | collective-permute-start | bytes 3551240 | tf_op jit(solution)/shard_map/ppermute | solution.py:349
  (270 other events, 3627.1 us)
Sparse Core Ops, SparseCore 0:
  13.2 34.3 all-gather.8
  49.8 30.9 all-gather.10
  82.9 30.8 all-gather.12
  115.2 30.5 all-gather.14
  147.9 30.7 all-gather.16
  180.1 30.7 all-gather.18
  545.7 27.4 reduce-scatter.18
  606.0 27.5 reduce-scatter.20
  795.3 28.7 reduce-scatter.22
  854.8 26.8 reduce-scatter.28
  895.3 26.8 reduce-scatter.26
  942.0 28.3 reduce-scatter.24

commit v5 on v4

--- a/solution.py
+++ b/solution.py
@@ -302,6 +302,7 @@
         jnp.einsum("te,de->td", piece, chunk, preferred_element_type=jnp.float32)
         for piece, chunk in zip(pieces, qkv_weight)
     )
+    grad_normed = pipe.advance(grad_normed)
     first_value, first_pull = jax.vjp(
         layer_norm, stream, norm1_gain.astype(jnp.float32), norm1_shift.astype(jnp.float32)
     )
@@ -751,7 +752,11 @@
                 pipe,
                 lambda name, group, l=l: sum_group(name, l, group),
             )
-            shares[l] = sum_vectors(layout, vectors)
+            shares[l] = vectors
+        joint = pipe.advance([vector for vectors in shares for vector in vectors])
+        joint = sum_vectors(layout, joint)
+        kinds = len(joint) // layer_count
+        shares = [joint[l * kinds : (l + 1) * kinds] for l in range(layer_count)]
         pipe.drain()
 
         def stacked(i):

time: 1020 us -> 1030 us (level)
  waiting for transfers between devices: 268 us -> 285 us
    ppermute x78, waiting for transfers between devices: 191 us -> 248 us  [move(): return lax.ppermute(value, 'replica', self.pairs(way))]
    ppermute x6 -> x3, waiting for transfers between devices: 20.3 us -> 0.01 us  [sum_vectors(): total = total + lax.ppermute(total, 'replica', pairs)]
    ppermute x6 -> x3, waiting for transfers between devices: 24.9 us -> 11.3 us  [sum_vectors(): total = lax.ppermute(total, 'shard', [(i, (i + 1) % n) for i in range(n)])]
    unnamed x436 -> x450, local copies, waits for them, and re-layouts: 50.2 us -> 52.1 us
  transfers between devices with their start and end apart: 102 -> 96, of which waited for: 36 -> 31; matrix products, arithmetic and copies ran while one was open for 35% -> 36% of each run, Pallas kernels for 20% -> 20%
where the time goes in v5:
time: 1030 us
  waiting for transfers between devices  285 us (28%)
  Pallas kernels  236 us (23%)
  local copies, waits for them, and re-layouts  140 us (14%)
  matrix products  139 us (13%)
  other arithmetic  138 us (13%)
  starting transfers between devices  58.6 us (6%)
  between operations  17.6 us (2%)
  blocking collectives  13.5 us (1%)
    ppermute x78, waiting for transfers between devices, move(): return lax.ppermute(value, 'replica', self.pairs(way))  248 us
    pallas_call x18, Pallas kernels, products(): pl.pallas_call(product_kernel, out_shape=jax.ShapeDtypeStruct((steps, hei...  78.7 us
    ppermute x78, starting transfers between devices, move(): return lax.ppermute(value, 'replica', self.pairs(way))  55 us
    unnamed x450, local copies, waits for them, and re-layouts  52.1 us
    pallas_call x2, Pallas kernels, attend_back(): pl.pallas_call(attend_back_kernel, out_shape=(shape, shape, shape), scrat...  51.3 us
    pallas_call x6, Pallas kernels, assemble(): pl.pallas_call(functools.partial(place_kernel, by_shard), out_shape=jax.S...  47.1 us
    pallas_call x2, Pallas kernels, attend(): pl.pallas_call(attend_kernel, out_shape=(jax.ShapeDtypeStruct((count, wid...  40.1 us
    dot_general x16, matrix products, dot_columns(): jnp.dot(rows, chunk, preferred_element_type=jnp.float32)  35.7 us
  transfers between devices with their start and end apart: 96, of which 31 were waited for; matrix products, arithmetic and copies ran while one was open for 36% of the time, Pallas kernels for 20%

profile of v5, /device:TPU:0, one launch (start us, length us, event | category | flops | bytes accessed | tf_op | source)
XLA Modules:
  0.0 1027.9 jit_solution(14547076683519139664)
XLA Ops:
  24.0 23.6 %all-gather.9.cloned.1.call-done.refs_0_ = bf16[4,136,1088]{2,1,0:T(8,128)(2,1)} async-done(((bf16[1,136,1088]{2,1,0:T(8,128)(2,1)}), bf16[4,136,1088]{2,1,0:T(8,128)(2,1)}) %all-gather.9.cloned.1.call-update) | async-done | bytes 1183760 | tf_op jit(solution)/shard_map/all_gather | solution.py:407
  52.6 24.3 %collective-permute-done.refs_1_ = bf16[4,136,1088]{2,1,0:T(8,128)(2,1)} collective-permute-done((bf16[4,136,1088]{2,1,0:T(8,128)(2,1)}, bf16[4,136,1088]{2,1,0:T(8,128)(2,1)}, u32[]{:S(2)}, u32[]{:S(2)}) %collective-permute-start) | collective-permute-done | bytes 1183776 | tf_op jit(solution)/shard_map/ppermute | solution.py:350
  80.6 13.5 %all-gather.1 = bf16[4,2,3264]{2,1,0:T(2,128)(2,1)S(1)} all-gather(bf16[1,2,3264]{2,1,0:T(2,128)(2,1)S(1)} %bitcast.364), channel_id=2, replica_groups=mesh['replica'=8,'shard'=4] {'shard'}, dimensions={0}, use_global_device_ids=true | all-gather | bytes 65280 | tf_op jit(solution)/shard_map/all_gather | solution.py:676
  117.2 8.7 shard_map.271
  126.0 5.8 fusion.109
  131.8 10.3 %collective-permute-done.8.refs_2_ = bf16[4,136,1088]{2,1,0:T(8,128)(2,1)} collective-permute-done((bf16[4,136,1088]{2,1,0:T(8,128)(2,1)}, bf16[4,136,1088]{2,1,0:T(8,128)(2,1)}, u32[]{:S(2)}, u32[]{:S(2)}) %collective-permute-start.8) | collective-permute-done | bytes 1183776 | tf_op jit(solution)/shard_map/ppermute | solution.py:350
  142.1 14.3 %collective-permute-done.9.refs_3_ = bf16[4,136,1088]{2,1,0:T(8,128)(2,1)S(1)} collective-permute-done((bf16[4,136,1088]{2,1,0:T(8,128)(2,1)}, bf16[4,136,1088]{2,1,0:T(8,128)(2,1)S(1)}, u32[]{:S(2)}, u32[]{:S(2)}) %collective-permute-start.9) | collective-permute-done | bytes 1183776 | tf_op jit(solution)/shard_map/ppermute | solution.py:350
  163.2 20.2 %shard_map.272 = (bf16[512,1088]{1,0:T(8,128)(2,1)S(1)}, f32[17,512,1]{2,1,0:T(8,128)}) custom-call(s32[512,1]{1,0:T(8,128)S(1)} %copy.186.starts_ref, bf16[512,1088]{1,0:T(8,128)(2,1)S(1)} %fusion.26.q_ref, bf16[512,1088]{1,0:T(8,128)(2,1)S(1)} %convolution_convert_fusion.3.k_ref, bf16[512,1088]{1,0:T(8,128)(2,1)S(1)} %fusion.27.v_ref), custom_call_target="tpu_custom_call" | custom-call | flops 1140850688 | bytes 4456448 | tf_op jit(solution)/shard_map/pallas_call | solution.py:109
  195.4 7.7 shard_map.273
  203.1 7.3 fusion.108
  210.4 11.0 %collective-permute-done.16.refs_3_ = bf16[4,136,1088]{2,1,0:T(8,128)(2,1)} collective-permute-done((bf16[4,136,1088]{2,1,0:T(8,128)(2,1)}, bf16[4,136,1088]{2,1,0:T(8,128)(2,1)}, u32[]{:S(2)}, u32[]{:S(2)}) %collective-permute-start.16) | collective-permute-done | bytes 1183776 | tf_op jit(solution)/shard_map/ppermute | solution.py:350
  233.6 18.0 %collective-permute-done.22.refs_2_ = bf16[4,136,1088]{2,1,0:T(8,128)(2,1)} collective-permute-done((bf16[4,136,1088]{2,1,0:T(8,128)(2,1)}, bf16[4,136,1088]{2,1,0:T(8,128)(2,1)}, u32[]{:S(2)}, u32[]{:S(2)}) %collective-permute-start.22) | collective-permute-done | bytes 1183776 | tf_op jit(solution)/shard_map/ppermute | solution.py:350
  251.6 14.0 %collective-permute-done.23.refs_3_ = bf16[4,136,1088]{2,1,0:T(8,128)(2,1)} collective-permute-done((bf16[4,136,1088]{2,1,0:T(8,128)(2,1)}, bf16[4,136,1088]{2,1,0:T(8,128)(2,1)}, u32[]{:S(2)}, u32[]{:S(2)}) %collective-permute-start.23) | collective-permute-done | bytes 1183776 | tf_op jit(solution)/shard_map/ppermute | solution.py:350
  265.6 14.9 %fusion.5 = (f32[512,4352]{0,1:T(8,128)}, bf16[512,4352]{0,1:T(8,128)(2,1)S(1)}) fusion(f32[512,1088]{0,1:T(8,128)S(1)} %fusion.122, f32[512,1088]{0,1:T(8,128)S(1)} %fusion.121, f32[512,1088]{0,1:T(8,128)S(1)} %fusion.120, f32[512,1088]{0,1:T(8,128)S(1)} %fusion.119, f32[4352]{0:T(1024)S(1)} %reshape.584), kind=kLoop, calls=%fused_computation.9 | loop fusion | flops 51249152 | bytes 22299648 | tf_op jit(solution)/shard_map/add | solution.py:30
  282.6 7.9 shard_map.274
  290.5 11.4 %fusion.117 = (f32[512]{0:T(512)S(1)}, f32[512,1088]{1,0:T(8,128)}) fusion(f32[1088]{0:T(1024)S(1)} %reshape.585, f32[512,1088]{1,0:T(8,128)S(1)} %copy-done.79, bf16[512,4352]{0,1:T(8,128)(2,1)S(1)} %get-tuple-element.85, bf16[4352,1088]{1,0:T(8,128)(2,1)} %bitcast.286), kind=kOutput, calls=%fused_computation.283 | convolution fusion | flops 4850286080 | bytes 18389248 | tf_op jit(solution)/shard_map/dot_general | solution.py:236
  309.4 7.7 shard_map.275
  317.2 5.7 fusion.107
  322.9 12.2 %collective-permute-done.30.refs_3_ = bf16[4,136,1088]{2,1,0:T(8,128)(2,1)S(1)} collective-permute-done((bf16[4,136,1088]{2,1,0:T(8,128)(2,1)}, bf16[4,136,1088]{2,1,0:T(8,128)(2,1)S(1)}, u32[]{:S(2)}, u32[]{:S(2)}) %collective-permute-start.30) | collective-permute-done | bytes 1183776 | tf_op jit(solution)/shard_map/ppermute | solution.py:350
  341.9 20.0 %shard_map.276 = (bf16[512,1088]{1,0:T(8,128)(2,1)S(1)}, f32[17,512,1]{2,1,0:T(8,128)}) custom-call(s32[512,1]{1,0:T(8,128)S(1)} %copy-done.51, bf16[512,1088]{1,0:T(8,128)(2,1)S(1)} %fusion.28.q_ref, bf16[512,1088]{1,0:T(8,128)(2,1)S(1)} %convolution_convert_fusion.2.k_ref, bf16[512,1088]{1,0:T(8,128)(2,1)S(1)} %fusion.29.v_ref), custom_call_target="tpu_custom_call" | custom-call | flops 1140850688 | bytes 4456448 | tf_op jit(solution)/shard_map/pallas_call | solution.py:109
  370.8 6.7 shard_map.277
  389.4 14.5 %fusion.11 = (f32[512,4352]{0,1:T(8,128)}, bf16[512,4352]{0,1:T(8,128)(2,1)S(1)}) fusion(f32[512,1088]{0,1:T(8,128)S(1)} %fusion.126, f32[512,1088]{0,1:T(8,128)S(1)} %fusion.125, f32[512,1088]{0,1:T(8,128)S(1)} %fusion.124, f32[512,1088]{0,1:T(8,128)S(1)} %fusion.123, f32[4352]{0:T(1024)S(1)} %copy-done.157), kind=kLoop, calls=%fused_computation.15 | loop fusion | flops 51249152 | bytes 22299648 | tf_op jit(solution)/shard_map/add | solution.py:30
  406.0 5.4 shard_map.279
  427.3 8.4 shard_map.278
  435.7 12.1 %multiply_convert_fusion.1 = bf16[512,4352]{0,1:T(8,128)(2,1)} fusion(f32[512,4352]{0,1:T(8,128)S(1)} %bitcast.293, bf16[4352,1088]{1,0:T(8,128)(2,1)} %bitcast.284, bf16[512,1088]{0,1:T(8,128)(2,1)S(1)} %copy-done.100), kind=kOutput, calls=%fused_computation.21 | convolution fusion | flops 4853071872 | bytes 23953408 | tf_op jit(solution)/shard_map/td,fd->tf/dot_general | solution.py:275
  447.8 6.6 copy.201
  456.8 5.4 shard_map.282
  496.8 12.2 %collective-permute-done.43 = bf16[2,544,1088]{2,1,0:T(8,128)(2,1)} collective-permute-done((bf16[2,544,1088]{2,1,0:T(8,128)(2,1)S(1)}, bf16[2,544,1088]{2,1,0:T(8,128)(2,1)}, u32[]{:S(2)}, u32[]{:S(2)}) %collective-permute-start.43) | collective-permute-done | bytes 2367520 | tf_op jit(solution)/shard_map/ppermute | solution.py:350
  513.0 5.2 shard_map.283
  525.8 9.2 collective-permute-done.45
  541.6 25.7 %shard_map.285 = (bf16[512,1088]{1,0:T(8,128)(2,1)S(1)}, bf16[512,1088]{1,0:T(8,128)(2,1)S(1)}, bf16[512,1088]{1,0:T(8,128)(2,1)S(1)}) custom-call(s32[512,1]{1,0:T(8,128)S(1)} %copy-done.52, bf16[512,1088]{1,0:T(8,128)(2,1)S(1)} %copy-done.71, bf16[512,1088]{1,0:T(8,128)(2,1)S(1)} %copy-done.69, bf16[512,1088]{1,0:T(8,128)(2,1)} %copy-done.72, ...), custom_call_target="tpu_custom_call" | custom-call | flops 2852126720 | bytes 7798784 | tf_op jit(solution)/shard_map/pallas_call | solution.py:168
  569.0 5.4 shard_map.286
  577.4 15.8 %collective-permute-done.47 = bf16[544,1088]{1,0:T(8,128)(2,1)S(1)} collective-permute-done((bf16[544,1088]{1,0:T(8,128)(2,1)S(1)}, bf16[544,1088]{1,0:T(8,128)(2,1)S(1)}, u32[]{:S(2)}, u32[]{:S(2)}) %collective-permute-start.47) | collective-permute-done | bytes 1183776 | tf_op jit(solution)/shard_map/ppermute | solution.py:350
  616.9 6.8 fusion.19
  644.6 5.5 shard_map.289
  652.1 12.0 %collective-permute-done.50 = bf16[2,544,1088]{2,1,0:T(8,128)(2,1)} collective-permute-done((bf16[2,544,1088]{2,1,0:T(8,128)(2,1)S(1)}, bf16[2,544,1088]{2,1,0:T(8,128)(2,1)}, u32[]{:S(2)}, u32[]{:S(2)}) %collective-permute-start.50) | collective-permute-done | bytes 2367520 | tf_op jit(solution)/shard_map/ppermute | solution.py:350
  687.2 12.8 %multiply_convert_fusion = bf16[512,4352]{0,1:T(8,128)(2,1)} fusion(f32[512,4352]{0,1:T(8,128)} %get-tuple-element.113, bf16[512,1088]{1,0:T(8,128)(2,1)S(1)} %copy-done.10, bf16[4352,1088]{1,0:T(8,128)(2,1)} %bitcast.287), kind=kOutput, calls=%fused_computation.20 | convolution fusion | flops 4853071872 | bytes 23953408 | tf_op jit(solution)/shard_map/td,fd->tf/dot_general | solution.py:275
  700.0 6.5 copy.219
  710.2 5.4 shard_map.292
  740.7 9.3 collective-permute-done.56
  759.7 9.0 collective-permute-done.59
  787.0 25.7 %shard_map.295 = (bf16[512,1088]{1,0:T(8,128)(2,1)S(1)}, bf16[512,1088]{1,0:T(8,128)(2,1)S(1)}, bf16[512,1088]{1,0:T(8,128)(2,1)S(1)}) custom-call(s32[512,1]{1,0:T(8,128)S(1)} %copy-done.53, bf16[512,1088]{1,0:T(8,128)(2,1)S(1)} %copy-done.66, bf16[512,1088]{1,0:T(8,128)(2,1)S(1)} %copy-done.64, bf16[512,1088]{1,0:T(8,128)(2,1)} %copy-done.67, ...), custom_call_target="tpu_custom_call" | custom-call | flops 2852126720 | bytes 7798784 | tf_op jit(solution)/shard_map/pallas_call | solution.py:168
  814.5 5.4 shard_map.296
  824.4 12.3 %fusion.30 = bf16[512,1088]{1,0:T(8,128)(2,1)} fusion(f32[512,1088]{1,0:T(8,128)} %copy-done.76, bf16[512,4352]{0,1:T(8,128)(2,1)} %copy-done.89, bf16[4352,1088]{1,0:T(8,128)(2,1)} %bitcast.285, f32[1088]{0:T(1024)S(1)} %reshape.594), kind=kOutput, calls=%fused_computation.66 | convolution fusion | flops 4850286592 | bytes 17273088 | tf_op jit(solution)/shard_map/dot_general | solution.py:236
  843.7 9.0 collective-permute-done.58
  885.9 38.3 %collective-permute-done.81 = bf16[2,136,1088]{2,1,0:T(8,128)(2,1)S(1)} collective-permute-done((bf16[2,136,1088]{2,1,0:T(8,128)(2,1)S(1)}, bf16[2,136,1088]{2,1,0:T(8,128)(2,1)S(1)}, u32[]{:S(2)}, u32[]{:S(2)}) %collective-permute-start.81) | collective-permute-done | bytes 591904 | tf_op jit(solution)/shard_map/ppermute | solution.py:350
  944.8 8.9 collective-permute-done.72
  978.5 6.4 collective-permute-done.68
  (890 shorter events, 446.1 us)
Async XLA Ops:
  7.2 40.5 %all-gather.9.cloned.1.call-start = ((), (), s32[]{:S(2)}) async-start(), calls=%async_computation.6 | async-start | bytes 1566720 | tf_op jit(solution)/shard_map/all_gather | solution.py:407
  13.1 81.3 %all-gather.11.cloned.1.call-start = ((), (), s32[]{:S(2)}) async-start(), calls=%async_computation.7 | async-start | bytes 1566720 | tf_op jit(solution)/shard_map/all_gather | solution.py:407
  18.2 95.6 %all-gather.13.cloned.1.call-start = ((), (), s32[]{:S(2)}) async-start(), calls=%async_computation.8 | async-start | bytes 1566720 | tf_op jit(solution)/shard_map/all_gather | solution.py:407
  22.0 163.5 %all-gather.15.cloned.1.call-start = ((), (), s32[]{:S(2)}) async-start(), calls=%async_computation.9 | async-start | bytes 1566720 | tf_op jit(solution)/shard_map/all_gather | solution.py:407
  24.0 199.5 %all-gather.17.cloned.1.call-start = ((), (), s32[]{:S(2)}) async-start(), calls=%async_computation.10 | async-start | bytes 1566720 | tf_op jit(solution)/shard_map/all_gather | solution.py:407
  51.0 250.9 %all-gather.19.cloned.1.call-start = ((), (), s32[]{:S(2)}) async-start(), calls=%async_computation.11 | async-start | bytes 1566720 | tf_op jit(solution)/shard_map/all_gather | solution.py:407
  51.1 46.1 %collective-permute-start.1 = (bf16[4,136,1088]{2,1,0:T(8,128)(2,1)}, bf16[4,136,1088]{2,1,0:T(8,128)(2,1)}, u32[]{:S(2)}, u32[]{:S(2)}) collective-permute-start(bf16[4,136,1088]{2,1,0:T(8,128)(2,1)} %all-gather.9.cloned.1.call-done.refs_0_), channel_id=1, source_target_pairs={{0,16},{4,12},{8,24},{12,4},{16,0},{20,28},{24,8},{28,20},{1,17},{... | collective-permute-start | bytes 3551240 | tf_op jit(solution)/shard_map/ppermute | solution.py:350
  80.2 535.5 %reduce-scatter.19.cloned.1.call-start = ((), (), s32[]{:S(2)}) async-start(), calls=%async_computation.12 | async-start | bytes 1566720
  113.8 42.6 %collective-permute-start.9 = (bf16[4,136,1088]{2,1,0:T(8,128)(2,1)}, bf16[4,136,1088]{2,1,0:T(8,128)(2,1)S(1)}, u32[]{:S(2)}, u32[]{:S(2)}) collective-permute-start(bf16[4,136,1088]{2,1,0:T(8,128)(2,1)} %collective-permute-done.7.refs_1_), channel_id=1, source_target_pairs={{0,16},{4,12},{8,24},{12,4},{16,0},{20,28},{24,8},{28,20},{1,17},{... | collective-permute-start | bytes 3551240 | tf_op jit(solution)/shard_map/ppermute | solution.py:350
  115.1 41.2 %collective-permute-start.14 = (bf16[4,136,1088]{2,1,0:T(8,128)(2,1)}, bf16[4,136,1088]{2,1,0:T(8,128)(2,1)}, u32[]{:S(2)}, u32[]{:S(2)}) collective-permute-start(bf16[4,136,1088]{2,1,0:T(8,128)(2,1)} %all-gather.13.cloned.1.call-done.refs_0_), channel_id=1, source_target_pairs={{0,8},{4,20},{8,0},{12,28},{16,24},{20,4},{24,16},{28,12},{1,9},{5... | collective-permute-start | bytes 3551240 | tf_op jit(solution)/shard_map/ppermute | solution.py:350
  116.6 74.3 %collective-permute-start.10 = (bf16[4,136,1088]{2,1,0:T(8,128)(2,1)}, bf16[4,136,1088]{2,1,0:T(8,128)(2,1)}, u32[]{:S(2)}, u32[]{:S(2)}) collective-permute-start(bf16[4,136,1088]{2,1,0:T(8,128)(2,1)} %all-gather.11.cloned.1.call-done.refs_0_), channel_id=1, source_target_pairs={{0,4},{4,0},{8,12},{12,8},{16,20},{20,16},{24,28},{28,24},{1,5},{5... | collective-permute-start | bytes 3551240 | tf_op jit(solution)/shard_map/ppermute | solution.py:350
  116.7 75.8 %collective-permute-start.11 = (bf16[4,136,1088]{2,1,0:T(8,128)(2,1)}, bf16[4,136,1088]{2,1,0:T(8,128)(2,1)}, u32[]{:S(2)}, u32[]{:S(2)}) collective-permute-start(bf16[4,136,1088]{2,1,0:T(8,128)(2,1)} %collective-permute-done.7.refs_1_), channel_id=1, source_target_pairs={{0,4},{4,0},{8,12},{12,8},{16,20},{20,16},{24,28},{28,24},{1,5},{5... | collective-permute-start | bytes 3551240 | tf_op jit(solution)/shard_map/ppermute | solution.py:350
  156.4 54.0 %collective-permute-start.15 = (bf16[4,136,1088]{2,1,0:T(8,128)(2,1)S(1)}, bf16[4,136,1088]{2,1,0:T(8,128)(2,1)}, u32[]{:S(2)}, u32[]{:S(2)}) collective-permute-start(bf16[4,136,1088]{2,1,0:T(8,128)(2,1)S(1)} %copy-done.38), channel_id=1, source_target_pairs={{0,16},{4,12},{8,24},{12,4},{16,0},{20,28},{24,8},{28,20},{1,17},{... | collective-permute-start | bytes 3551240 | tf_op jit(solution)/shard_map/ppermute | solution.py:350
  190.9 30.5 %collective-permute-start.16 = (bf16[4,136,1088]{2,1,0:T(8,128)(2,1)}, bf16[4,136,1088]{2,1,0:T(8,128)(2,1)}, u32[]{:S(2)}, u32[]{:S(2)}) collective-permute-start(bf16[4,136,1088]{2,1,0:T(8,128)(2,1)} %collective-permute-done.14.refs_1_), channel_id=1, source_target_pairs={{0,16},{4,12},{8,24},{12,4},{16,0},{20,28},{24,8},{28,20},{1,17},{... | collective-permute-start | bytes 3551240 | tf_op jit(solution)/shard_map/ppermute | solution.py:350
  194.8 86.3 %collective-permute-start.17 = (bf16[4,136,1088]{2,1,0:T(8,128)(2,1)S(1)}, bf16[4,136,1088]{2,1,0:T(8,128)(2,1)}, u32[]{:S(2)}, u32[]{:S(2)}) collective-permute-start(bf16[4,136,1088]{2,1,0:T(8,128)(2,1)S(1)} %copy-done.38), channel_id=1, source_target_pairs={{0,4},{4,0},{8,12},{12,8},{16,20},{20,16},{24,28},{28,24},{1,5},{5... | collective-permute-start | bytes 3551240 | tf_op jit(solution)/shard_map/ppermute | solution.py:350
  194.9 86.3 %collective-permute-start.18 = (bf16[4,136,1088]{2,1,0:T(8,128)(2,1)}, bf16[4,136,1088]{2,1,0:T(8,128)(2,1)}, u32[]{:S(2)}, u32[]{:S(2)}) collective-permute-start(bf16[4,136,1088]{2,1,0:T(8,128)(2,1)} %collective-permute-done.14.refs_1_), channel_id=1, source_target_pairs={{0,4},{4,0},{8,12},{12,8},{16,20},{20,16},{24,28},{28,24},{1,5},{5... | collective-permute-start | bytes 3551240 | tf_op jit(solution)/shard_map/ppermute | solution.py:350
  221.4 30.2 %collective-permute-start.22 = (bf16[4,136,1088]{2,1,0:T(8,128)(2,1)}, bf16[4,136,1088]{2,1,0:T(8,128)(2,1)}, u32[]{:S(2)}, u32[]{:S(2)}) collective-permute-start(bf16[4,136,1088]{2,1,0:T(8,128)(2,1)} %all-gather.15.cloned.1.call-done.refs_0_), channel_id=1, source_target_pairs={{0,16},{4,12},{8,24},{12,4},{16,0},{20,28},{24,8},{28,20},{1,17},{... | collective-permute-start | bytes 3551240 | tf_op jit(solution)/shard_map/ppermute | solution.py:350
  222.8 42.8 %collective-permute-start.23 = (bf16[4,136,1088]{2,1,0:T(8,128)(2,1)}, bf16[4,136,1088]{2,1,0:T(8,128)(2,1)}, u32[]{:S(2)}, u32[]{:S(2)}) collective-permute-start(bf16[4,136,1088]{2,1,0:T(8,128)(2,1)} %collective-permute-done.21.refs_1_), channel_id=1, source_target_pairs={{0,16},{4,12},{8,24},{12,4},{16,0},{20,28},{24,8},{28,20},{1,17},{... | collective-permute-start | bytes 3551240 | tf_op jit(solution)/shard_map/ppermute | solution.py:350
  223.4 57.1 %collective-permute-start.28 = (bf16[4,136,1088]{2,1,0:T(8,128)(2,1)}, bf16[4,136,1088]{2,1,0:T(8,128)(2,1)}, u32[]{:S(2)}, u32[]{:S(2)}) collective-permute-start(bf16[4,136,1088]{2,1,0:T(8,128)(2,1)} %all-gather.17.cloned.1.call-done.refs_0_), channel_id=1, source_target_pairs={{0,8},{4,20},{8,0},{12,28},{16,24},{20,4},{24,16},{28,12},{1,9},{5... | collective-permute-start | bytes 3551240 | tf_op jit(solution)/shard_map/ppermute | solution.py:350
  251.6 31.0 %collective-permute-start.19 = (bf16[4,136,1088]{2,1,0:T(8,128)(2,1)}, bf16[4,136,1088]{2,1,0:T(8,128)(2,1)S(1)}, u32[]{:S(2)}, u32[]{:S(2)}) collective-permute-start(bf16[4,136,1088]{2,1,0:T(8,128)(2,1)} %collective-permute-done.15.refs_2_), channel_id=1, source_target_pairs={{0,4},{4,0},{8,12},{12,8},{16,20},{20,16},{24,28},{28,24},{1,5},{5... | collective-permute-start | bytes 3551240 | tf_op jit(solution)/shard_map/ppermute | solution.py:350
  281.2 41.7 %collective-permute-start.29 = (bf16[4,136,1088]{2,1,0:T(8,128)(2,1)}, bf16[4,136,1088]{2,1,0:T(8,128)(2,1)}, u32[]{:S(2)}, u32[]{:S(2)}) collective-permute-start(bf16[4,136,1088]{2,1,0:T(8,128)(2,1)} %all-gather.17.cloned.1.call-done.refs_0_), channel_id=1, source_target_pairs={{0,16},{4,12},{8,24},{12,4},{16,0},{20,28},{24,8},{28,20},{1,17},{... | collective-permute-start | bytes 3551240 | tf_op jit(solution)/shard_map/ppermute | solution.py:350
  304.6 30.5 %collective-permute-start.30 = (bf16[4,136,1088]{2,1,0:T(8,128)(2,1)}, bf16[4,136,1088]{2,1,0:T(8,128)(2,1)S(1)}, u32[]{:S(2)}, u32[]{:S(2)}) collective-permute-start(bf16[4,136,1088]{2,1,0:T(8,128)(2,1)} %collective-permute-done.28.refs_1_), channel_id=1, source_target_pairs={{0,16},{4,12},{8,24},{12,4},{16,0},{20,28},{24,8},{28,20},{1,17},{... | collective-permute-start | bytes 3551240 | tf_op jit(solution)/shard_map/ppermute | solution.py:350
  308.8 58.7 %collective-permute-start.31 = (bf16[4,136,1088]{2,1,0:T(8,128)(2,1)}, bf16[4,136,1088]{2,1,0:T(8,128)(2,1)S(1)}, u32[]{:S(2)}, u32[]{:S(2)}) collective-permute-start(bf16[4,136,1088]{2,1,0:T(8,128)(2,1)} %all-gather.17.cloned.1.call-done.refs_0_), channel_id=1, source_target_pairs={{0,4},{4,0},{8,12},{12,8},{16,20},{20,16},{24,28},{28,24},{1,5},{5... | collective-permute-start | bytes 3551240 | tf_op jit(solution)/shard_map/ppermute | solution.py:350
  308.9 59.7 %collective-permute-start.32 = (bf16[4,136,1088]{2,1,0:T(8,128)(2,1)}, bf16[4,136,1088]{2,1,0:T(8,128)(2,1)S(1)}, u32[]{:S(2)}, u32[]{:S(2)}) collective-permute-start(bf16[4,136,1088]{2,1,0:T(8,128)(2,1)} %collective-permute-done.28.refs_1_), channel_id=1, source_target_pairs={{0,4},{4,0},{8,12},{12,8},{16,20},{20,16},{24,28},{28,24},{1,5},{5... | collective-permute-start | bytes 3551240 | tf_op jit(solution)/shard_map/ppermute | solution.py:350
  335.1 77.0 %collective-permute-start.36 = (bf16[4,136,1088]{2,1,0:T(8,128)(2,1)S(1)}, bf16[4,136,1088]{2,1,0:T(8,128)(2,1)}, u32[]{:S(2)}, u32[]{:S(2)}) collective-permute-start(bf16[4,136,1088]{2,1,0:T(8,128)(2,1)S(1)} %copy-done.37), channel_id=1, source_target_pairs={{0,16},{4,12},{8,24},{12,4},{16,0},{20,28},{24,8},{28,20},{1,17},{... | collective-permute-start | bytes 3551240 | tf_op jit(solution)/shard_map/ppermute | solution.py:350
  367.5 45.0 %collective-permute-start.37 = (bf16[4,136,1088]{2,1,0:T(8,128)(2,1)}, bf16[4,136,1088]{2,1,0:T(8,128)(2,1)}, u32[]{:S(2)}, u32[]{:S(2)}) collective-permute-start(bf16[4,136,1088]{2,1,0:T(8,128)(2,1)} %collective-permute-done.35.refs_1_), channel_id=1, source_target_pairs={{0,16},{4,12},{8,24},{12,4},{16,0},{20,28},{24,8},{28,20},{1,17},{... | collective-permute-start | bytes 3551240 | tf_op jit(solution)/shard_map/ppermute | solution.py:350
  411.4 60.3 %collective-permute-start.42 = (bf16[4,544,1088]{2,1,0:T(8,128)(2,1)}, bf16[4,544,1088]{2,1,0:T(8,128)(2,1)}, u32[]{:S(2)}, u32[]{:S(2)}) collective-permute-start(bf16[4,544,1088]{2,1,0:T(8,128)(2,1)} %shard_map.279), channel_id=1, source_target_pairs={{0,4},{4,0},{8,12},{12,8},{16,20},{20,16},{24,28},{28,24},{1,5},{5... | collective-permute-start | bytes 14204936 | tf_op jit(solution)/shard_map/ppermute | solution.py:350
  462.2 50.6 %collective-permute-start.44 = (bf16[4,544,1088]{2,1,0:T(8,128)(2,1)}, bf16[4,544,1088]{2,1,0:T(8,128)(2,1)}, u32[]{:S(2)}, u32[]{:S(2)}) collective-permute-start(bf16[4,544,1088]{2,1,0:T(8,128)(2,1)} %shard_map.282), channel_id=1, source_target_pairs={{0,4},{4,0},{8,12},{12,8},{16,20},{20,16},{24,28},{28,24},{1,5},{5... | collective-permute-start | bytes 14204936 | tf_op jit(solution)/shard_map/ppermute | solution.py:350
  478.4 30.6 %collective-permute-start.43 = (bf16[2,544,1088]{2,1,0:T(8,128)(2,1)S(1)}, bf16[2,544,1088]{2,1,0:T(8,128)(2,1)}, u32[]{:S(2)}, u32[]{:S(2)}) collective-permute-start(bf16[2,544,1088]{2,1,0:T(8,128)(2,1)S(1)} %shard_map.280), channel_id=1, source_target_pairs={{0,16},{4,12},{8,24},{12,4},{16,0},{20,28},{24,8},{28,20},{1,17},{... | collective-permute-start | bytes 7102472 | tf_op jit(solution)/shard_map/ppermute | solution.py:350
  518.1 56.3 %collective-permute-start.46 = (bf16[2,544,1088]{2,1,0:T(8,128)(2,1)}, bf16[2,544,1088]{2,1,0:T(8,128)(2,1)}, u32[]{:S(2)}, u32[]{:S(2)}) collective-permute-start(bf16[2,544,1088]{2,1,0:T(8,128)(2,1)} %shard_map.283), channel_id=1, source_target_pairs={{0,16},{4,12},{8,24},{12,4},{16,0},{20,28},{24,8},{28,20},{1,17},{... | collective-permute-start | bytes 7102472 | tf_op jit(solution)/shard_map/ppermute | solution.py:350
  537.9 87.2 %reduce-scatter.21.cloned.1.call-start = ((), (), s32[]{:S(2)}) async-start(), calls=%async_computation.13 | async-start | bytes 1566720
  574.4 52.0 %collective-permute-start.48 = (bf16[4,544,1088]{2,1,0:T(8,128)(2,1)}, bf16[4,544,1088]{2,1,0:T(8,128)(2,1)}, u32[]{:S(2)}, u32[]{:S(2)}) collective-permute-start(bf16[4,544,1088]{2,1,0:T(8,128)(2,1)} %shard_map.286), channel_id=1, source_target_pairs={{0,4},{4,0},{8,12},{12,8},{16,20},{20,16},{24,28},{28,24},{1,5},{5... | collective-permute-start | bytes 14204936 | tf_op jit(solution)/shard_map/ppermute | solution.py:350
  596.0 188.4 %reduce-scatter.23.cloned.1.call-start = ((), (), s32[]{:S(2)}) async-start(), calls=%async_computation.14 | async-start | bytes 1566720
  624.6 49.9 %collective-permute-start.51 = (bf16[2,136,1088]{2,1,0:T(8,128)(2,1)}, bf16[2,136,1088]{2,1,0:T(8,128)(2,1)}, u32[]{:S(2)}, u32[]{:S(2)}) collective-permute-start(bf16[2,136,1088]{2,1,0:T(8,128)(2,1)} %pad_maximum_fusion.16), channel_id=1, source_target_pairs={{0,16},{4,12},{8,24},{12,4},{16,0},{20,28},{24,8},{28,20},{1,17},{... | collective-permute-start | bytes 1775624 | tf_op jit(solution)/shard_map/ppermute | solution.py:350
  632.5 31.6 %collective-permute-start.50 = (bf16[2,544,1088]{2,1,0:T(8,128)(2,1)S(1)}, bf16[2,544,1088]{2,1,0:T(8,128)(2,1)}, u32[]{:S(2)}, u32[]{:S(2)}) collective-permute-start(bf16[2,544,1088]{2,1,0:T(8,128)(2,1)S(1)} %shard_map.287), channel_id=1, source_target_pairs={{0,16},{4,12},{8,24},{12,4},{16,0},{20,28},{24,8},{28,20},{1,17},{... | collective-permute-start | bytes 7102472 | tf_op jit(solution)/shard_map/ppermute | solution.py:350
  650.1 65.5 %collective-permute-start.54 = (bf16[4,544,1088]{2,1,0:T(8,128)(2,1)}, bf16[4,544,1088]{2,1,0:T(8,128)(2,1)}, u32[]{:S(2)}, u32[]{:S(2)}) collective-permute-start(bf16[4,544,1088]{2,1,0:T(8,128)(2,1)} %shard_map.289), channel_id=1, source_target_pairs={{0,4},{4,0},{8,12},{12,8},{16,20},{20,16},{24,28},{28,24},{1,5},{5... | collective-permute-start | bytes 14204936 | tf_op jit(solution)/shard_map/ppermute | solution.py:350
  706.5 158.4 %reduce-scatter.25.cloned.1.call-start = ((), (), s32[]{:S(2)}) async-start(), calls=%async_computation.15 | async-start | bytes 1566720
  715.5 56.0 %collective-permute-start.57 = (bf16[4,544,1088]{2,1,0:T(8,128)(2,1)}, bf16[4,544,1088]{2,1,0:T(8,128)(2,1)S(1)}, u32[]{:S(2)}, u32[]{:S(2)}) collective-permute-start(bf16[4,544,1088]{2,1,0:T(8,128)(2,1)} %shard_map.292), channel_id=1, source_target_pairs={{0,4},{4,0},{8,12},{12,8},{16,20},{20,16},{24,28},{28,24},{1,5},{5... | collective-permute-start | bytes 14204936 | tf_op jit(solution)/shard_map/ppermute | solution.py:350
  719.4 30.6 %collective-permute-start.56 = (bf16[2,544,1088]{2,1,0:T(8,128)(2,1)S(1)}, bf16[2,544,1088]{2,1,0:T(8,128)(2,1)}, u32[]{:S(2)}, u32[]{:S(2)}) collective-permute-start(bf16[2,544,1088]{2,1,0:T(8,128)(2,1)S(1)} %shard_map.290), channel_id=1, source_target_pairs={{0,16},{4,12},{8,24},{12,4},{16,0},{20,28},{24,8},{28,20},{1,17},{... | collective-permute-start | bytes 7102472 | tf_op jit(solution)/shard_map/ppermute | solution.py:350
  819.9 46.3 %collective-permute-start.63 = (bf16[4,544,1088]{2,1,0:T(8,128)(2,1)}, bf16[4,544,1088]{2,1,0:T(8,128)(2,1)}, u32[]{:S(2)}, u32[]{:S(2)}) collective-permute-start(bf16[4,544,1088]{2,1,0:T(8,128)(2,1)} %shard_map.296), channel_id=1, source_target_pairs={{0,4},{4,0},{8,12},{12,8},{16,20},{20,16},{24,28},{28,24},{1,5},{5... | collective-permute-start | bytes 14204936 | tf_op jit(solution)/shard_map/ppermute | solution.py:350
  822.2 31.2 %collective-permute-start.83 = (bf16[4,136,1088]{2,1,0:T(8,128)(2,1)}, bf16[4,136,1088]{2,1,0:T(8,128)(2,1)}, u32[]{:S(2)}, u32[]{:S(2)}) collective-permute-start(bf16[4,136,1088]{2,1,0:T(8,128)(2,1)} %pad_maximum_fusion.10), channel_id=1, source_target_pairs={{0,4},{4,0},{8,12},{12,8},{16,20},{20,16},{24,28},{28,24},{1,5},{5... | collective-permute-start | bytes 3551240 | tf_op jit(solution)/shard_map/ppermute | solution.py:350
  822.8 137.4 %reduce-scatter.27.cloned.1.call-start = ((), (), s32[]{:S(2)}) async-start(), calls=%async_computation.16 | async-start | bytes 1566720
  822.9 51.7 %collective-permute-start.60 = (bf16[2,544,1088]{2,1,0:T(8,128)(2,1)}, bf16[2,544,1088]{2,1,0:T(8,128)(2,1)}, u32[]{:S(2)}, u32[]{:S(2)}) collective-permute-start(bf16[2,544,1088]{2,1,0:T(8,128)(2,1)} %copy-done.36), channel_id=1, source_target_pairs={{0,16},{4,12},{8,24},{12,4},{16,0},{20,28},{24,8},{28,20},{1,17},{... | collective-permute-start | bytes 7102472 | tf_op jit(solution)/shard_map/ppermute | solution.py:350
  873.5 61.3 %collective-permute-start.65 = (bf16[2,544,1088]{2,1,0:T(8,128)(2,1)}, bf16[2,544,1088]{2,1,0:T(8,128)(2,1)}, u32[]{:S(2)}, u32[]{:S(2)}) collective-permute-start(bf16[2,544,1088]{2,1,0:T(8,128)(2,1)} %shard_map.297), channel_id=1, source_target_pairs={{0,16},{4,12},{8,24},{12,4},{16,0},{20,28},{24,8},{28,20},{1,17},{... | collective-permute-start | bytes 7102472 | tf_op jit(solution)/shard_map/ppermute | solution.py:350
  876.2 49.3 %collective-permute-start.62 = (bf16[544,1088]{1,0:T(8,128)(2,1)S(1)}, bf16[544,1088]{1,0:T(8,128)(2,1)S(1)}, u32[]{:S(2)}, u32[]{:S(2)}) collective-permute-start(bf16[544,1088]{1,0:T(8,128)(2,1)S(1)} %fusion.47), channel_id=1, source_target_pairs={{0,8},{4,20},{8,0},{12,28},{16,24},{20,4},{24,16},{28,12},{1,9},{5... | collective-permute-start | bytes 3551240 | tf_op jit(solution)/shard_map/ppermute | solution.py:350
  877.6 46.7 %collective-permute-start.81 = (bf16[2,136,1088]{2,1,0:T(8,128)(2,1)S(1)}, bf16[2,136,1088]{2,1,0:T(8,128)(2,1)S(1)}, u32[]{:S(2)}, u32[]{:S(2)}) collective-permute-start(bf16[2,136,1088]{2,1,0:T(8,128)(2,1)S(1)} %pad_maximum_fusion.19), channel_id=1, source_target_pairs={{0,16},{4,12},{8,24},{12,4},{16,0},{20,28},{24,8},{28,20},{1,17},{... | collective-permute-start | bytes 1775624 | tf_op jit(solution)/shard_map/ppermute | solution.py:350
  925.5 46.5 %collective-permute-start.82 = (bf16[4,136,1088]{2,1,0:T(8,128)(2,1)}, bf16[4,136,1088]{2,1,0:T(8,128)(2,1)}, u32[]{:S(2)}, u32[]{:S(2)}) collective-permute-start(bf16[4,136,1088]{2,1,0:T(8,128)(2,1)} %pad_maximum_fusion.15), channel_id=1, source_target_pairs={{0,4},{4,0},{8,12},{12,8},{16,20},{20,16},{24,28},{28,24},{1,5},{5... | collective-permute-start | bytes 3551240 | tf_op jit(solution)/shard_map/ppermute | solution.py:350
  928.3 61.8 %reduce-scatter.29.cloned.1.call-start = ((), (), s32[]{:S(2)}) async-start(), calls=%async_computation.17 | async-start | bytes 1566720
  (271 other events, 3349.9 us)
Sparse Core Ops, SparseCore 0:
  13.2 34.3 all-gather.8
  49.8 30.9 all-gather.10
  82.9 30.8 all-gather.12
  115.2 30.5 all-gather.14
  147.9 30.7 all-gather.16
  180.1 30.7 all-gather.18
  538.1 27.1 reduce-scatter.18
  596.1 27.1 reduce-scatter.20
  706.7 28.0 reduce-scatter.22
  823.0 28.0 reduce-scatter.24
  928.5 27.7 reduce-scatter.26
  959.1 31.0 reduce-scatter.28
